TPU v7x, 32 devices: a whole 2x2x4 slice. The times are simulated.
32 devices in a mesh: dp: 8 (over z, y), mp: 4 (over x, core).
Axes of the slice: x: 2, y: 2, z: 4, core: 2. Of those that a mesh axis runs over, the one named last changes fastest.
Arguments:
- images: bfloat16 [64, 196, 256], P('dp'), may hold values from -6 to 6
- labels: int32 [64, 196, 256], P('dp'), may hold values from 0 to 8
- background: int32 [64], P('dp'), may hold values 0 or 1
- patients: int32 [64], P('dp'), may hold values from 0 to 15
- stem_w: float32 [256, 1024], P('dp'), may hold values from -0.375 to 0.375
- embed_w: float32 [1024, 768], P('dp'), may hold values from -0.1875 to 0.1875
- token_params: float32 [202, 768], P(None, 'dp')
- qkv_w: float32 [768, 2304], P('dp', 'mp'), may hold values from -0.21875 to 0.21875
- out_w: float32 [768, 768], P('mp', 'dp'), may hold values from -0.625 to 0.625
- mlp_in_w: float32 [768, 3072], P('dp', 'mp'), may hold values from -0.21875 to 0.21875
- mlp_out_w: float32 [3072, 768], P('mp', 'dp'), may hold values from -0.109375 to 0.109375
- skip_w: float32 [1024, 2560], P('dp'), may hold values from -0.1875 to 0.1875
- decoder_w: float32 [365120], P('dp')
- stem_m: float32 [256, 1024], P('dp'), may hold values from -4.172325e-07 to 4.172325e-07
- embed_m: float32 [1024, 768], P('dp'), may hold values from -4.172325e-07 to 4.172325e-07
- token_m: float32 [202, 768], P(None, 'dp'), may hold values from -4.172325e-07 to 4.172325e-07
- qkv_m: float32 [768, 2304], P('dp', 'mp'), may hold values from -4.172325e-07 to 4.172325e-07
- out_m: float32 [768, 768], P('mp', 'dp'), may hold values from -4.172325e-07 to 4.172325e-07
- mlp_in_m: float32 [768, 3072], P('dp', 'mp'), may hold values from -4.172325e-07 to 4.172325e-07
- mlp_out_m: float32 [3072, 768], P('mp', 'dp'), may hold values from -4.172325e-07 to 4.172325e-07
- skip_m: float32 [1024, 2560], P('dp'), may hold values from -4.172325e-07 to 4.172325e-07
- decoder_m: float32 [365120], P('dp'), may hold values from -4.172325e-07 to 4.172325e-07
- stem_v: float32 [256, 1024], P('dp'), may hold values from 3.5498253e-16 to 1.4199301e-15
- embed_v: float32 [1024, 768], P('dp'), may hold values from 3.5498253e-16 to 1.4199301e-15
- token_v: float32 [202, 768], P(None, 'dp'), may hold values from 3.5498253e-16 to 1.4199301e-15
- qkv_v: float32 [768, 2304], P('dp', 'mp'), may hold values from 3.5498253e-16 to 1.4199301e-15
- out_v: float32 [768, 768], P('mp', 'dp'), may hold values from 3.5498253e-16 to 1.4199301e-15
- mlp_in_v: float32 [768, 3072], P('dp', 'mp'), may hold values from 3.5498253e-16 to 1.4199301e-15
- mlp_out_v: float32 [3072, 768], P('mp', 'dp'), may hold values from 3.5498253e-16 to 1.4199301e-15
- skip_v: float32 [1024, 2560], P('dp'), may hold values from 3.5498253e-16 to 1.4199301e-15
- decoder_v: float32 [365120], P('dp'), may hold values from 3.5498253e-16 to 1.4199301e-15
Outputs:
- loss: float32 [], replicated
- pixel_count: float32 [], replicated
- grad_norm: float32 [], replicated
- new_stem_w: float32 [256, 1024], P('dp')
- new_embed_w: float32 [1024, 768], P('dp')
- new_token_params: float32 [202, 768], P(None, 'dp')
- new_qkv_w: float32 [768, 2304], P('dp', 'mp')
- new_out_w: float32 [768, 768], P('mp', 'dp')
- new_mlp_in_w: float32 [768, 3072], P('dp', 'mp')
- new_mlp_out_w: float32 [3072, 768], P('mp', 'dp')
- new_skip_w: float32 [1024, 2560], P('dp')
- new_decoder_w: float32 [365120], P('dp')
- new_stem_m: float32 [256, 1024], P('dp')
- new_embed_m: float32 [1024, 768], P('dp')
- new_token_m: float32 [202, 768], P(None, 'dp')
- new_qkv_m: float32 [768, 2304], P('dp', 'mp')
- new_out_m: float32 [768, 768], P('mp', 'dp')
- new_mlp_in_m: float32 [768, 3072], P('dp', 'mp')
- new_mlp_out_m: float32 [3072, 768], P('mp', 'dp')
- new_skip_m: float32 [1024, 2560], P('dp')
- new_decoder_m: float32 [365120], P('dp')
- new_stem_v: float32 [256, 1024], P('dp')
- new_embed_v: float32 [1024, 768], P('dp')
- new_token_v: float32 [202, 768], P(None, 'dp')
- new_qkv_v: float32 [768, 2304], P('dp', 'mp')
- new_out_v: float32 [768, 768], P('mp', 'dp')
- new_mlp_in_v: float32 [768, 3072], P('dp', 'mp')
- new_mlp_out_v: float32 [3072, 768], P('mp', 'dp')
- new_skip_v: float32 [1024, 2560], P('dp')
- new_decoder_v: float32 [365120], P('dp')
All inputs are finite; a program needn't handle non-finite values. No bound on the sum of `background` on one device may be relied on, other than what follows from the above.
Results may differ from a plain program's by a relative error of at most 0.0075.
Values may be sent and summed in bfloat16 or wider, within the bound.
No kernel may reach another device: no remote copies, remote signals or barrier semaphores. Data moves between devices by JAX's collectives and lax.ppermute only.
A program may use at most 256 MiB of HBM per device.

v0:
```python
import jax
import jax.numpy as jnp
from jax import lax
from jax.sharding import PartitionSpec as P

D = 768
HEAD_DIM = 64
PATCHES = 196
PIXELS = 256
CHAN_A = 256
CHAN_B = 128
CHAN_C = 64
CHAN_D = 16
CLASSES = 9
PATIENTS = 16
STEP = 10


norm_eps = 1e-06
dice_eps = 1e-05
clip_limit = 0.002
learn_rate = 0.05
token_rate = 0.5
beta_one = 0.9
beta_two = 0.999
adam_eps = 1e-08
decay_rate = 0.01
highest = lax.Precision.HIGHEST


def gelu_fn(value):
    return jax.nn.gelu(value, approximate=True)


def layer_norm(inputs, gain, shift):
    center = inputs - jnp.mean(inputs, axis=-1, keepdims=True)
    spread = jnp.mean(center * center, axis=-1, keepdims=True)
    return center * lax.rsqrt(spread + norm_eps) * gain + shift


def matmul(left, right):
    return jnp.dot(left, right, preferred_element_type=jnp.float32)


def back_linear(grad_low, input_low, weight_low):
    return (matmul(input_low.T, grad_low), matmul(grad_low, weight_low.T))


def gelu_back(pre_value, grad):
    return jax.vjp(gelu_fn, pre_value)[1](grad)[0]


def norm_back(inputs, gain, shift, grad):
    return jax.vjp(layer_norm, inputs, gain, shift)[1](grad)


def split_decoder(flat):
    edge_one = D * CHAN_A
    edge_two = edge_one + CHAN_A * 4 * CHAN_B
    edge_three = edge_two + CHAN_B * 4 * CHAN_C
    edge_four = edge_three + CHAN_C * 4 * CHAN_D
    return (
        flat[:edge_one].reshape(D, CHAN_A),
        flat[edge_one:edge_two].reshape(CHAN_A, 4 * CHAN_B),
        flat[edge_two:edge_three].reshape(CHAN_B, 4 * CHAN_C),
        flat[edge_three:edge_four].reshape(CHAN_C, 4 * CHAN_D),
        flat[edge_four:].reshape(CHAN_D, 4 * CLASSES),
    )


def block_diag(weight, parents, inner, children, channels):
    eye_block = jnp.eye(parents, dtype=jnp.bfloat16)
    split = weight.reshape(inner, children, channels)
    return jnp.einsum("pt,kjc->pktjc", eye_block, split).reshape(
        parents * inner, parents * children * channels
    )


def block_diag_grad(grad_big, parents, inner, children, channels):
    shaped = grad_big.reshape(parents, inner, parents, children, channels)
    return jnp.einsum("pkpjc->kjc", shaped).reshape(inner, children * channels)


def mp_sum(partial_value):
    return lax.psum(partial_value, "mp")


def back_sum(partial_value):
    return lax.psum(partial_value, "mp")


def layer_forward(embed, tokens, qkv_b, out_b, in_b, down_b, slices):
    num_rows = embed.shape[0]
    local_heads = qkv_b.shape[1] // (3 * HEAD_DIM)
    normed = layer_norm(embed, tokens[PATCHES], tokens[PATCHES + 1]).astype(jnp.bfloat16)
    triple = (
        matmul(normed, qkv_b)
        .astype(jnp.bfloat16)
        .reshape(slices, PATCHES, local_heads, 3, HEAD_DIM)
    )
    queries = triple[:, :, :, 0]
    keys_low = triple[:, :, :, 1]
    values = triple[:, :, :, 2]
    scores = jnp.einsum(
        "sqhd,skhd->shqk", queries, keys_low, preferred_element_type=jnp.float32
    ) * HEAD_DIM ** (-0.5)
    attend = jax.nn.softmax(scores, axis=-1)
    attend_low = attend.astype(jnp.bfloat16)
    context = jnp.einsum("shqk,skhd->sqhd", attend_low, values, preferred_element_type=jnp.float32)
    context = context.astype(jnp.bfloat16).reshape(num_rows, local_heads * HEAD_DIM)
    resid = embed + mp_sum(matmul(context, out_b))
    normed2 = layer_norm(resid, tokens[PATCHES + 2], tokens[PATCHES + 3]).astype(jnp.bfloat16)
    pre_inner = matmul(normed2, in_b)
    inner = gelu_fn(pre_inner).astype(jnp.bfloat16)
    resid2 = resid + mp_sum(matmul(inner, down_b))
    final = layer_norm(resid2, tokens[PATCHES + 4], tokens[PATCHES + 5])
    kept = (
        embed,
        normed,
        queries,
        keys_low,
        values,
        attend,
        attend_low,
        context,
        resid,
        normed2,
        pre_inner,
        inner,
        resid2,
    )
    return (kept, final)


def layer_backward(kept, tokens, qkv_b, out_b, in_b, down_b, grad_final):
    (
        embed,
        normed,
        queries,
        keys_low,
        values,
        attend,
        attend_low,
        context,
        resid,
        normed2,
        pre_inner,
        inner,
        resid2,
    ) = kept
    num_rows = embed.shape[0]
    grad_resid2, grad_gf, grad_bf = norm_back(
        resid2, tokens[PATCHES + 4], tokens[PATCHES + 5], grad_final
    )
    grad_down, grad_inner = back_linear(grad_resid2.astype(jnp.bfloat16), inner, down_b)
    grad_pre = gelu_back(pre_inner, grad_inner).astype(jnp.bfloat16)
    grad_in, part_normed2 = back_linear(grad_pre, normed2, in_b)
    grad_resid_ln, grad_g2, grad_b2 = norm_back(
        resid, tokens[PATCHES + 2], tokens[PATCHES + 3], back_sum(part_normed2)
    )
    grad_resid = grad_resid2 + grad_resid_ln
    grad_out, grad_context = back_linear(grad_resid.astype(jnp.bfloat16), context, out_b)
    grad_context = grad_context.astype(jnp.bfloat16).reshape(values.shape)
    grad_attend = jnp.einsum(
        "sqhd,skhd->shqk", grad_context, values, preferred_element_type=jnp.float32
    )
    grad_values = jnp.einsum(
        "shqk,sqhd->skhd", attend_low, grad_context, preferred_element_type=jnp.float32
    )
    grad_scores = attend * (grad_attend - jnp.sum(attend * grad_attend, axis=-1, keepdims=True))
    grad_scores = (grad_scores * HEAD_DIM ** (-0.5)).astype(jnp.bfloat16)
    grad_queries = jnp.einsum(
        "shqk,skhd->sqhd", grad_scores, keys_low, preferred_element_type=jnp.float32
    )
    grad_keys = jnp.einsum(
        "shqk,sqhd->skhd", grad_scores, queries, preferred_element_type=jnp.float32
    )
    grad_triple = (
        jnp.stack([grad_queries, grad_keys, grad_values], axis=3)
        .reshape(num_rows, -1)
        .astype(jnp.bfloat16)
    )
    grad_qkv, part_normed = back_linear(grad_triple, normed, qkv_b)
    grad_embed_ln, grad_g1, grad_b1 = norm_back(
        embed, tokens[PATCHES], tokens[PATCHES + 1], back_sum(part_normed)
    )
    grad_embed = grad_resid + grad_embed_ln
    gains = jnp.stack([grad_g1, grad_b1, grad_g2, grad_b2, grad_gf, grad_bf])
    return (grad_embed, gains, grad_qkv, grad_out, grad_in, grad_down)


def adamw(weight, grad, first, second, rate):
    first_new = beta_one * first + (1.0 - beta_one) * grad
    second_new = beta_two * second + (1.0 - beta_two) * grad * grad
    first_hat = first_new / (1.0 - beta_one**STEP)
    second_hat = second_new / (1.0 - beta_two**STEP)
    new_weight = weight - rate * (
        first_hat / (jnp.sqrt(second_hat) + adam_eps) + decay_rate * weight
    )
    return (new_weight, first_new, second_new)


def body(
    images,
    labels,
    background,
    patients,
    stem_w,
    embed_w,
    token_params,
    qkv_w,
    out_w,
    mlp_in_w,
    mlp_out_w,
    skip_w,
    decoder_w,
    stem_m,
    embed_m,
    token_m,
    qkv_m,
    out_m,
    mlp_in_m,
    mlp_out_m,
    skip_m,
    decoder_m,
    stem_v,
    embed_v,
    token_v,
    qkv_v,
    out_v,
    mlp_in_v,
    mlp_out_v,
    skip_v,
    decoder_v,
):
    full = (
        lax.all_gather(stem_w.astype(jnp.bfloat16), "dp", axis=0, tiled=True),
        lax.all_gather(embed_w.astype(jnp.bfloat16), "dp", axis=0, tiled=True),
        lax.all_gather(token_params.astype(jnp.bfloat16), "dp", axis=1, tiled=True),
        lax.all_gather(qkv_w.astype(jnp.bfloat16), "dp", axis=0, tiled=True),
        lax.all_gather(out_w.astype(jnp.bfloat16), "dp", axis=1, tiled=True),
        lax.all_gather(mlp_in_w.astype(jnp.bfloat16), "dp", axis=0, tiled=True),
        lax.all_gather(mlp_out_w.astype(jnp.bfloat16), "dp", axis=1, tiled=True),
        lax.all_gather(skip_w.astype(jnp.bfloat16), "dp", axis=0, tiled=True),
        lax.all_gather(decoder_w.astype(jnp.bfloat16), "dp", axis=0, tiled=True),
    )
    stem_b, embed_b, token_b, qkv_b, out_b, in_b, down_b, skip_b, decoder_b = full
    dec_b, one_b, two_b, three_b, head_b = split_decoder(decoder_b)
    big_two = block_diag(two_b, 4, CHAN_B, 4, CHAN_C)
    big_three = block_diag(three_b, 16, CHAN_C, 4, CHAN_D)
    head_eye = jnp.eye(64, dtype=jnp.bfloat16)
    big_head = jnp.einsum("st,kqc->skctq", head_eye, head_b.reshape(CHAN_D, 4, CLASSES)).reshape(
        64 * CHAN_D, CLASSES * PIXELS
    )
    tokens = token_b.astype(jnp.float32)
    slices = images.shape[0]
    images_own, labels_own, background_own, patients_own = (images, labels, background, patients)
    num_rows = slices * PATCHES
    pixels = images_own.reshape(num_rows, PIXELS)
    pre_stem = matmul(pixels, stem_b)
    hidden = gelu_fn(pre_stem).astype(jnp.bfloat16)
    embed = (matmul(hidden, embed_b).reshape(slices, PATCHES, D) + tokens[:PATCHES]).reshape(
        num_rows, D
    )
    kept, final = layer_forward(embed, tokens, qkv_b, out_b, in_b, down_b, slices)
    final_low = final.astype(jnp.bfloat16)
    pre_zero = matmul(final_low, dec_b)
    level0 = gelu_fn(pre_zero).astype(jnp.bfloat16)
    skips = matmul(hidden, skip_b)
    split_a = 4 * CHAN_B
    split_b = split_a + 16 * CHAN_C
    pre_one = matmul(level0, one_b) + skips[:, :split_a]
    level1 = gelu_fn(pre_one).astype(jnp.bfloat16)
    pre_two = matmul(level1, big_two) + skips[:, split_a:split_b]
    level2 = gelu_fn(pre_two).astype(jnp.bfloat16)
    pre_three = matmul(level2, big_three) + skips[:, split_b:]
    level3 = gelu_fn(pre_three).astype(jnp.bfloat16)
    logits = matmul(level3, big_head).reshape(slices, PATCHES, CLASSES, PIXELS)
    class_ids = jnp.arange(CLASSES, dtype=jnp.int32)[None, None, :, None]
    onehot = (labels_own[:, :, None, :] == class_ids).astype(jnp.float32)
    keep = (1 - background_own).astype(jnp.float32)
    keep_wide = keep[:, None, None, None]
    log_prob = jax.nn.log_softmax(logits, axis=2)
    class_prob = jnp.exp(log_prob)
    owner = (patients_own[:, None] == jnp.arange(PATIENTS, dtype=jnp.int32)).astype(jnp.float32)
    local_stats = (
        -jnp.sum(keep_wide * onehot * log_prob),
        jnp.sum(keep) * (PATCHES * PIXELS),
        jnp.dot(owner.T, jnp.sum(class_prob * onehot, axis=(1, 3)), precision=highest),
        jnp.dot(owner.T, jnp.sum(class_prob, axis=(1, 3)), precision=highest),
        jnp.dot(owner.T, jnp.sum(onehot, axis=(1, 3)), precision=highest),
    )
    ce_total, pixel_count, pat_over, pat_pred, pat_true = lax.psum(
        (local_stats[0], local_stats[1], local_stats[2], local_stats[3], local_stats[4]), "dp"
    )
    denominator = pat_pred + pat_true + dice_eps
    dice = (2.0 * pat_over + dice_eps) / denominator
    count_floor = jnp.maximum(pixel_count, 1.0)
    loss = ce_total / count_floor + 1.0 - jnp.mean(dice)
    cells = PATIENTS * CLASSES
    over_slice = jnp.dot(owner, -2.0 / (cells * denominator), precision=highest)
    pred_slice = jnp.dot(
        owner, (2.0 * pat_over + dice_eps) / (cells * denominator * denominator), precision=highest
    )

    def local_loss(logit_values):
        log_local = jax.nn.log_softmax(logit_values, axis=2)
        prob_local = jnp.exp(log_local)
        cross = -jnp.sum(keep_wide * onehot * log_local) / count_floor
        dice_part = jnp.sum(over_slice * jnp.sum(prob_local * onehot, axis=(1, 3)))
        return cross + dice_part + jnp.sum(pred_slice * jnp.sum(prob_local, axis=(1, 3)))

    grad_logits = jax.vjp(local_loss, logits)[1](jnp.ones((), jnp.float32))[0]
    grad_logits = grad_logits.reshape(num_rows, CLASSES * PIXELS).astype(jnp.bfloat16)
    grad_big_head, grad_level3 = back_linear(grad_logits, level3, big_head)
    grad_head = jnp.einsum("skcsq->kqc", grad_big_head.reshape(64, CHAN_D, CLASSES, 64, 4)).reshape(
        CHAN_D, 4 * CLASSES
    )
    grad_pre3 = gelu_back(pre_three, grad_level3)
    grad_big3, grad_level2 = back_linear(grad_pre3.astype(jnp.bfloat16), level2, big_three)
    grad_three = block_diag_grad(grad_big3, 16, CHAN_C, 4, CHAN_D)
    grad_pre2 = gelu_back(pre_two, grad_level2)
    grad_big2, grad_level1 = back_linear(grad_pre2.astype(jnp.bfloat16), level1, big_two)
    grad_two = block_diag_grad(grad_big2, 4, CHAN_B, 4, CHAN_C)
    grad_pre1 = gelu_back(pre_one, grad_level1)
    grad_one, grad_level0 = back_linear(grad_pre1.astype(jnp.bfloat16), level0, one_b)
    grad_pre0 = gelu_back(pre_zero, grad_level0).astype(jnp.bfloat16)
    grad_dec, grad_final = back_linear(grad_pre0, final_low, dec_b)
    grad_skips = jnp.concatenate([grad_pre1, grad_pre2, grad_pre3], axis=1).astype(jnp.bfloat16)
    grad_skip, grad_hidden_skip = back_linear(grad_skips, hidden, skip_b)
    grad_decoder = jnp.concatenate(
        [
            grad_dec.reshape(-1),
            grad_one.reshape(-1),
            grad_two.reshape(-1),
            grad_three.reshape(-1),
            grad_head.reshape(-1),
        ]
    )
    grad_embed, gains, grad_qkv, grad_out, grad_in, grad_down = layer_backward(
        kept, tokens, qkv_b, out_b, in_b, down_b, grad_final
    )
    grad_token = jnp.concatenate(
        [jnp.sum(grad_embed.reshape(slices, PATCHES, D), axis=0), gains], axis=0
    )
    grad_embed_w, grad_hidden = back_linear(grad_embed.astype(jnp.bfloat16), hidden, embed_b)
    grad_pre_stem = gelu_back(pre_stem, grad_hidden + grad_hidden_skip).astype(jnp.bfloat16)
    grad_stem = matmul(pixels.T, grad_pre_stem)
    red_stem, red_embed, red_token, red_qkv, red_out, red_in, red_down, red_skip, red_decoder = (
        lax.psum_scatter(grad_stem, "dp", scatter_dimension=0, tiled=True),
        lax.psum_scatter(grad_embed_w, "dp", scatter_dimension=0, tiled=True),
        lax.psum_scatter(grad_token, "dp", scatter_dimension=1, tiled=True),
        lax.psum_scatter(grad_qkv, "dp", scatter_dimension=0, tiled=True),
        lax.psum_scatter(grad_out, "dp", scatter_dimension=1, tiled=True),
        lax.psum_scatter(grad_in, "dp", scatter_dimension=0, tiled=True),
        lax.psum_scatter(grad_down, "dp", scatter_dimension=1, tiled=True),
        lax.psum_scatter(grad_skip, "dp", scatter_dimension=0, tiled=True),
        lax.psum_scatter(grad_decoder, "dp", scatter_dimension=0, tiled=True),
    )
    reduced = (
        red_stem,
        red_embed,
        red_token,
        red_qkv,
        red_out,
        red_in,
        red_down,
        red_skip,
        red_decoder,
    )
    split_squares = sum((jnp.sum(grad * grad) for grad in (red_qkv, red_out, red_in, red_down)))
    shared_squares = sum(
        (jnp.sum(grad * grad) for grad in (red_stem, red_embed, red_token, red_skip, red_decoder))
    )
    total = lax.psum(split_squares + shared_squares / lax.axis_size("mp"), ("dp", "mp"))
    grad_norm = jnp.sqrt(total)
    factor = jnp.minimum(1.0, clip_limit / (grad_norm + 1e-06))
    masters = (stem_w, embed_w, token_params, qkv_w, out_w, mlp_in_w, mlp_out_w, skip_w, decoder_w)
    firsts = (stem_m, embed_m, token_m, qkv_m, out_m, mlp_in_m, mlp_out_m, skip_m, decoder_m)
    seconds = (stem_v, embed_v, token_v, qkv_v, out_v, mlp_in_v, mlp_out_v, skip_v, decoder_v)
    rates = (
        learn_rate,
        learn_rate,
        token_rate,
        learn_rate,
        learn_rate,
        learn_rate,
        learn_rate,
        learn_rate,
        learn_rate,
    )
    results = [
        adamw(weight, grad * factor, first, second, rate)
        for weight, grad, first, second, rate in zip(masters, reduced, firsts, seconds, rates)
    ]
    news = [item[0] for item in results]
    moms = [item[1] for item in results]
    secs = [item[2] for item in results]
    return (
        loss,
        pixel_count,
        grad_norm,
        news[0],
        news[1],
        news[2],
        news[3],
        news[4],
        news[5],
        news[6],
        news[7],
        news[8],
        moms[0],
        moms[1],
        moms[2],
        moms[3],
        moms[4],
        moms[5],
        moms[6],
        moms[7],
        moms[8],
        secs[0],
        secs[1],
        secs[2],
        secs[3],
        secs[4],
        secs[5],
        secs[6],
        secs[7],
        secs[8],
    )


def solution(mesh):
    placed = (
        P("dp", None, None),
        P("dp", None, None),
        P("dp"),
        P("dp"),
        P("dp", None),
        P("dp", None),
        P(None, "dp"),
        P("dp", "mp"),
        P("mp", "dp"),
        P("dp", "mp"),
        P("mp", "dp"),
        P("dp", None),
        P("dp"),
        P("dp", None),
        P("dp", None),
        P(None, "dp"),
        P("dp", "mp"),
        P("mp", "dp"),
        P("dp", "mp"),
        P("mp", "dp"),
        P("dp", None),
        P("dp"),
        P("dp", None),
        P("dp", None),
        P(None, "dp"),
        P("dp", "mp"),
        P("mp", "dp"),
        P("dp", "mp"),
        P("mp", "dp"),
        P("dp", None),
        P("dp"),
    )
    return jax.shard_map(
        body,
        mesh=mesh,
        in_specs=placed,
        out_specs=(
            P(),
            P(),
            P(),
            P("dp", None),
            P("dp", None),
            P(None, "dp"),
            P("dp", "mp"),
            P("mp", "dp"),
            P("dp", "mp"),
            P("mp", "dp"),
            P("dp", None),
            P("dp"),
            P("dp", None),
            P("dp", None),
            P(None, "dp"),
            P("dp", "mp"),
            P("mp", "dp"),
            P("dp", "mp"),
            P("mp", "dp"),
            P("dp", None),
            P("dp"),
            P("dp", None),
            P("dp", None),
            P(None, "dp"),
            P("dp", "mp"),
            P("mp", "dp"),
            P("dp", "mp"),
            P("mp", "dp"),
            P("dp", None),
            P("dp"),
        ),
        check_vma=False,
    )
```

profile of v0, /device:TPU:0, one launch (start us, length us, event | category | flops | bytes accessed | tf_op | source)
XLA Modules:
  0.0 1933.3 jit_solution(13428143892235876752)
XLA Ops:
  10.0 33.5 %all_gather.29 = bf16[202,768]{0,1:T(8,128)(2,1)S(1)} all-gather(bf16[202,96]{0,1:T(8,128)(2,1)S(1)} %convert_element_type.128), channel_id=1, replica_groups=mesh['dp'=8,'mp'=4] {'dp'}, dimensions={1}, use_global_device_ids=true | all-gather | bytes 349056 | tf_op jit(solution)/shard_map/all_gather | solution.py:239
  53.9 31.0 %all_gather.31 = bf16[192,768]{0,1:T(8,128)(2,1)S(1)} all-gather(bf16[192,96]{0,1:T(8,128)(2,1)S(1)} %copy.203), channel_id=1, replica_groups=mesh['dp'=8,'mp'=4] {'dp'}, dimensions={1}, use_global_device_ids=true | all-gather | bytes 331776 | tf_op jit(solution)/shard_map/all_gather | solution.py:241
  86.6 31.9 %all_gather.27 = bf16[256,1024]{1,0:T(8,128)(2,1)S(1)} all-gather(bf16[32,1024]{1,0:T(8,128)(2,1)S(1)} %copy-done.70), channel_id=1, replica_groups=mesh['dp'=8,'mp'=4] {'dp'}, dimensions={0}, use_global_device_ids=true | all-gather | bytes 589824 | tf_op jit(solution)/shard_map/all_gather | solution.py:237
  118.5 32.5 %all_gather.30 = bf16[768,576]{1,0:T(8,128)(2,1)S(1)} all-gather(bf16[96,576]{1,0:T(8,128)(2,1)S(1)} %convert_element_type.131), channel_id=1, replica_groups=mesh['dp'=8,'mp'=4] {'dp'}, dimensions={0}, use_global_device_ids=true | all-gather | bytes 995328 | tf_op jit(solution)/shard_map/all_gather | solution.py:240
  192.8 90.8 %all-reduce.10.cloned.1.call-done = f32[1568,768]{1,0:T(8,128)} async-done(((f32[1568,768]{1,0:T(8,128)}), f32[1568,768]{1,0:T(8,128)}) %all-reduce.10.cloned.1.call-update) | async-done | bytes 4816912 | tf_op jit(solution)/shard_map/psum | solution.py:85
  291.3 36.3 %all-gather.7.cloned.1.call-done = bf16[768,768]{1,0:T(8,128)(2,1)} async-done(((bf16[96,768]{1,0:T(8,128)(2,1)}), bf16[768,768]{1,0:T(8,128)(2,1)}) %all-gather.7.cloned.1.call-update) | async-done | bytes 1179664 | tf_op jit(solution)/shard_map/all_gather | solution.py:242
  333.1 37.0 %all-gather.9.cloned.1.call-done = bf16[768,768]{0,1:T(8,128)(2,1)} async-done(((bf16[768,96]{0,1:T(8,128)(2,1)}), bf16[768,768]{0,1:T(8,128)(2,1)}) %all-gather.9.cloned.1.call-update) | async-done | bytes 1179664 | tf_op jit(solution)/shard_map/all_gather | solution.py:243
  384.4 62.6 %all-reduce.18.cloned.1.call-done = bf16[365120]{0:T(1024)(128)(2,1)} async-done(((bf16[365120]{0:T(1024)(128)(2,1)}), bf16[365120]{0:T(1024)(128)(2,1)}) %all-reduce.18.cloned.1.call-update) | async-done | bytes 730256
  461.1 64.7 %reshape.251 = bf16[1024,2304]{0,1:T(8,128)(2,1)} reshape(bf16[64,16,9,64,4]{1,0,4,3,2:T(8,128)(2,1)} %multiply_bitcast_fusion) | data formatting | bytes 9437184 | tf_op jit(solution)/shard_map/reshape | solution.py:252
  553.6 79.3 %all-gather.11.cloned.1.call-done = bf16[1024,2560]{1,0:T(8,128)(2,1)} async-done(((bf16[128,2560]{1,0:T(8,128)(2,1)}), bf16[1024,2560]{1,0:T(8,128)(2,1)}) %all-gather.11.cloned.1.call-update) | async-done | bytes 5242896 | tf_op jit(solution)/shard_map/all_gather | solution.py:244
  673.5 13.9 fusion.181
  709.4 35.3 %all-reduce.2 = (f32[16,9]{1,0:T(8,128)}, f32[16,9]{1,0:T(8,128)}, f32[]{:T(128)}) all-reduce(f32[16,9]{1,0:T(8,128)} %convolution_add_fusion.2, f32[16,9]{1,0:T(8,128)} %fusion.131, f32[]{:T(128)S(6)} %mul.984), channel_id=1, replica_groups=mesh['dp'=8,'mp'=4] {'dp'}, use_global_device_ids=true, to_apply=%region_19.20 | all-reduce | flops 289 | bytes 2312 | tf_op jit(solution)/shard_map/psum | solution.py:293
  772.2 13.2 copy.207
  785.4 16.6 convert_element_type.150
  802.0 16.7 fusion.28
  883.5 13.8 dot_general.236
  897.3 21.0 %select_reduce_fusion = f32[16,9,4]{0,2,1:T(4,128)} fusion(pred[64,64]{1,0:T(8,128)(4,1)} %iota_compare_fusion.1, bf16[64,16,1568,1,1]{2,1,4,3,0:T(8,128)(2,1)S(1)} %bitcast.172, bf16[9,64,4,1568]{3,2,1,0:T(4,128)(2,1)} %dot_general.236), kind=kOutput, calls=%fused_computation.5 | convolution fusion | flops 7403470336 | bytes 10443008 | tf_op jit(solution)/shard_map/dot_general | solution.py:42
  921.4 32.8 %all-reduce.14.cloned.1.call-done = f32[1568,768]{1,0:T(8,128)} async-done(((f32[1568,768]{1,0:T(8,128)}), f32[1568,768]{1,0:T(8,128)}) %all-reduce.14.cloned.1.call-update) | async-done | bytes 4816912 | tf_op jit(solution)/shard_map/psum | solution.py:89
  1033.8 14.3 fusion.45
  1048.1 52.4 %all-reduce.16.cloned.1.call-done = f32[1568,768]{1,0:T(8,128)} async-done(((f32[1568,768]{1,0:T(8,128)}), f32[1568,768]{1,0:T(8,128)}) %all-reduce.16.cloned.1.call-update) | async-done | bytes 4816912 | tf_op jit(solution)/shard_map/psum | solution.py:89
  1122.8 13.6 fusion.76
  1146.4 15.5 fusion.44
  1164.5 22.1 %psum.72 = f32[]{:T(128)} all-reduce(f32[]{:T(128)S(6)} %neg.19), channel_id=1, replica_groups=mesh['dp'=8,'mp'=4] {'dp'}, use_global_device_ids=true, to_apply=%region_13.14 | all-reduce | flops 1 | bytes 8 | tf_op jit(solution)/shard_map/psum | solution.py:293
  1192.9 64.3 %reduce-scatter.25.cloned.1.call-done = f32[96,192]{1,0:T(8,128)} async-done(((f32[768,192]{1,0:T(8,128)}), f32[96,192]{1,0:T(8,128)}) %reduce-scatter.25.cloned.1.call-update) | async-done | bytes 73744
  1258.8 70.3 %reduce-scatter.17.cloned.1.call-done = f32[96,768]{1,0:T(8,128)} async-done(((f32[768,768]{1,0:T(8,128)}), f32[96,768]{1,0:T(8,128)}) %reduce-scatter.17.cloned.1.call-update) | async-done | bytes 294928 | tf_op jit(solution)/shard_map/reduce_scatter | solution.py:355
  1330.7 70.5 %reduce-scatter.19.cloned.1.call-done = f32[768,96]{0,1:T(8,128)} async-done(((f32[768,768]{0,1:T(8,128)}), f32[768,96]{0,1:T(8,128)}) %reduce-scatter.19.cloned.1.call-update) | async-done | bytes 294928 | tf_op jit(solution)/shard_map/reduce_scatter | solution.py:356
  1402.8 67.9 %reduce-scatter.15.cloned.1.call-done = f32[96,576]{1,0:T(8,128)} async-done(((f32[768,576]{1,0:T(8,128)}), f32[96,576]{1,0:T(8,128)}) %reduce-scatter.15.cloned.1.call-update) | async-done | bytes 221200 | tf_op jit(solution)/shard_map/reduce_scatter | solution.py:353
  1475.0 60.3 %reduce-scatter.29.cloned.1.call-done = f32[96,202]{1,0:T(8,128)} async-done(((f32[768,202]{1,0:T(8,128)}), f32[96,202]{1,0:T(8,128)}) %reduce-scatter.29.cloned.1.call-update) | async-done | bytes 77584
  1536.9 64.9 %reduce-scatter.27.cloned.1.call-done = f32[32,1024]{1,0:T(8,128)} async-done(((f32[256,1024]{1,0:T(8,128)}), f32[32,1024]{1,0:T(8,128)}) %reduce-scatter.27.cloned.1.call-update) | async-done | bytes 131088 | tf_op jit(solution)/shard_map/reduce_scatter | solution.py:350
  1603.7 75.0 %reduce-scatter.21.cloned.1.call-done = f32[128,768]{1,0:T(8,128)} async-done(((f32[1024,768]{1,0:T(8,128)}), f32[128,768]{1,0:T(8,128)}) %reduce-scatter.21.cloned.1.call-update) | async-done | bytes 393232 | tf_op jit(solution)/shard_map/reduce_scatter | solution.py:351
  1682.4 177.0 %reduce-scatter.23.cloned.1.call-done = f32[128,2560]{1,0:T(8,128)} async-done(((f32[1024,2560]{1,0:T(8,128)}), f32[128,2560]{1,0:T(8,128)}) %reduce-scatter.23.cloned.1.call-update) | async-done | bytes 1310736 | tf_op jit(solution)/shard_map/reduce_scatter | solution.py:357
  1863.1 39.4 %psum.79 = f32[]{:T(128)} all-reduce(f32[]{:T(128)S(6)} %add.411), channel_id=1, replica_groups=mesh['dp'=8,'mp'=4] {'dp','mp'}, use_global_device_ids=true, to_apply=%region_61.62 | all-reduce | flops 1 | bytes 8 | tf_op jit(solution)/shard_map/psum | solution.py:375
  (492 shorter events, 432.9 us)
Async XLA Ops:
  7.2 148.5 %all-gather.5.cloned.1.call-start = ((), (), s32[]{:S(2)}) async-start(), calls=%async_computation.8 | async-start | bytes 1769472 | tf_op jit(solution)/shard_map/all_gather | solution.py:238
  9.0 274.6 %all-reduce.10.cloned.1.call-start = ((), (), s32[]{:S(2)}) async-start(), calls=%async_computation.9 | async-start | bytes 9633792 | tf_op jit(solution)/shard_map/psum | solution.py:85
  45.1 105.9 %copy-start.61 = (bf16[1568,256]{1,0:T(8,128)(2,1)}, bf16[1568,256]{1,0:T(8,128)(2,1)S(1)}, u32[]{:S(2)}) copy-start(bf16[1568,256]{1,0:T(8,128)(2,1)S(1)} %reshape.244) | copy-start | bytes 2408452
  84.9 99.0 %copy-start.27 = (bf16[192,768]{0,1:T(8,128)(2,1)}, bf16[192,768]{0,1:T(8,128)(2,1)S(1)}, u32[]{:S(2)}) copy-start(bf16[192,768]{0,1:T(8,128)(2,1)S(1)} %all_gather.31) | copy-start | bytes 884740
  86.6 76.5 %copy-start.90 = (f32[768]{0:T(1024)}, f32[768]{0:T(1024)S(1)}, u32[]{:S(2)}) copy-start(f32[768]{0:T(1024)S(1)} %get-tuple-element.199) | copy-start | bytes 9220
  187.0 140.6 %all-gather.7.cloned.1.call-start = ((), (), s32[]{:S(2)}) async-start(), calls=%async_computation.10 | async-start | bytes 1327104 | tf_op jit(solution)/shard_map/all_gather | solution.py:242
  188.6 181.5 %all-gather.9.cloned.1.call-start = ((), (), s32[]{:S(2)}) async-start(), calls=%async_computation.11 | async-start | bytes 1327104 | tf_op jit(solution)/shard_map/all_gather | solution.py:243
  189.3 257.6 %all-reduce.18.cloned.1.call-start = ((), (), s32[]{:S(2)}) async-start(), calls=%async_computation.21 | async-start | bytes 1462272
  192.7 351.3 %all-reduce.12.cloned.1.call-start = ((), (), s32[]{:S(2)}) async-start(), calls=%async_computation.12 | async-start | bytes 9633792 | tf_op jit(solution)/shard_map/psum | solution.py:85
  378.0 254.9 %all-gather.11.cloned.1.call-start = ((), (), s32[]{:S(2)}) async-start(), calls=%async_computation.13 | async-start | bytes 5898240 | tf_op jit(solution)/shard_map/all_gather | solution.py:244
  380.3 574.0 %all-reduce.14.cloned.1.call-start = ((), (), s32[]{:S(2)}) async-start(), calls=%async_computation.14 | async-start | bytes 9633792 | tf_op jit(solution)/shard_map/psum | solution.py:89
  553.6 90.9 %copy-start.15 = (f32[1568,256]{1,0:T(8,128)}, f32[1568,256]{1,0:T(8,128)S(1)}, u32[]{:S(2)}) copy-start(f32[1568,256]{1,0:T(8,128)S(1)} %fusion.184) | copy-start | bytes 4816900
  861.3 239.2 %all-reduce.16.cloned.1.call-start = ((), (), s32[]{:S(2)}) async-start(), calls=%async_computation.18 | async-start | bytes 9633792 | tf_op jit(solution)/shard_map/psum | solution.py:89
  1004.6 186.6 %all-reduce.20.cloned.1.call-start = ((), (), s32[]{:S(2)}) async-start(), calls=%async_computation.25 | async-start | bytes 2924544
  1008.5 248.6 %reduce-scatter.25.cloned.1.call-start = ((), (), s32[]{:S(2)}) async-start(), calls=%async_computation.22 | async-start | bytes 884736
  1014.3 314.8 %reduce-scatter.17.cloned.1.call-start = ((), (), s32[]{:S(2)}) async-start(), calls=%async_computation.16 | async-start | bytes 2654208 | tf_op jit(solution)/shard_map/reduce_scatter | solution.py:355
  1019.9 381.3 %reduce-scatter.19.cloned.1.call-start = ((), (), s32[]{:S(2)}) async-start(), calls=%async_computation.17 | async-start | bytes 2654208 | tf_op jit(solution)/shard_map/reduce_scatter | solution.py:356
  1028.3 442.4 %reduce-scatter.15.cloned.1.call-start = ((), (), s32[]{:S(2)}) async-start(), calls=%async_computation.15 | async-start | bytes 2211840 | tf_op jit(solution)/shard_map/reduce_scatter | solution.py:353
  1033.5 67.0 %copy-start.72 = (f32[1568]{0:T(1024)S(1)}, f32[1568]{0:T(1024)}, u32[]{:S(2)}) copy-start(f32[1568]{0:T(1024)} %copy-done.71) | copy-start | bytes 18820
  1033.5 67.0 %copy-start.78 = (f32[1568]{0:T(1024)S(1)}, f32[1568]{0:T(1024)}, u32[]{:S(2)}) copy-start(f32[1568]{0:T(1024)} %copy-done.77) | copy-start | bytes 18820
  1033.6 501.7 %reduce-scatter.29.cloned.1.call-start = ((), (), s32[]{:S(2)}) async-start(), calls=%async_computation.24 | async-start | bytes 884736
  1122.6 479.2 %reduce-scatter.27.cloned.1.call-start = ((), (), s32[]{:S(2)}) async-start(), calls=%async_computation.23 | async-start | bytes 1179648 | tf_op jit(solution)/shard_map/reduce_scatter | solution.py:350
  1137.8 540.9 %reduce-scatter.21.cloned.1.call-start = ((), (), s32[]{:S(2)}) async-start(), calls=%async_computation.19 | async-start | bytes 3538944 | tf_op jit(solution)/shard_map/reduce_scatter | solution.py:351
  1146.1 713.3 %reduce-scatter.23.cloned.1.call-start = ((), (), s32[]{:S(2)}) async-start(), calls=%async_computation.20 | async-start | bytes 11796480 | tf_op jit(solution)/shard_map/reduce_scatter | solution.py:357
  1162.9 745.9 %copy-start.67 = (f32[32,1024]{1,0:T(8,128)S(1)}, f32[32,1024]{1,0:T(8,128)}, u32[]{:S(2)}) copy-start(f32[32,1024]{1,0:T(8,128)} %param.35) | copy-start | bytes 393220
  1162.9 747.9 %copy-start.44 = (f32[128,768]{1,0:T(8,128)S(1)}, f32[128,768]{1,0:T(8,128)}, u32[]{:S(2)}) copy-start(f32[128,768]{1,0:T(8,128)} %param.36) | copy-start | bytes 1179652
  1330.7 582.4 %copy-start.57 = (f32[96,576]{1,0:T(8,128)S(1)}, f32[96,576]{1,0:T(8,128)}, u32[]{:S(2)}) copy-start(f32[96,576]{1,0:T(8,128)} %param.38) | copy-start | bytes 663556
  1470.7 442.4 %copy-start.58 = (f32[96,576]{1,0:T(8,128)S(1)}, f32[96,576]{1,0:T(8,128)}, u32[]{:S(2)}) copy-start(f32[96,576]{1,0:T(8,128)} %reduce-scatter.15.cloned.1.call-done) | copy-start | bytes 663556
  1601.8 307.0 %copy-start.65 = (f32[32,1024]{1,0:T(8,128)S(1)}, f32[32,1024]{1,0:T(8,128)}, u32[]{:S(2)}) copy-start(f32[32,1024]{1,0:T(8,128)} %reduce-scatter.27.cloned.1.call-done) | copy-start | bytes 393220
  1603.0 312.1 %copy-start.51 = (f32[96,768]{1,0:T(8,128)S(1)}, f32[96,768]{1,0:T(8,128)}, u32[]{:S(2)}) copy-start(f32[96,768]{1,0:T(8,128)} %param.40) | copy-start | bytes 884740
  1603.0 312.1 %copy-start.54 = (f32[96,768]{1,0:T(8,128)S(1)}, f32[96,768]{1,0:T(8,128)}, u32[]{:S(2)}) copy-start(f32[96,768]{1,0:T(8,128)} %reduce-scatter.17.cloned.1.call-done) | copy-start | bytes 884740
  1678.7 232.0 %copy-start.45 = (f32[128,768]{1,0:T(8,128)S(1)}, f32[128,768]{1,0:T(8,128)}, u32[]{:S(2)}) copy-start(f32[128,768]{1,0:T(8,128)} %reduce-scatter.21.cloned.1.call-done) | copy-start | bytes 1179652
  (120 other events, 1243.5 us)
Sparse Core Ops, SparseCore 0:
  10.8 48.9 all-gather.4
  187.1 96.4 all-reduce.9
  286.3 41.2 all-gather.6
  330.2 39.8 all-gather.8
  374.0 72.9 all-reduce.17
  449.4 94.6 all-reduce.11
  546.5 86.4 all-gather.10
  861.4 92.8 all-reduce.13
  1004.7 95.7 all-reduce.15
  1104.4 86.7 all-reduce.19
  1195.1 62.0 reduce-scatter.24
  1260.9 68.0 reduce-scatter.16
  1332.9 68.1 reduce-scatter.18
  1404.9 65.7 reduce-scatter.14
  1473.8 61.3 reduce-scatter.28
  1539.5 62.2 reduce-scatter.26
  1605.2 73.4 reduce-scatter.20
  1682.2 177.2 reduce-scatter.22
where the time goes:
time: 1940 us; the launch traced here: 1930 us
  waiting for transfers between devices  1050 us (54%)
  matrix products  264 us (14%)
  blocking collectives  226 us (12%)
  local copies, waits for them, and re-layouts  211 us (11%)
  other arithmetic  149 us (8%)
  between operations  29.9 us (2%)
    dot_general x33, matrix products, matmul(): return jnp.dot(left, right, preferred_element_type=jnp.float32)  229 us
    unnamed x22, waiting for transfers between devices  190 us
    reduce_scatter x1, waiting for transfers between devices, body(): lax.psum_scatter(grad_skip, 'dp', scatter_dimension=0, tiled=True)  177 us
    psum x2, waiting for transfers between devices, mp_sum(): return lax.psum(partial_value, 'mp')  97.2 us
    psum x2, waiting for transfers between devices, back_sum(): return lax.psum(partial_value, 'mp')  85.3 us
    all_gather x1, waiting for transfers between devices, body(): lax.all_gather(skip_w.astype(jnp.bfloat16), 'dp', axis=0, tiled=True)  79.3 us
    reduce_scatter x1, waiting for transfers between devices, body(): lax.psum_scatter(grad_embed_w, 'dp', scatter_dimension=0, tiled=True)  75 us
    reduce_scatter x1, waiting for transfers between devices, body(): lax.psum_scatter(grad_down, 'dp', scatter_dimension=1, tiled=True)  70.5 us
  transfers between devices with their start and end apart: 18, of which 17 were waited for; matrix products, arithmetic and copies ran while one was open for 17% of the time, Pallas kernels for 0%

commit v1 on v0

v1 whole, which is shorter than its diff:
```python
import jax
import jax.numpy as jnp
from jax import lax
from jax.experimental import pallas as pl
from jax.experimental.pallas import tpu as pltpu
from jax.sharding import PartitionSpec as P

D = 768
HEAD_DIM = 64
PATCHES = 196
PAD = 208
PIXELS = 256
C_STEM = 1024
CHAN_A = 256
CHAN_B = 128
CHAN_C = 64
CHAN_D = 16
CLASSES = 9
PATIENTS = 16
STEP = 10
GROUP = 32
LANES = 128

norm_eps = 1e-06
dice_eps = 1e-05
clip_limit = 0.002
learn_rate = 0.05
token_rate = 0.5
beta_one = 0.9
beta_two = 0.999
adam_eps = 1e-08
decay_rate = 0.01
highest = lax.Precision.HIGHEST
bf16 = jnp.bfloat16
f32 = jnp.float32
MIB = 1024 * 1024


def gelu_fn(value):
    return jax.nn.gelu(value, approximate=True)


def layer_norm(inputs, gain, shift):
    center = inputs - jnp.mean(inputs, axis=-1, keepdims=True)
    spread = jnp.mean(center * center, axis=-1, keepdims=True)
    return center * lax.rsqrt(spread + norm_eps) * gain + shift


def matmul(left, right):
    return jnp.dot(left, right, preferred_element_type=f32)


def matmul_t(left, right):
    return lax.dot_general(left, right, (((1,), (1,)), ((), ())), preferred_element_type=f32)


def t_matmul(left, right):
    return lax.dot_general(left, right, (((0,), (0,)), ((), ())), preferred_element_type=f32)


def gelu_back(pre_value, grad):
    return jax.vjp(gelu_fn, pre_value)[1](grad)[0]


def norm_back(inputs, gain, shift, grad):
    return jax.vjp(layer_norm, inputs, gain, shift)[1](grad)


def swap(value, axis, bit):
    size = lax.axis_size(axis)
    return lax.ppermute(value, axis, [(i, i ^ (1 << bit)) for i in range(size)])


def my_bit(axis, bit):
    return (lax.axis_index(axis) >> bit) & 1


def double(value, axis, bit, dim):
    other = swap(value, axis, bit)
    mine = my_bit(axis, bit)
    low_half = jnp.where(mine == 0, value, other)
    high_half = jnp.where(mine == 0, other, value)
    return jnp.stack([low_half, high_half], axis=dim)


def halve(kept, axis, bit, dim):
    mine = my_bit(axis, bit)
    send = lax.dynamic_index_in_dim(kept, 1 - mine, dim, keepdims=False).astype(bf16)
    keep = lax.dynamic_index_in_dim(kept, mine, dim, keepdims=False).astype(f32)
    return keep + swap(send, axis, bit).astype(f32)


def log_two(size):
    return size.bit_length() - 1


def gather_rows(block):
    bits = log_two(lax.axis_size("dp"))
    value = block
    for step, bit in enumerate(reversed(range(bits))):
        value = double(value, "dp", bit, step)
    return value.reshape(-1, block.shape[-1])


def scatter_rows(kept):
    size = lax.axis_size("dp")
    bits = log_two(size)
    rows = kept.shape[0] // size
    value = kept.reshape((2,) * bits + (rows, kept.shape[1]))
    for bit in range(bits):
        value = halve(value, "dp", bit, bits - 1 - bit)
    return value


def butterfly(value):
    for axis, bits in (("mp", 2), ("dp", log_two(lax.axis_size("dp")))):
        for bit in range(bits):
            value = value + swap(value, axis, bit)
    return value


def attn_forward_kernel(tri_ref, ctx_ref):
    slices = tri_ref.shape[0] // PAD
    heads = tri_ref.shape[1] // (3 * HEAD_DIM)
    column = lax.broadcasted_iota(jnp.int32, (PAD, PAD), 1)
    for s in range(slices):
        rows = pl.ds(s * PAD, PAD)
        for h in range(heads):
            base = h * 3 * HEAD_DIM
            queries = tri_ref[rows, base : base + HEAD_DIM]
            keys_low = tri_ref[rows, base + HEAD_DIM : base + 2 * HEAD_DIM]
            values = tri_ref[rows, base + 2 * HEAD_DIM : base + 3 * HEAD_DIM]
            attend = soft_rows(matmul_t(queries, keys_low), column)
            context = matmul(attend.astype(bf16), values)
            ctx_ref[rows, h * HEAD_DIM : (h + 1) * HEAD_DIM] = context.astype(bf16)


def soft_rows(scores, column):
    scores = jnp.where(column < PATCHES, scores * HEAD_DIM ** (-0.5), -jnp.inf)
    top = jnp.max(scores, axis=-1, keepdims=True)
    weight = jnp.exp(scores - top)
    return weight / jnp.sum(weight, axis=-1, keepdims=True)


def attn_backward_kernel(tri_ref, gctx_ref, gtri_ref):
    slices = tri_ref.shape[0] // PAD
    heads = tri_ref.shape[1] // (3 * HEAD_DIM)
    column = lax.broadcasted_iota(jnp.int32, (PAD, PAD), 1)
    for s in range(slices):
        rows = pl.ds(s * PAD, PAD)
        for h in range(heads):
            base = h * 3 * HEAD_DIM
            queries = tri_ref[rows, base : base + HEAD_DIM]
            keys_low = tri_ref[rows, base + HEAD_DIM : base + 2 * HEAD_DIM]
            values = tri_ref[rows, base + 2 * HEAD_DIM : base + 3 * HEAD_DIM]
            gctx = gctx_ref[rows, h * HEAD_DIM : (h + 1) * HEAD_DIM]
            attend = soft_rows(matmul_t(queries, keys_low), column)
            g_attend = matmul_t(gctx, values)
            g_values = t_matmul(attend.astype(bf16), gctx)
            inner = jnp.sum(attend * g_attend, axis=-1, keepdims=True)
            g_scores = attend * (g_attend - inner) * HEAD_DIM ** (-0.5)
            g_low = g_scores.astype(bf16)
            g_queries = matmul(g_low, keys_low)
            g_keys = t_matmul(g_low, queries)
            gtri_ref[rows, base : base + HEAD_DIM] = g_queries.astype(bf16)
            gtri_ref[rows, base + HEAD_DIM : base + 2 * HEAD_DIM] = g_keys.astype(bf16)
            gtri_ref[rows, base + 2 * HEAD_DIM : base + 3 * HEAD_DIM] = g_values.astype(bf16)


def attn_forward(triple):
    rows, width = triple.shape
    part = 3 * 3 * HEAD_DIM
    steps = width // (2 * part)
    return pl.pallas_call(
        attn_forward_kernel,
        grid=(steps,),
        in_specs=[pl.BlockSpec((rows, 2 * part), lambda i: (0, i))],
        out_specs=pl.BlockSpec((rows, 2 * part // 3), lambda i: (0, i)),
        out_shape=jax.ShapeDtypeStruct((rows, width // 3), bf16),
        compiler_params=pltpu.CompilerParams(vmem_limit_bytes=32 * MIB),
        name="attn_forward",
    )(triple)


def attn_backward(triple, gctx):
    rows, width = triple.shape
    part = 3 * 3 * HEAD_DIM
    steps = width // (2 * part)
    return pl.pallas_call(
        attn_backward_kernel,
        grid=(steps,),
        in_specs=[
            pl.BlockSpec((rows, 2 * part), lambda i: (0, i)),
            pl.BlockSpec((rows, 2 * part // 3), lambda i: (0, i)),
        ],
        out_specs=pl.BlockSpec((rows, 2 * part), lambda i: (0, i)),
        out_shape=jax.ShapeDtypeStruct((rows, width), bf16),
        compiler_params=pltpu.CompilerParams(vmem_limit_bytes=32 * MIB),
        name="attn_backward",
    )(triple, gctx)


CHUNK = 16


def class_probs(logits_ref, rows, group):
    width = CLASSES * LANES
    values = [
        logits_ref[rows, group * width + c * LANES : group * width + (c + 1) * LANES]
        for c in range(CLASSES)
    ]
    top = values[0]
    for value in values[1:]:
        top = jnp.maximum(top, value)
    weights = [jnp.exp(value - top) for value in values]
    total = weights[0]
    for weight in weights[1:]:
        total = total + weight
    scale = 1.0 / total
    return values, [weight * scale for weight in weights], top + jnp.log(total)


def loss_forward_kernel(level_ref, head_ref, label_ref, logits_ref, stats_ref):
    inner = head_ref.shape[0]
    width = head_ref.shape[1]
    groups = level_ref.shape[1] // inner
    for g in range(groups):
        logits_ref[:, g * width : (g + 1) * width] = matmul(
            level_ref[:, g * inner : (g + 1) * inner], head_ref[...]
        )
    stats_ref[...] = jnp.zeros_like(stats_ref)

    @pl.loop(0, PAD // CHUNK)
    def _(i):
        start = pl.multiple_of(i * CHUNK, CHUNK)
        rows = pl.ds(start, CHUNK)
        row_id = lax.broadcasted_iota(jnp.int32, (CHUNK, LANES), 0) + start
        inside = (row_id < PATCHES).astype(f32)
        for g in range(groups):
            values, probs, log_total = class_probs(logits_ref, rows, g)
            label = label_ref[rows, g * LANES : (g + 1) * LANES]
            cross = jnp.zeros((CHUNK, LANES), f32)
            for c in range(CLASSES):
                hot = (label == c).astype(f32)
                cross = cross + hot * (log_total - values[c])
                for k, term in enumerate((hot * probs[c], inside * probs[c], hot)):
                    spot = 8 * (3 * c + k)
                    part = term[:8]
                    for r in range(8, CHUNK, 8):
                        part = part + term[r : r + 8]
                    stats_ref[0, spot : spot + 8, :] += part
            spot = 8 * 3 * CLASSES
            part = cross[:8]
            for r in range(8, CHUNK, 8):
                part = part + cross[r : r + 8]
            stats_ref[0, spot : spot + 8, :] += part


def loss_forward(level, head, labels):
    rows, width = level.shape
    slices = rows // PAD
    out_width = CLASSES * PIXELS
    stat_rows = 8 * (3 * CLASSES + 1)
    return pl.pallas_call(
        loss_forward_kernel,
        grid=(slices,),
        in_specs=[
            pl.BlockSpec((PAD, width), lambda i: (i, 0)),
            pl.BlockSpec(head.shape, lambda i: (0, 0)),
            pl.BlockSpec((PAD, PIXELS), lambda i: (i, 0)),
        ],
        out_specs=[
            pl.BlockSpec((PAD, out_width), lambda i: (i, 0)),
            pl.BlockSpec((1, stat_rows, LANES), lambda i: (i, 0, 0)),
        ],
        out_shape=[
            jax.ShapeDtypeStruct((rows, out_width), f32),
            jax.ShapeDtypeStruct((slices, stat_rows, LANES), f32),
        ],
        compiler_params=pltpu.CompilerParams(vmem_limit_bytes=40 * MIB),
        name="loss_forward",
    )(level, head, labels)


def loss_backward_kernel(
    coef_ref, logits_ref, label_ref, level_ref, head_ref, g_level_ref, g_head_ref, g_scr
):
    step = pl.program_id(0)
    inner = head_ref.shape[0]
    width = head_ref.shape[1]
    groups = level_ref.shape[1] // inner
    cross_scale = coef_ref[step, 2 * CLASSES]

    @pl.when(step == 0)
    def _():
        g_head_ref[...] = jnp.zeros_like(g_head_ref)

    @pl.loop(0, PAD // CHUNK)
    def _(i):
        start = pl.multiple_of(i * CHUNK, CHUNK)
        rows = pl.ds(start, CHUNK)
        row_id = lax.broadcasted_iota(jnp.int32, (CHUNK, LANES), 0) + start
        inside = (row_id < PATCHES).astype(f32)
        for g in range(groups):
            values, probs, log_total = class_probs(logits_ref, rows, g)
            label = label_ref[rows, g * LANES : (g + 1) * LANES]
            mean = jnp.zeros((CHUNK, LANES), f32)
            pulls = []
            for c in range(CLASSES):
                hot = label == c
                pull = jnp.where(hot, coef_ref[step, c], 0.0) + coef_ref[step, CLASSES + c]
                pulls.append(pull)
                mean = mean + probs[c] * pull
            mean = mean - cross_scale
            for c in range(CLASSES):
                grad = probs[c] * (pulls[c] - mean)
                grad = grad - jnp.where(label == c, cross_scale, 0.0)
                spot = g * width + c * LANES
                g_scr[rows, spot : spot + LANES] = (grad * inside).astype(bf16)

    for g in range(groups):
        part = g_scr[:, g * width : (g + 1) * width]
        g_level_ref[:, g * inner : (g + 1) * inner] = matmul_t(part, head_ref[...])
        g_head_ref[...] += t_matmul(level_ref[:, g * inner : (g + 1) * inner], part)


def loss_backward(coef, logits, labels, level, head):
    rows, width = level.shape
    slices = rows // PAD
    out_width = CLASSES * PIXELS
    return pl.pallas_call(
        loss_backward_kernel,
        grid=(slices,),
        in_specs=[
            pl.BlockSpec(memory_space=pltpu.SMEM),
            pl.BlockSpec((PAD, out_width), lambda i: (i, 0)),
            pl.BlockSpec((PAD, PIXELS), lambda i: (i, 0)),
            pl.BlockSpec((PAD, width), lambda i: (i, 0)),
            pl.BlockSpec(head.shape, lambda i: (0, 0)),
        ],
        out_specs=[
            pl.BlockSpec((PAD, width), lambda i: (i, 0)),
            pl.BlockSpec(head.shape, lambda i: (0, 0)),
        ],
        out_shape=[
            jax.ShapeDtypeStruct((rows, width), f32),
            jax.ShapeDtypeStruct(head.shape, f32),
        ],
        scratch_shapes=[pltpu.VMEM((PAD, out_width), bf16)],
        compiler_params=pltpu.CompilerParams(vmem_limit_bytes=40 * MIB),
        name="loss_backward",
    )(coef, logits, labels, level, head)


def split_decoder(flat):
    edge_one = D * CHAN_A
    edge_two = edge_one + CHAN_A * 4 * CHAN_B
    edge_three = edge_two + CHAN_B * 4 * CHAN_C
    edge_four = edge_three + CHAN_C * 4 * CHAN_D
    return (
        flat[:edge_one].reshape(D, CHAN_A),
        flat[edge_one:edge_two].reshape(CHAN_A, 4 * CHAN_B),
        flat[edge_two:edge_three].reshape(CHAN_B, 4 * CHAN_C),
        flat[edge_three:edge_four].reshape(CHAN_C, 4 * CHAN_D),
        flat[edge_four:].reshape(CHAN_D, 4 * CLASSES),
    )


def same_block(rows, columns, inner, outer):
    row = lax.broadcasted_iota(jnp.int32, (rows, columns), 0) // inner
    column = lax.broadcasted_iota(jnp.int32, (rows, columns), 1) // outer
    return row == column


def block_diag(weight, parents):
    inner, outer = weight.shape
    mask = same_block(parents * inner, parents * outer, inner, outer)
    tiled = jnp.tile(weight, (parents, parents))
    return jnp.where(mask, tiled, jnp.zeros_like(tiled))


def block_diag_grad(grad_big, parents, inner, outer):
    mask = same_block(parents * inner, parents * outer, inner, outer)
    masked = jnp.where(mask, grad_big, 0.0)
    folded = jnp.sum(masked.reshape(parents, inner, parents * outer), axis=0)
    return jnp.sum(folded.reshape(inner, parents, outer), axis=1)


def head_masks():
    wide = CLASSES * GROUP * 4
    column = lax.broadcasted_iota(jnp.int32, (4 * CLASSES, wide), 1)
    source = lax.broadcasted_iota(jnp.int32, (4 * CLASSES, wide), 0)
    pick = source == (column % 4) * CLASSES + column // (GROUP * 4)
    row = lax.broadcasted_iota(jnp.int32, (GROUP * CHAN_D, wide), 0)
    across = lax.broadcasted_iota(jnp.int32, (GROUP * CHAN_D, wide), 1)
    mask = row // CHAN_D == (across // 4) % GROUP
    return pick, mask


def big_head_of(head_b):
    pick, mask = head_masks()
    spread = matmul(head_b, pick.astype(bf16)).astype(bf16)
    tiled = jnp.tile(spread, (GROUP, 1))
    return jnp.where(mask, tiled, jnp.zeros_like(tiled))


def head_grad_of(grad_big):
    pick, mask = head_masks()
    masked = jnp.where(mask, grad_big, 0.0)
    folded = jnp.sum(masked.reshape(GROUP, CHAN_D, -1), axis=0)
    return lax.dot_general(
        folded, pick.astype(f32), (((1,), (1,)), ((), ())), precision=highest,
        preferred_element_type=f32,
    )


def stack_columns(value, width):
    count = value.shape[-1] // width
    return jnp.concatenate(
        [value[..., i * width : (i + 1) * width] for i in range(count)], axis=-2
    )


def unstack_columns(value, count):
    rows = value.shape[-2] // count
    return jnp.concatenate(
        [value[..., i * rows : (i + 1) * rows, :] for i in range(count)], axis=-1
    )


def pad_to(value, axis, size):
    widths = [(0, 0)] * value.ndim
    widths[axis] = (0, size - value.shape[axis])
    return jnp.pad(value, widths)


class Shared:
    def __init__(self, stem_w, embed_w, token_params, decoder_w):
        self.stem_rows = stem_w.shape[0]
        self.embed_rows = embed_w.shape[0]
        self.token_rows = token_params.shape[1]
        self.flat = decoder_w.shape[0]
        self.flat_rows = -(-self.flat // (2 * LANES * 16)) * 16
        self.stem_count = C_STEM // 2 // LANES
        self.embed_count = D // 2 // LANES
        self.cuts = [0]
        for rows in (
            self.stem_rows * self.stem_count,
            self.embed_rows * self.embed_count,
            self.token_rows,
            self.flat_rows,
        ):
            self.cuts.append(self.cuts[-1] + rows)

    def half_flat(self, flat):
        padded = pad_to(flat, flat.ndim - 1, 2 * self.flat_rows * LANES)
        return padded.reshape(flat.shape[:-1] + (2, self.flat_rows, LANES))

    def pieces(self, value):
        one, two, three, four = (
            value[..., a:b, :] for a, b in zip(self.cuts[:-1], self.cuts[1:], strict=True)
        )
        return (
            unstack_columns(one, self.stem_count),
            unstack_columns(two, self.embed_count),
            three,
            four,
        )


def half_columns(value, core, axis=-1):
    axis = axis % value.ndim
    size = value.shape[axis] // 2
    return lax.dynamic_slice_in_dim(value, core * size, size, axis)


def adamw(weight, grad, first, second, rate):
    first_new = beta_one * first + (1.0 - beta_one) * grad
    second_new = beta_two * second + (1.0 - beta_two) * grad * grad
    first_hat = first_new / (1.0 - beta_one**STEP)
    second_hat = second_new / (1.0 - beta_two**STEP)
    new_weight = weight - rate * (
        first_hat / (jnp.sqrt(second_hat) + adam_eps) + decay_rate * weight
    )
    return (new_weight, first_new, second_new)


def body(
    images,
    labels,
    background,
    patients,
    *state,
):
    masters, firsts, seconds = state[:9], state[9:18], state[18:]
    stem_w, embed_w, token_params, qkv_w, out_w, mlp_in_w, mlp_out_w, skip_w, decoder_w = masters
    n_dp = lax.axis_size("dp")
    n_mp = lax.axis_size("mp")
    mp_id = lax.axis_index("mp")
    core = mp_id & 1
    slices = images.shape[0] // n_mp
    rows = slices * PAD
    shared = Shared(stem_w, embed_w, token_params, decoder_w)
    attn_cut = qkv_w.shape[1]
    heads_each = attn_cut // (3 * HEAD_DIM)
    ctx_each = heads_each * HEAD_DIM
    in_each = mlp_in_w.shape[1]

    token_t = pad_to(token_params.T, 1, 2 * LANES)
    dec_half = lax.dynamic_index_in_dim(shared.half_flat(decoder_w), core, 0, keepdims=False)
    first_block = jnp.concatenate(
        [
            stack_columns(half_columns(stem_w, core), LANES),
            stack_columns(half_columns(embed_w, core), LANES),
            half_columns(token_t, core),
            dec_half,
        ],
        axis=0,
    ).astype(bf16)
    attn_block = jnp.concatenate([qkv_w, out_w.T], axis=1).astype(bf16)
    mlp_block = jnp.concatenate([mlp_in_w, mlp_out_w.T], axis=1).astype(bf16)
    skip_block = half_columns(skip_w, core).astype(bf16)

    first_all = double(gather_rows(first_block), "mp", 0, 0)
    first_all = first_all.reshape((2, n_dp) + first_block.shape)
    pieces = shared.pieces(first_all)
    stem_b = jnp.concatenate([pieces[0][0], pieces[0][1]], axis=-1).reshape(PIXELS, C_STEM)
    embed_b = jnp.concatenate([pieces[1][0], pieces[1][1]], axis=-1).reshape(C_STEM, D)
    token_all = jnp.concatenate([pieces[2][0], pieces[2][1]], axis=-1).reshape(D, 2 * LANES)
    tokens = token_all.T.astype(f32)[: PATCHES + 6]
    dec_flat = jnp.swapaxes(pieces[3], 0, 1).reshape(n_dp, -1)[:, : shared.flat].reshape(-1)
    dec_b, one_b, two_b, three_b, head_b = split_decoder(dec_flat)

    def gather_split(block):
        both = double(gather_rows(block), "mp", 1, 1)
        both = both.reshape(both.shape[0], -1)
        return double(both, "mp", 0, 0)

    attn_all = gather_split(attn_block)
    mlp_all = gather_split(mlp_block)
    skip_all = double(gather_rows(skip_block), "mp", 0, 0)

    attn_width = attn_block.shape[1]
    qkv_parts = [
        attn_all[c][:, x * attn_width : x * attn_width + attn_cut]
        for c in range(2)
        for x in range(2)
    ]
    out_parts = [
        attn_all[c][:, x * attn_width + attn_cut : (x + 1) * attn_width]
        for c in range(2)
        for x in range(2)
    ]
    in_parts = [
        mlp_all[c][:, 2 * x * in_each : (2 * x + 1) * in_each] for c in range(2) for x in range(2)
    ]
    down_parts = [
        mlp_all[c][:, (2 * x + 1) * in_each : (2 * x + 2) * in_each]
        for c in range(2)
        for x in range(2)
    ]
    qkv_b = jnp.concatenate(qkv_parts, axis=1)
    out_t = jnp.concatenate(out_parts, axis=1)
    in_b = jnp.concatenate(in_parts, axis=1)
    down_t = jnp.concatenate(down_parts, axis=1)
    skip_b = jnp.concatenate([skip_all[0], skip_all[1]], axis=1)

    take = lambda value: lax.dynamic_slice_in_dim(value, mp_id * slices, slices, 0)
    pixels = pad_to(take(images), 1, PAD).reshape(rows, PIXELS)
    label_own = jnp.pad(take(labels), ((0, 0), (0, PAD - PATCHES), (0, 0)), constant_values=-1)
    label_own = label_own.reshape(rows, PIXELS)
    keep = (1 - take(background)).astype(f32)
    owner = (take(patients)[:, None] == jnp.arange(PATIENTS, dtype=jnp.int32)).astype(f32)

    pos = jnp.tile(pad_to(tokens[:PATCHES], 0, PAD), (slices, 1))
    g1, b1, g2, b2, gf, bf = (tokens[PATCHES + i] for i in range(6))
    pre_stem = matmul(pixels, stem_b)
    hidden = gelu_fn(pre_stem).astype(bf16)
    embed = matmul(hidden, embed_b) + pos
    normed = layer_norm(embed, g1, b1).astype(bf16)
    triple = matmul(normed, qkv_b).astype(bf16)
    context = attn_forward(triple)
    resid = embed + matmul_t(context, out_t)
    normed2 = layer_norm(resid, g2, b2).astype(bf16)
    pre_inner = matmul(normed2, in_b)
    inner = gelu_fn(pre_inner).astype(bf16)
    resid2 = resid + matmul_t(inner, down_t)
    final_low = layer_norm(resid2, gf, bf).astype(bf16)
    pre_zero = matmul(final_low, dec_b)
    level0 = gelu_fn(pre_zero).astype(bf16)
    skips = matmul(hidden, skip_b)
    split_a = 4 * CHAN_B
    split_b = split_a + 16 * CHAN_C
    big_two = block_diag(two_b, 4)
    big_three = block_diag(three_b, 16)
    big_head = big_head_of(head_b)
    pre_one = matmul(level0, one_b) + skips[:, :split_a]
    level1 = gelu_fn(pre_one).astype(bf16)
    pre_two = matmul(level1, big_two) + skips[:, split_a:split_b]
    level2 = gelu_fn(pre_two).astype(bf16)
    pre_three = matmul(level2, big_three) + skips[:, split_b:]
    level3 = gelu_fn(pre_three).astype(bf16)
    logits, stats = loss_forward(level3, big_head, label_own)

    sums = jnp.sum(stats.reshape(slices, 3 * CLASSES + 1, 8 * LANES), axis=-1)
    class_sums = sums[:, : 3 * CLASSES]
    pat_sums = jnp.sum(owner[:, :, None] * class_sums[:, None, :], axis=0)
    cross_sum = jnp.sum(keep * sums[:, 3 * CLASSES])
    packed = jnp.concatenate(
        [pat_sums.reshape(-1), cross_sum[None], jnp.sum(keep)[None]]
    )
    packed = pad_to(packed, 0, 4 * LANES).reshape(4, LANES)
    packed = butterfly(packed).reshape(-1)
    pat_all = packed[: PATIENTS * 3 * CLASSES].reshape(PATIENTS, CLASSES, 3)
    ce_total = packed[PATIENTS * 3 * CLASSES]
    pixel_count = packed[PATIENTS * 3 * CLASSES + 1] * (PATCHES * PIXELS)
    pat_over, pat_pred, pat_true = pat_all[..., 0], pat_all[..., 1], pat_all[..., 2]
    denominator = pat_pred + pat_true + dice_eps
    dice = (2.0 * pat_over + dice_eps) / denominator
    count_floor = jnp.maximum(pixel_count, 1.0)
    loss = ce_total / count_floor + 1.0 - jnp.mean(dice)
    cells = PATIENTS * CLASSES
    over_coef = -2.0 / (cells * denominator)
    pred_coef = (2.0 * pat_over + dice_eps) / (cells * denominator * denominator)
    pick_own = lambda table: jnp.sum(owner[:, :, None] * table[None], axis=1)
    coef = jnp.concatenate(
        [pick_own(over_coef), pick_own(pred_coef), (keep / count_floor)[:, None]], axis=1
    )

    grad_level3, grad_big_head = loss_backward(coef, logits, label_own, level3, big_head)
    grad_head = head_grad_of(grad_big_head)
    grad_pre3 = gelu_back(pre_three, grad_level3).astype(bf16)
    grad_level2 = matmul_t(grad_pre3, big_three)
    grad_pre2 = gelu_back(pre_two, grad_level2).astype(bf16)
    grad_level1 = matmul_t(grad_pre2, big_two)
    grad_pre1 = gelu_back(pre_one, grad_level1).astype(bf16)

    def shared_pair(left, right):
        send = t_matmul(left, half_columns(right, 1 - core)).astype(bf16)
        return send, t_matmul(left, half_columns(right, core))

    def core_sum(send, own):
        return own + swap(send, "mp", 0).astype(f32)

    def shared_finish(kept):
        value = lax.reduce_precision(scatter_rows(kept), 8, 7).astype(bf16)
        return value.astype(f32) + swap(value, "mp", 1).astype(f32)

    grad_skips = jnp.concatenate([grad_pre1, grad_pre2, grad_pre3], axis=1)
    skip_half = shared_finish(core_sum(*shared_pair(hidden, grad_skips)))
    grad_hidden_skip = matmul_t(grad_skips, skip_b)
    grad_level0 = matmul_t(grad_pre1, one_b)
    grad_pre0 = gelu_back(pre_zero, grad_level0).astype(bf16)
    grad_final = matmul_t(grad_pre0, dec_b)
    grad_three = block_diag_grad(t_matmul(level2, grad_pre3), 16, CHAN_C, 4 * CHAN_D)
    grad_two = block_diag_grad(t_matmul(level1, grad_pre2), 4, CHAN_B, 4 * CHAN_C)
    grad_one = t_matmul(level0, grad_pre1)
    grad_dec = t_matmul(final_low, grad_pre0)
    grad_decoder = jnp.concatenate(
        [
            grad_dec.reshape(-1),
            grad_one.reshape(-1),
            grad_two.reshape(-1),
            grad_three.reshape(-1),
            grad_head.reshape(-1),
        ]
    )

    grad_resid2, grad_gf, grad_bf = norm_back(resid2, gf, bf, grad_final)
    grad_resid2_low = grad_resid2.astype(bf16)
    grad_inner = matmul(grad_resid2_low, down_t)
    grad_pre = gelu_back(pre_inner, grad_inner).astype(bf16)

    def mlp_half(which):
        g_in = t_matmul(normed2, half_columns(grad_pre, which))
        g_down = t_matmul(grad_resid2_low, half_columns(inner, which))
        return jnp.concatenate(
            [
                g_in[:, :in_each],
                g_down[:, :in_each],
                g_in[:, in_each:],
                g_down[:, in_each:],
            ],
            axis=1,
        )

    def split_finish(kept):
        width = kept.shape[1] // 2
        x = my_bit("mp", 1)
        send = lax.dynamic_slice_in_dim(kept, (1 - x) * width, width, 1).astype(bf16)
        own = lax.dynamic_slice_in_dim(kept, x * width, width, 1)
        return scatter_rows(own + swap(send, "mp", 1).astype(f32))

    mlp_own = split_finish(core_sum(mlp_half(1 - core).astype(bf16), mlp_half(core)))

    grad_resid_ln, grad_g2, grad_b2 = norm_back(resid, g2, b2, matmul_t(grad_pre, in_b))
    grad_resid = grad_resid2 + grad_resid_ln
    grad_resid_low = grad_resid.astype(bf16)
    grad_context = matmul(grad_resid_low, out_t).astype(bf16)
    grad_triple = attn_backward(triple, grad_context)

    def attn_half(which):
        g_qkv = t_matmul(normed, half_columns(grad_triple, which))
        g_out = t_matmul(grad_resid_low, half_columns(context, which))
        return jnp.concatenate(
            [
                g_qkv[:, :attn_cut],
                g_out[:, :ctx_each],
                g_qkv[:, attn_cut:],
                g_out[:, ctx_each:],
            ],
            axis=1,
        )

    attn_own = split_finish(core_sum(attn_half(1 - core).astype(bf16), attn_half(core)))

    grad_embed_ln, grad_g1, grad_b1 = norm_back(embed, g1, b1, matmul_t(grad_triple, qkv_b))
    grad_embed = grad_resid + grad_embed_ln
    gains = jnp.stack([grad_g1, grad_b1, grad_g2, grad_b2, grad_gf, grad_bf])
    grad_pos = jnp.sum(grad_embed.reshape(slices, PAD, D), axis=0)[:PATCHES]
    grad_token = pad_to(jnp.concatenate([grad_pos, gains], axis=0).T, 1, 2 * LANES)
    grad_embed_low = grad_embed.astype(bf16)
    grad_hidden = matmul_t(grad_embed_low, embed_b) + grad_hidden_skip
    grad_pre_stem = gelu_back(pre_stem, grad_hidden).astype(bf16)
    stem_pair = shared_pair(pixels, grad_pre_stem)
    embed_pair = shared_pair(hidden, grad_embed_low)
    decoder_halves = shared.half_flat(grad_decoder.reshape(n_dp, -1))

    def first_half(which, stem_part, embed_part):
        blocks = lambda value: value.reshape(n_dp, -1, value.shape[-1])
        packed_half = jnp.concatenate(
            [
                stack_columns(blocks(stem_part), LANES),
                stack_columns(blocks(embed_part), LANES),
                blocks(half_columns(grad_token, which)).astype(stem_part.dtype),
                lax.dynamic_index_in_dim(decoder_halves, which, 1, keepdims=False).astype(
                    stem_part.dtype
                ),
            ],
            axis=1,
        )
        return packed_half.reshape(-1, LANES)

    first_half_sum = shared_finish(
        core_sum(
            first_half(1 - core, stem_pair[0], embed_pair[0]),
            first_half(core, stem_pair[1], embed_pair[1]),
        )
    )

    square = lambda value: jnp.sum(value * value)
    n_copies = n_mp // 2
    local = (
        square(mlp_own)
        + square(attn_own)
        + (square(skip_half) + square(first_half_sum)) / n_copies
    )
    total = butterfly(jnp.broadcast_to(local, (8, LANES)))[0, 0]
    grad_norm = jnp.sqrt(total)
    factor = jnp.minimum(1.0, clip_limit / (grad_norm + 1e-06))

    skip_both = double(skip_half, "mp", 0, 0)
    red_skip = jnp.concatenate([skip_both[0], skip_both[1]], axis=1)
    own = shared.pieces(double(first_half_sum, "mp", 0, 0))
    red_stem = jnp.concatenate([own[0][0], own[0][1]], axis=-1)
    red_embed = jnp.concatenate([own[1][0], own[1][1]], axis=-1)
    token_both = jnp.concatenate([own[2][0], own[2][1]], axis=-1)
    red_token = token_both[:, : PATCHES + 6].T
    red_decoder = own[3].reshape(-1)[: shared.flat]
    red_qkv = attn_own[:, :attn_cut]
    red_out = attn_own[:, attn_cut:].T
    red_in = mlp_own[:, :in_each]
    red_down = mlp_own[:, in_each:].T
    reduced = (
        red_stem, red_embed, red_token, red_qkv, red_out, red_in, red_down, red_skip, red_decoder,
    )
    rates = [learn_rate] * 9
    rates[2] = token_rate
    results = [
        adamw(weight, grad * factor, first, second, rate)
        for weight, grad, first, second, rate in zip(
            masters, reduced, firsts, seconds, rates, strict=True
        )
    ]
    news = [item[0] for item in results]
    moms = [item[1] for item in results]
    secs = [item[2] for item in results]
    return (loss, pixel_count, grad_norm, *news, *moms, *secs)


def solution(mesh):
    weights = (
        P("dp", None),
        P("dp", None),
        P(None, "dp"),
        P("dp", "mp"),
        P("mp", "dp"),
        P("dp", "mp"),
        P("mp", "dp"),
        P("dp", None),
        P("dp"),
    )
    placed = (P("dp", None, None), P("dp", None, None), P("dp"), P("dp")) + weights * 3
    outs = (P(), P(), P()) + weights * 3
    return jax.shard_map(body, mesh=mesh, in_specs=placed, out_specs=outs, check_vma=False)
```

time: 1940 us -> 685 us (0.35)
  waiting for transfers between devices: 1050 us -> 252 us
  blocking collectives: 226 us -> 0 us
  matrix products: 264 us -> 100 us
  local copies, waits for them, and re-layouts: 211 us -> 133 us
  other arithmetic: 149 us -> 109 us
  starting transfers between devices: 1.96 us -> 40.5 us
  Pallas kernels: 0 us -> 30.1 us
    reduce_scatter x6 -> x0, waiting for transfers between devices: 526 us -> none  [the longest x1 177 us: body(): lax.psum_scatter(grad_skip, 'dp', scatter_dimension=0, tiled=True)]
    ppermute x0 -> x50, waiting for transfers between devices: none -> 252 us  [swap(): return lax.ppermute(value, axis, [(i, i ^ 1 << bit) for i in range(size)])]
    unnamed x22 -> x0, waiting for transfers between devices: 190 us -> none
    psum x4 -> x0, waiting for transfers between devices: 182 us -> none  [the longest x2 97.2 us: mp_sum(): return lax.psum(partial_value, 'mp')]
    dot_general x44 -> x41, matrix products: 259 us -> 100 us  [the longest x12 40.3 us: matmul(): return jnp.dot(left, right, preferred_element_type=f32)]
    all_gather x4 -> x0, waiting for transfers between devices: 153 us -> none  [the longest x1 79.3 us: body(): lax.all_gather(skip_w.astype(jnp.bfloat16), 'dp', axis=0, tiled=True)]
    all_gather x4 -> x0, blocking collectives: 129 us -> none  [the longest x1 33.5 us: body(): lax.all_gather(token_params.astype(jnp.bfloat16), 'dp', axis=1, tiled=True)]
    psum x3 -> x0, blocking collectives: 96.7 us -> none  [the longest x2 57.4 us: body(): lax.psum((local_stats[0], local_stats[1], local_stats[2], local_stats[3],...]
  transfers between devices with their start and end apart: 18 -> 50, of which waited for: 17 -> 31; matrix products, arithmetic and copies ran while one was open for 17% -> 28% of each run, Pallas kernels for 0% -> 1%
where the time goes in v1:
time: 685 us; the launch traced here: 678 us
  waiting for transfers between devices  252 us (37%)
  local copies, waits for them, and re-layouts  133 us (19%)
  other arithmetic  109 us (16%)
  matrix products  100 us (15%)
  starting transfers between devices  40.5 us (6%)
  Pallas kernels  30.1 us (4%)
  between operations  13.3 us (2%)
    ppermute x50, waiting for transfers between devices, swap(): return lax.ppermute(value, axis, [(i, i ^ 1 << bit) for i in range(size)])  252 us
    unnamed x498, local copies, waits for them, and re-layouts  45.8 us
    ppermute x50, starting transfers between devices, swap(): return lax.ppermute(value, axis, [(i, i ^ 1 << bit) for i in range(size)])  40.5 us
    dot_general x12, matrix products, matmul(): return jnp.dot(left, right, preferred_element_type=f32)  40.3 us
    dot_general x18, matrix products, t_matmul(): lax.dot_general(left, right, (((0,), (0,)), ((), ())), preferred_element_...  35.5 us
    dot_general x10, matrix products, matmul_t(): lax.dot_general(left, right, (((1,), (1,)), ((), ())), preferred_element_...  24 us
    another operation x30, other arithmetic, double(): return jnp.stack([low_half, high_half], axis=dim)  20.2 us
    select_n x5, other arithmetic, double(): low_half = jnp.where(mine == 0, value, other)  14.6 us
  transfers between devices with their start and end apart: 50, of which 31 were waited for; matrix products, arithmetic and copies ran while one was open for 28% of the time, Pallas kernels for 1%

profile of v1, /device:TPU:0, one launch (start us, length us, event | category | flops | bytes accessed | tf_op | source)
XLA Modules:
  0.0 678.3 jit_solution(13358024045853124771)
XLA Ops:
  27.7 23.5 %collective-permute-done.4 = bf16[96,768]{1,0:T(8,128)(2,1)} collective-permute-done((bf16[96,768]{1,0:T(8,128)(2,1)}, bf16[96,768]{1,0:T(8,128)(2,1)}, u32[]{:S(2)}, u32[]{:S(2)}) %collective-permute-start.4) | collective-permute-done | bytes 147488 | tf_op jit(solution)/shard_map/ppermute | solution.py:71
  64.8 7.0 %collective-permute-done.1 = bf16[2,800,128]{2,1,0:T(8,128)(2,1)S(1)} collective-permute-done((bf16[2,800,128]{2,1,0:T(8,128)(2,1)S(1)}, bf16[2,800,128]{2,1,0:T(8,128)(2,1)S(1)}, u32[]{:S(2)}, u32[]{:S(2)}) %collective-permute-start.1) | collective-permute-done | bytes 409632 | tf_op jit(solution)/shard_map/ppermute | solution.py:71
  73.6 10.8 %collective-permute-done.10 = bf16[2,96,1536]{2,1,0:T(8,128)(2,1)S(1)} collective-permute-done((bf16[2,96,1536]{2,1,0:T(8,128)(2,1)S(1)}, bf16[2,96,1536]{2,1,0:T(8,128)(2,1)S(1)}, u32[]{:S(2)}, u32[]{:S(2)}) %collective-permute-start.10) | collective-permute-done | bytes 589856 | tf_op jit(solution)/shard_map/ppermute | solution.py:71
  86.3 12.1 %collective-permute-done.15 = bf16[2,128,1280]{2,1,0:T(8,128)(2,1)S(1)} collective-permute-done((bf16[2,128,1280]{2,1,0:T(8,128)(2,1)S(1)}, bf16[2,128,1280]{2,1,0:T(8,128)(2,1)S(1)}, u32[]{:S(2)}, u32[]{:S(2)}) %collective-permute-start.15) | collective-permute-done | bytes 655392 | tf_op jit(solution)/shard_map/ppermute | solution.py:71
  104.7 17.5 %collective-permute-done.11 = bf16[2,2,96,1536]{3,2,1,0:T(8,128)(2,1)S(1)} collective-permute-done((bf16[2,2,96,1536]{3,2,1,0:T(8,128)(2,1)S(1)}, bf16[2,2,96,1536]{3,2,1,0:T(8,128)(2,1)S(1)}, u32[]{:S(2)}, u32[]{:S(2)}) %collective-permute-start.11) | collective-permute-done | bytes 1179680 | tf_op jit(solution)/shard_map/ppermute | solution.py:71
  125.6 4.9 collective-permute-done.7
  133.7 15.7 %collective-permute-done.16 = bf16[2,2,128,1280]{3,2,1,0:T(8,128)(2,1)} collective-permute-done((bf16[2,2,128,1280]{3,2,1,0:T(8,128)(2,1)}, bf16[2,2,128,1280]{3,2,1,0:T(8,128)(2,1)}, u32[]{:S(2)}, u32[]{:S(2)}) %collective-permute-start.16) | collective-permute-done | bytes 1310752 | tf_op jit(solution)/shard_map/ppermute | solution.py:71
  171.1 8.9 %collective-permute-done.12 = bf16[768,1536]{1,0:T(8,128)(2,1)} collective-permute-done((bf16[768,1536]{1,0:T(8,128)(2,1)}, bf16[768,1536]{1,0:T(8,128)(2,1)}, u32[]{:S(2)}, u32[]{:S(2)}) %collective-permute-start.12) | collective-permute-done | bytes 2359328 | tf_op jit(solution)/shard_map/ppermute | solution.py:71
  185.2 6.7 copy.346
  201.8 6.6 tile.42
  213.6 5.3 convolution_convert_fusion.tri_ref
  218.9 6.1 attn_forward.1
  234.1 6.5 broadcast_select_fusion.1
  245.1 5.1 multiply_convert_fusion
  309.5 6.7 loss_backward.1
  319.9 5.0 fusion.26
  332.9 13.7 %fusion.6 = bf16[416,3072]{1,0:T(8,128)(2,1)S(1)} fusion(f32[416,3072]{1,0:T(8,128)S(1)} %bitcast.402, bf16[416,768]{1,0:T(8,128)(2,1)S(1)} %add_convert_fusion.3, bf16[768,768]{0,1:T(8,128)(2,1)S(1)} %copy-done.67, bf16[768,768]{0,1:T(8,128)(2,1)S(1)} %copy-done.69, bf16[768,768]{0,1:T(8,128)(2,1)S(1)} %copy-done.65, bf16[768,768]{0,1:T(8,128)(2,1)S(1)} %copy-done.63), kind=kOutput, calls=%fused_computation.11 | convolution fusion | flops 2007367680 | bytes 13025280 | tf_op jit(solution)/shard_map/dot_general | solution.py:50
  359.8 13.4 %attn_backward.1 = bf16[416,2304]{1,0:T(8,128)(2,1)S(1)} custom-call(bf16[416,2304]{1,0:T(8,128)(2,1)S(1)} %convolution_convert_fusion.tri_ref, bf16[416,768]{1,0:T(8,128)(2,1)S(1)} %convolution_convert_fusion.7.gctx_ref), custom_call_target="tpu_custom_call" | custom-call | tf_op jit(solution)/shard_map/attn_backward/pallas_call | solution.py:189
  398.3 5.3 concatenate.135
  404.3 4.9 convolution_convert_fusion.1
  462.4 6.3 concatenate.134
  474.3 5.4 collective-permute-done.39
  496.1 6.9 %collective-permute-done.41 = bf16[800,128]{1,0:T(8,128)(2,1)S(1)} collective-permute-done((bf16[800,128]{1,0:T(8,128)(2,1)S(1)}, bf16[800,128]{1,0:T(8,128)(2,1)S(1)}, u32[]{:S(2)}, u32[]{:S(2)}) %collective-permute-start.41) | collective-permute-done | bytes 204832 | tf_op jit(solution)/shard_map/ppermute | solution.py:71
  505.3 11.6 %collective-permute-done.42 = bf16[800,128]{1,0:T(8,128)(2,1)S(1)} collective-permute-done((bf16[800,128]{1,0:T(8,128)(2,1)S(1)}, bf16[800,128]{1,0:T(8,128)(2,1)S(1)}, u32[]{:S(2)}, u32[]{:S(2)}) %collective-permute-start.42) | collective-permute-done | bytes 204832 | tf_op jit(solution)/shard_map/ppermute | solution.py:71
  525.9 10.8 %collective-permute-done.34 = bf16[2,2,128,1280]{3,2,0,1:T(8,128)(2,1)} collective-permute-done((bf16[2,2,128,1280]{3,2,0,1:T(8,128)(2,1)S(1)}, bf16[2,2,128,1280]{3,2,0,1:T(8,128)(2,1)}, u32[]{:S(2)}, u32[]{:S(2)}) %collective-permute-start.34) | collective-permute-done | bytes 1310752 | tf_op jit(solution)/shard_map/ppermute | solution.py:71
  540.3 6.7 collective-permute-done.30
  547.2 6.6 collective-permute-done.35
  553.9 21.8 %collective-permute-done.24 = bf16[768,1536]{1,0:T(8,128)(2,1)S(1)} collective-permute-done((bf16[768,1536]{1,0:T(8,128)(2,1)S(1)}, bf16[768,1536]{1,0:T(8,128)(2,1)S(1)}, u32[]{:S(2)}, u32[]{:S(2)}) %collective-permute-start.24) | collective-permute-done | bytes 2359328 | tf_op jit(solution)/shard_map/ppermute | solution.py:71
  578.2 15.9 %collective-permute-done.36 = bf16[128,1280]{1,0:T(8,128)(2,1)S(1)} collective-permute-done((bf16[128,1280]{1,0:T(8,128)(2,1)S(1)}, bf16[128,1280]{1,0:T(8,128)(2,1)S(1)}, u32[]{:S(2)}, u32[]{:S(2)}) %collective-permute-start.36) | collective-permute-done | bytes 327712 | tf_op jit(solution)/shard_map/ppermute | solution.py:71
  595.7 8.7 %collective-permute-done.25 = bf16[2,2,96,1536]{3,2,0,1:T(8,128)(2,1)S(1)} collective-permute-done((bf16[2,2,96,1536]{3,2,0,1:T(8,128)(2,1)S(1)}, bf16[2,2,96,1536]{3,2,0,1:T(8,128)(2,1)S(1)}, u32[]{:S(2)}, u32[]{:S(2)}) %collective-permute-start.25) | collective-permute-done | bytes 1179680 | tf_op jit(solution)/shard_map/ppermute | solution.py:71
  606.1 16.1 %collective-permute-done.26 = bf16[2,96,1536]{2,1,0:T(8,128)(2,1)S(1)} collective-permute-done((bf16[2,96,1536]{2,1,0:T(8,128)(2,1)S(1)}, bf16[2,96,1536]{2,1,0:T(8,128)(2,1)S(1)}, u32[]{:S(2)}, u32[]{:S(2)}) %collective-permute-start.26) | collective-permute-done | bytes 589856 | tf_op jit(solution)/shard_map/ppermute | solution.py:71
  626.5 10.9 %collective-permute-done.27 = bf16[96,1536]{1,0:T(8,128)(2,1)} collective-permute-done((bf16[96,1536]{1,0:T(8,128)(2,1)}, bf16[96,1536]{1,0:T(8,128)(2,1)}, u32[]{:S(2)}, u32[]{:S(2)}) %collective-permute-start.27) | collective-permute-done | bytes 294944 | tf_op jit(solution)/shard_map/ppermute | solution.py:71
  (861 shorter events, 351.6 us)
Async XLA Ops:
  9.9 42.5 %collective-permute-start = (bf16[800,128]{1,0:T(8,128)(2,1)}, bf16[800,128]{1,0:T(8,128)(2,1)}, u32[]{:S(2)}, u32[]{:S(2)}) collective-permute-start(bf16[800,128]{1,0:T(8,128)(2,1)} %constant_dynamic-update-slice_fusion), channel_id=1, source_target_pairs={{0,16},{4,20},{8,24},{12,28},{16,0},{20,4},{24,8},{28,12},{1,17},{... | collective-permute-start | bytes 614408 | tf_op jit(solution)/shard_map/ppermute | solution.py:71
  15.8 42.9 %collective-permute-start.14 = (bf16[128,1280]{1,0:T(8,128)(2,1)}, bf16[128,1280]{1,0:T(8,128)(2,1)}, u32[]{:S(2)}, u32[]{:S(2)}) collective-permute-start(bf16[128,1280]{1,0:T(8,128)(2,1)} %dynamic-slice_convert_fusion.8), channel_id=1, source_target_pairs={{0,16},{4,20},{8,24},{12,28},{16,0},{20,4},{24,8},{28,12},{1,17},{... | collective-permute-start | bytes 983048 | tf_op jit(solution)/shard_map/ppermute | solution.py:71
  16.7 34.5 %collective-permute-start.4 = (bf16[96,768]{1,0:T(8,128)(2,1)}, bf16[96,768]{1,0:T(8,128)(2,1)}, u32[]{:S(2)}, u32[]{:S(2)}) collective-permute-start(bf16[96,768]{1,0:T(8,128)(2,1)} %pad_maximum_fusion.51), channel_id=1, source_target_pairs={{0,16},{4,20},{8,24},{12,28},{16,0},{20,4},{24,8},{28,12},{1,17},{... | collective-permute-start | bytes 442376 | tf_op jit(solution)/shard_map/ppermute | solution.py:71
  20.4 36.4 %collective-permute-start.9 = (bf16[96,1536]{1,0:T(8,128)(2,1)}, bf16[96,1536]{1,0:T(8,128)(2,1)}, u32[]{:S(2)}, u32[]{:S(2)}) collective-permute-start(bf16[96,1536]{1,0:T(8,128)(2,1)} %pad_maximum_fusion.47), channel_id=1, source_target_pairs={{0,16},{4,20},{8,24},{12,28},{16,0},{20,4},{24,8},{28,12},{1,17},{... | collective-permute-start | bytes 884744 | tf_op jit(solution)/shard_map/ppermute | solution.py:71
  53.5 18.3 %collective-permute-start.1 = (bf16[2,800,128]{2,1,0:T(8,128)(2,1)S(1)}, bf16[2,800,128]{2,1,0:T(8,128)(2,1)S(1)}, u32[]{:S(2)}, u32[]{:S(2)}) collective-permute-start(bf16[2,800,128]{2,1,0:T(8,128)(2,1)S(1)} %pad_maximum_fusion.42), channel_id=1, source_target_pairs={{0,8},{4,12},{8,0},{12,4},{16,24},{20,28},{24,16},{28,20},{1,9},{5... | collective-permute-start | bytes 1228808 | tf_op jit(solution)/shard_map/ppermute | solution.py:71
  58.0 26.5 %collective-permute-start.10 = (bf16[2,96,1536]{2,1,0:T(8,128)(2,1)S(1)}, bf16[2,96,1536]{2,1,0:T(8,128)(2,1)S(1)}, u32[]{:S(2)}, u32[]{:S(2)}) collective-permute-start(bf16[2,96,1536]{2,1,0:T(8,128)(2,1)S(1)} %pad_maximum_fusion.37), channel_id=1, source_target_pairs={{0,8},{4,12},{8,0},{12,4},{16,24},{20,28},{24,16},{28,20},{1,9},{5... | collective-permute-start | bytes 1769480 | tf_op jit(solution)/shard_map/ppermute | solution.py:71
  60.1 38.3 %collective-permute-start.15 = (bf16[2,128,1280]{2,1,0:T(8,128)(2,1)S(1)}, bf16[2,128,1280]{2,1,0:T(8,128)(2,1)S(1)}, u32[]{:S(2)}, u32[]{:S(2)}) collective-permute-start(bf16[2,128,1280]{2,1,0:T(8,128)(2,1)S(1)} %pad_maximum_fusion.33), channel_id=1, source_target_pairs={{0,8},{4,12},{8,0},{12,4},{16,24},{20,28},{24,16},{28,20},{1,9},{5... | collective-permute-start | bytes 1966088 | tf_op jit(solution)/shard_map/ppermute | solution.py:71
  63.2 38.2 %collective-permute-start.6 = (bf16[2,2,96,768]{3,2,1,0:T(8,128)(2,1)S(1)}, bf16[2,2,96,768]{3,2,1,0:T(8,128)(2,1)S(1)}, u32[]{:S(2)}, u32[]{:S(2)}) collective-permute-start(bf16[2,2,96,768]{3,2,1,0:T(8,128)(2,1)S(1)} %pad_maximum_fusion.36), channel_id=1, source_target_pairs={{0,4},{4,0},{8,12},{12,8},{16,20},{20,16},{24,28},{28,24},{1,5},{5... | collective-permute-start | bytes 1769480 | tf_op jit(solution)/shard_map/ppermute | solution.py:71
  72.0 31.1 %collective-permute-start.2 = (bf16[2,2,800,128]{3,2,0,1:T(8,128)(2,1)S(1)}, bf16[2,2,800,128]{3,2,0,1:T(8,128)(2,1)S(1)}, u32[]{:S(2)}, u32[]{:S(2)}) collective-permute-start(bf16[2,2,800,128]{3,2,0,1:T(8,128)(2,1)S(1)} %pad_maximum_fusion.25), channel_id=1, source_target_pairs={{0,4},{4,0},{8,12},{12,8},{16,20},{20,16},{24,28},{28,24},{1,5},{5... | collective-permute-start | bytes 2457608 | tf_op jit(solution)/shard_map/ppermute | solution.py:71
  84.7 37.6 %collective-permute-start.11 = (bf16[2,2,96,1536]{3,2,1,0:T(8,128)(2,1)S(1)}, bf16[2,2,96,1536]{3,2,1,0:T(8,128)(2,1)S(1)}, u32[]{:S(2)}, u32[]{:S(2)}) collective-permute-start(bf16[2,2,96,1536]{3,2,1,0:T(8,128)(2,1)S(1)} %pad_maximum_fusion.22), channel_id=1, source_target_pairs={{0,4},{4,0},{8,12},{12,8},{16,20},{20,16},{24,28},{28,24},{1,5},{5... | collective-permute-start | bytes 3538952 | tf_op jit(solution)/shard_map/ppermute | solution.py:71
  99.8 49.6 %collective-permute-start.16 = (bf16[2,2,128,1280]{3,2,1,0:T(8,128)(2,1)}, bf16[2,2,128,1280]{3,2,1,0:T(8,128)(2,1)}, u32[]{:S(2)}, u32[]{:S(2)}) collective-permute-start(bf16[2,2,128,1280]{3,2,1,0:T(8,128)(2,1)} %pad_maximum_fusion.19), channel_id=1, source_target_pairs={{0,4},{4,0},{8,12},{12,8},{16,20},{20,16},{24,28},{28,24},{1,5},{5... | collective-permute-start | bytes 3932168 | tf_op jit(solution)/shard_map/ppermute | solution.py:71
  101.6 28.9 %collective-permute-start.7 = (bf16[768,768]{1,0:T(8,128)(2,1)S(1)}, bf16[768,768]{1,0:T(8,128)(2,1)S(1)}, u32[]{:S(2)}, u32[]{:S(2)}) collective-permute-start(bf16[768,768]{1,0:T(8,128)(2,1)S(1)} %bitcast.356), channel_id=1, source_target_pairs={{0,2},{1,3},{2,0},{3,1},{4,6},{5,7},{6,4},{7,5},{8,10},{9,11},{10,... | collective-permute-start | bytes 3538952 | tf_op jit(solution)/shard_map/ppermute | solution.py:71
  104.7 48.0 %collective-permute-start.3 = (bf16[6400,128]{1,0:T(8,128)(2,1)}, bf16[6400,128]{1,0:T(8,128)(2,1)}, u32[]{:S(2)}, u32[]{:S(2)}) collective-permute-start(bf16[6400,128]{1,0:T(8,128)(2,1)} %bitcast.10), channel_id=1, source_target_pairs={{0,1},{1,0},{2,3},{3,2},{4,5},{5,4},{6,7},{7,6},{8,9},{9,8},{10,11... | collective-permute-start | bytes 4915208 | tf_op jit(solution)/shard_map/ppermute | solution.py:71
  124.0 55.9 %collective-permute-start.12 = (bf16[768,1536]{1,0:T(8,128)(2,1)}, bf16[768,1536]{1,0:T(8,128)(2,1)}, u32[]{:S(2)}, u32[]{:S(2)}) collective-permute-start(bf16[768,1536]{1,0:T(8,128)(2,1)} %bitcast.43), channel_id=1, source_target_pairs={{0,2},{1,3},{2,0},{3,1},{4,6},{5,7},{6,4},{7,5},{8,10},{9,11},{10,... | collective-permute-start | bytes 7077896 | tf_op jit(solution)/shard_map/ppermute | solution.py:71
  133.7 77.4 %collective-permute-start.8 = (bf16[768,1536]{0,1:T(8,128)(2,1)}, bf16[768,1536]{0,1:T(8,128)(2,1)}, u32[]{:S(2)}, u32[]{:S(2)}) collective-permute-start(bf16[768,1536]{0,1:T(8,128)(2,1)} %bitcast.344), channel_id=1, source_target_pairs={{0,1},{1,0},{2,3},{3,2},{4,5},{5,4},{6,7},{7,6},{8,9},{9,8},{10,11... | collective-permute-start | bytes 7077896 | tf_op jit(solution)/shard_map/ppermute | solution.py:71
  152.8 73.8 %collective-permute-start.17 = (bf16[1024,1280]{1,0:T(8,128)(2,1)}, bf16[1024,1280]{1,0:T(8,128)(2,1)}, u32[]{:S(2)}, u32[]{:S(2)}) collective-permute-start(bf16[1024,1280]{1,0:T(8,128)(2,1)} %bitcast.56), channel_id=1, source_target_pairs={{0,1},{1,0},{2,3},{3,2},{4,5},{5,4},{6,7},{7,6},{8,9},{9,8},{10,11... | collective-permute-start | bytes 7864328 | tf_op jit(solution)/shard_map/ppermute | solution.py:71
  191.9 42.2 %collective-permute-start.13 = (bf16[768,3072]{0,1:T(8,128)(2,1)}, bf16[768,3072]{0,1:T(8,128)(2,1)}, u32[]{:S(2)}, u32[]{:S(2)}) collective-permute-start(bf16[768,3072]{0,1:T(8,128)(2,1)} %bitcast.337), channel_id=1, source_target_pairs={{0,1},{1,0},{2,3},{3,2},{4,5},{5,4},{6,7},{7,6},{8,9},{9,8},{10,11... | collective-permute-start | bytes 14155784 | tf_op jit(solution)/shard_map/ppermute | solution.py:71
  394.5 123.2 %collective-permute-start.23 = (bf16[768,3072]{1,0:T(8,128)(2,1)}, bf16[768,3072]{1,0:T(8,128)(2,1)}, u32[]{:S(2)}, u32[]{:S(2)}) collective-permute-start(bf16[768,3072]{1,0:T(8,128)(2,1)} %pad_maximum_fusion.4), channel_id=1, source_target_pairs={{0,1},{1,0},{2,3},{3,2},{4,5},{5,4},{6,7},{7,6},{8,9},{9,8},{10,11... | collective-permute-start | bytes 14155784 | tf_op jit(solution)/shard_map/ppermute | solution.py:71
  403.7 79.4 %collective-permute-start.28 = (bf16[768,1536]{1,0:T(8,128)(2,1)}, bf16[768,1536]{1,0:T(8,128)(2,1)}, u32[]{:S(2)}, u32[]{:S(2)}) collective-permute-start(bf16[768,1536]{1,0:T(8,128)(2,1)} %concatenate.135), channel_id=1, source_target_pairs={{0,1},{1,0},{2,3},{3,2},{4,5},{5,4},{6,7},{7,6},{8,9},{9,8},{10,11... | collective-permute-start | bytes 7077896 | tf_op jit(solution)/shard_map/ppermute | solution.py:71
  409.1 83.6 %collective-permute-start.33 = (bf16[1024,1280]{1,0:T(8,128)(2,1)}, bf16[1024,1280]{1,0:T(8,128)(2,1)}, u32[]{:S(2)}, u32[]{:S(2)}) collective-permute-start(bf16[1024,1280]{1,0:T(8,128)(2,1)} %convolution_convert_fusion.1), channel_id=1, source_target_pairs={{0,1},{1,0},{2,3},{3,2},{4,5},{5,4},{6,7},{7,6},{8,9},{9,8},{10,11... | collective-permute-start | bytes 7864328 | tf_op jit(solution)/shard_map/ppermute | solution.py:71
  459.2 20.5 %collective-permute-start.39 = (bf16[2,2,800,128]{3,2,1,0:T(8,128)(2,1)}, bf16[2,2,800,128]{3,2,1,0:T(8,128)(2,1)}, u32[]{:S(2)}, u32[]{:S(2)}) collective-permute-start(bf16[2,2,800,128]{3,2,1,0:T(8,128)(2,1)} %fusion.63), channel_id=1, source_target_pairs={{0,4},{4,0},{8,12},{12,8},{16,20},{20,16},{24,28},{28,24},{1,5},{5... | collective-permute-start | bytes 2457608 | tf_op jit(solution)/shard_map/ppermute | solution.py:71
  485.7 37.9 %collective-permute-start.29 = (bf16[768,768]{1,0:T(8,128)(2,1)S(1)}, bf16[768,768]{1,0:T(8,128)(2,1)}, u32[]{:S(2)}, u32[]{:S(2)}) collective-permute-start(bf16[768,768]{1,0:T(8,128)(2,1)S(1)} %dynamic-slice_convert_fusion.1), channel_id=1, source_target_pairs={{0,2},{1,3},{2,0},{3,1},{4,6},{5,7},{6,4},{7,5},{8,10},{9,11},{10,... | collective-permute-start | bytes 3538952 | tf_op jit(solution)/shard_map/ppermute | solution.py:71
  504.8 31.9 %collective-permute-start.34 = (bf16[2,2,128,1280]{3,2,0,1:T(8,128)(2,1)S(1)}, bf16[2,2,128,1280]{3,2,0,1:T(8,128)(2,1)}, u32[]{:S(2)}, u32[]{:S(2)}) collective-permute-start(bf16[2,2,128,1280]{3,2,0,1:T(8,128)(2,1)S(1)} %fusion.39), channel_id=1, source_target_pairs={{0,4},{4,0},{8,12},{12,8},{16,20},{20,16},{24,28},{28,24},{1,5},{5... | collective-permute-start | bytes 3932168 | tf_op jit(solution)/shard_map/ppermute | solution.py:71
  517.7 20.8 %collective-permute-start.48 = (f32[800,128]{1,0:T(8,128)}, f32[800,128]{1,0:T(8,128)}, u32[]{:S(2)}, u32[]{:S(2)}) collective-permute-start(f32[800,128]{1,0:T(8,128)} %convert_add_fusion.5), channel_id=1, source_target_pairs={{0,1},{1,0},{2,3},{3,2},{4,5},{5,4},{6,7},{7,6},{8,9},{9,8},{10,11... | collective-permute-start | bytes 1228808 | tf_op jit(solution)/shard_map/ppermute | solution.py:71
  522.0 53.7 %collective-permute-start.24 = (bf16[768,1536]{1,0:T(8,128)(2,1)S(1)}, bf16[768,1536]{1,0:T(8,128)(2,1)S(1)}, u32[]{:S(2)}, u32[]{:S(2)}) collective-permute-start(bf16[768,1536]{1,0:T(8,128)(2,1)S(1)} %dynamic-slice_convert_fusion), channel_id=1, source_target_pairs={{0,2},{1,3},{2,0},{3,1},{4,6},{5,7},{6,4},{7,5},{8,10},{9,11},{10,... | collective-permute-start | bytes 7077896 | tf_op jit(solution)/shard_map/ppermute | solution.py:71
  525.3 21.6 %collective-permute-start.30 = (bf16[2,2,96,768]{3,2,1,0:T(8,128)(2,1)S(1)}, bf16[2,2,96,768]{3,2,1,0:T(8,128)(2,1)S(1)}, u32[]{:S(2)}, u32[]{:S(2)}) collective-permute-start(bf16[2,2,96,768]{3,2,1,0:T(8,128)(2,1)S(1)} %fusion.73), channel_id=1, source_target_pairs={{0,4},{4,0},{8,12},{12,8},{16,20},{20,16},{24,28},{28,24},{1,5},{5... | collective-permute-start | bytes 1769480 | tf_op jit(solution)/shard_map/ppermute | solution.py:71
  547.1 31.1 %collective-permute-start.31 = (bf16[2,96,768]{2,1,0:T(8,128)(2,1)S(1)}, bf16[2,96,768]{2,1,0:T(8,128)(2,1)S(1)}, u32[]{:S(2)}, u32[]{:S(2)}) collective-permute-start(bf16[2,96,768]{2,1,0:T(8,128)(2,1)S(1)} %fusion.111), channel_id=1, source_target_pairs={{0,8},{4,12},{8,0},{12,4},{16,24},{20,28},{24,16},{28,20},{1,9},{5... | collective-permute-start | bytes 884744 | tf_op jit(solution)/shard_map/ppermute | solution.py:71
  576.7 27.7 %collective-permute-start.25 = (bf16[2,2,96,1536]{3,2,0,1:T(8,128)(2,1)S(1)}, bf16[2,2,96,1536]{3,2,0,1:T(8,128)(2,1)S(1)}, u32[]{:S(2)}, u32[]{:S(2)}) collective-permute-start(bf16[2,2,96,1536]{3,2,0,1:T(8,128)(2,1)S(1)} %fusion.46), channel_id=1, source_target_pairs={{0,4},{4,0},{8,12},{12,8},{16,20},{20,16},{24,28},{28,24},{1,5},{5... | collective-permute-start | bytes 3538952 | tf_op jit(solution)/shard_map/ppermute | solution.py:71
  577.3 16.8 %collective-permute-start.36 = (bf16[128,1280]{1,0:T(8,128)(2,1)S(1)}, bf16[128,1280]{1,0:T(8,128)(2,1)S(1)}, u32[]{:S(2)}, u32[]{:S(2)}) collective-permute-start(bf16[128,1280]{1,0:T(8,128)(2,1)S(1)} %fusion.101), channel_id=1, source_target_pairs={{0,16},{4,20},{8,24},{12,28},{16,0},{20,4},{24,8},{28,12},{1,17},{... | collective-permute-start | bytes 983048 | tf_op jit(solution)/shard_map/ppermute | solution.py:71
  604.9 17.3 %collective-permute-start.26 = (bf16[2,96,1536]{2,1,0:T(8,128)(2,1)S(1)}, bf16[2,96,1536]{2,1,0:T(8,128)(2,1)S(1)}, u32[]{:S(2)}, u32[]{:S(2)}) collective-permute-start(bf16[2,96,1536]{2,1,0:T(8,128)(2,1)S(1)} %fusion.72), channel_id=1, source_target_pairs={{0,8},{4,12},{8,0},{12,4},{16,24},{20,28},{24,16},{28,20},{1,9},{5... | collective-permute-start | bytes 1769480 | tf_op jit(solution)/shard_map/ppermute | solution.py:71
  605.3 17.8 %collective-permute-start.32 = (bf16[96,768]{1,0:T(8,128)(2,1)S(1)}, bf16[96,768]{1,0:T(8,128)(2,1)S(1)}, u32[]{:S(2)}, u32[]{:S(2)}) collective-permute-start(bf16[96,768]{1,0:T(8,128)(2,1)S(1)} %fusion.116), channel_id=1, source_target_pairs={{0,16},{4,20},{8,24},{12,28},{16,0},{20,4},{24,8},{28,12},{1,17},{... | collective-permute-start | bytes 442376 | tf_op jit(solution)/shard_map/ppermute | solution.py:71
  606.0 18.4 %collective-permute-start.49 = (f32[128,1280]{1,0:T(8,128)S(1)}, f32[128,1280]{1,0:T(8,128)S(1)}, u32[]{:S(2)}, u32[]{:S(2)}) collective-permute-start(f32[128,1280]{1,0:T(8,128)S(1)} %convert_add_fusion.4), channel_id=1, source_target_pairs={{0,1},{1,0},{2,3},{3,2},{4,5},{5,4},{6,7},{7,6},{8,9},{9,8},{10,11... | collective-permute-start | bytes 1966088 | tf_op jit(solution)/shard_map/ppermute | solution.py:71
  (249 other events, 3063.5 us)

commit v2 on v1

v2 whole, which is shorter than its diff:
```python
import jax
import jax.numpy as jnp
from jax import lax
from jax.experimental import pallas as pl
from jax.experimental.pallas import tpu as pltpu
from jax.sharding import PartitionSpec as P

D = 768
HEAD_DIM = 64
PATCHES = 196
PAD = 208
PIXELS = 256
C_STEM = 1024
CHAN_A = 256
CHAN_B = 128
CHAN_C = 64
CHAN_D = 16
CLASSES = 9
PATIENTS = 16
STEP = 10
GROUP = 32
LANES = 128

norm_eps = 1e-06
dice_eps = 1e-05
clip_limit = 0.002
learn_rate = 0.05
token_rate = 0.5
beta_one = 0.9
beta_two = 0.999
adam_eps = 1e-08
decay_rate = 0.01
highest = lax.Precision.HIGHEST
bf16 = jnp.bfloat16
f32 = jnp.float32
MIB = 1024 * 1024


def layer_norm(inputs, gain, shift):
    center = inputs - jnp.mean(inputs, axis=-1, keepdims=True)
    spread = jnp.mean(center * center, axis=-1, keepdims=True)
    return center * lax.rsqrt(spread + norm_eps) * gain + shift


def matmul(left, right):
    return jnp.dot(left, right, preferred_element_type=f32)


def matmul_t(left, right):
    return lax.dot_general(left, right, (((1,), (1,)), ((), ())), preferred_element_type=f32)


def t_matmul(left, right):
    return lax.dot_general(left, right, (((0,), (0,)), ((), ())), preferred_element_type=f32)


FULL = pl.BlockSpec(memory_space=pltpu.VMEM)
SCALAR = pl.BlockSpec(memory_space=pltpu.SMEM)
BLOCK = 256
CHUNK = 16
GELU_SCALE = 0.7978845608028654
GELU_CUBE = 0.044715


def cost(micros):
    return pl.CostEstimate(
        flops=int(micros * 3e9), bytes_accessed=int(micros * 9e6), transcendentals=0
    )


def params():
    return pltpu.CompilerParams(vmem_limit_bytes=58 * MIB)


def run_after(kernel, count, after):
    extra = len(after)

    def ordered(*refs):
        kernel(*refs[:count], *refs[count + extra :])

    return ordered, [pl.BlockSpec(memory_space=pl.ANY)] * extra


def swap(value, axis, bit):
    size = lax.axis_size(axis)
    return lax.ppermute(value, axis, [(i, i ^ (1 << bit)) for i in range(size)])


def my_bit(axis, bit):
    return (lax.axis_index(axis) >> bit) & 1


def log_two(size):
    return size.bit_length() - 1


def gather_kernel(lanes, mine_ref, own_ref, other_ref, out_ref):
    mine = mine_ref[0]
    for which, source_ref in ((mine, own_ref), (1 - mine, other_ref)):
        if lanes:
            width = own_ref.shape[1]
            out_ref[:, pl.ds(pl.multiple_of(which * width, LANES), width)] = source_ref[...]
        else:
            for a in range(out_ref.shape[0]):
                out_ref[a, which] = source_ref[a]


def gate_kernel(value_ref, *refs):
    pass


def run_gate(value, *tokens):
    anywhere = pl.BlockSpec(memory_space=pl.ANY)
    return pl.pallas_call(
        gate_kernel,
        in_specs=[anywhere] * (1 + len(tokens)),
        out_specs=anywhere,
        out_shape=jax.ShapeDtypeStruct(value.shape, value.dtype),
        input_output_aliases={0: 0},
        name="gate",
    )(value, *tokens)


class Gather:
    def __init__(self, block):
        self.value = block
        self.bits = []
        self.pending = None

    def start(self, axis, bit):
        self.pending = (axis, bit, swap(self.value, axis, bit))
        return self.value

    def finish(self, after=()):
        axis, bit, other = self.pending
        rows, columns = self.value.shape
        lanes = axis == "mp"
        if lanes:
            shape, out = (rows, columns), (rows, 2 * columns)
        else:
            ahead = 2 ** sum(b > bit for b in self.bits)
            self.bits.append(bit)
            shape = (ahead, rows // ahead, columns)
            out = (ahead, 2, rows // ahead, columns)
        kernel, waits = run_after(lambda *refs: gather_kernel(lanes, *refs), 3, after)
        value = pl.pallas_call(
            kernel,
            in_specs=[SCALAR] + [FULL] * 2 + waits,
            out_specs=FULL,
            out_shape=jax.ShapeDtypeStruct(out, self.value.dtype),
            compiler_params=params(),
            cost_estimate=cost(0.1),
            name="gather_step",
        )(my_bit(axis, bit).reshape(1), self.value.reshape(shape), other.reshape(shape), *after)
        self.value = value.reshape(-1, value.shape[-1])
        return self.value

    def step(self, axis, bit, after=()):
        self.start(axis, bit)
        return self.finish(after)


def scatter_kernel(lanes, mine_ref, *refs):
    terms, (send_ref, keep_ref) = refs[:-2], refs[-2:]
    mine = mine_ref[0]
    for which, out_ref in ((1 - mine, send_ref), (mine, keep_ref)):
        if lanes:
            width = out_ref.shape[1]
            cols = pl.ds(pl.multiple_of(which * width, LANES), width)
            total = sum(term[:, cols].astype(f32) for term in terms)
            out_ref[...] = total.astype(out_ref.dtype)
        else:
            total = sum(term[0, which].astype(f32) for term in terms)
            out_ref[0] = total.astype(out_ref.dtype)


class Scatter:
    def __init__(self, *terms):
        self.bits = list(reversed(range(log_two(lax.axis_size("dp")))))
        self.terms = list(terms)
        self.send = None

    def step(self, axis, bit, kept_type=f32, after=()):
        rows, columns = self.terms[0].shape
        lanes = axis == "mp"
        if lanes:
            shape, half = (rows, columns), (rows, columns // 2)
            steps = max(rows // (LANES + CHUNK), 1)
            steps = next(k for k in range(steps, 0, -1) if rows % (k * CHUNK) == 0 or k == 1)
            block = lambda size: pl.BlockSpec((rows // steps, size[1]), lambda i: (i, 0))
        else:
            steps = 2 ** self.bits.index(bit)
            self.bits.remove(bit)
            shape = (steps, 2, rows // (2 * steps), columns)
            half = (steps, rows // (2 * steps), columns)
            block = lambda size: pl.BlockSpec(
                (1,) + size[1:], lambda i: (i,) + (0,) * (len(size) - 1)
            )
        count = len(self.terms)
        body_kernel = lambda *refs: scatter_kernel(lanes, *refs)
        kernel, waits = run_after(body_kernel, 1 + count, after)
        send, kept = pl.pallas_call(
            kernel,
            grid=(steps,),
            in_specs=[SCALAR] + [block(shape)] * count + waits,
            out_specs=[block(half)] * 2,
            out_shape=[jax.ShapeDtypeStruct(half, bf16), jax.ShapeDtypeStruct(half, kept_type)],
            compiler_params=params(),
            cost_estimate=cost(0.1),
            name="scatter_step",
        )(my_bit(axis, bit).reshape(1), *[term.reshape(shape) for term in self.terms], *after)
        flat = lambda value: value.reshape(-1, value.shape[-1])
        self.send = flat(send)
        self.terms = [flat(kept), swap(self.send, axis, bit)]
        return self.send

    def total(self):
        return sum(term.astype(f32) for term in self.terms)


def butterfly(value):
    for axis, bits in (("mp", 2), ("dp", log_two(lax.axis_size("dp")))):
        for bit in range(bits):
            value = value + swap(value, axis, bit)
    return value


def gelu_pair(value):
    square = value * value
    wave = jnp.tanh(value * (GELU_SCALE + (GELU_SCALE * GELU_CUBE) * square))
    half = 0.5 + 0.5 * wave
    inner = GELU_SCALE + (3.0 * GELU_SCALE * GELU_CUBE) * square
    return value * half, half + 0.5 * value * (1.0 - wave * wave) * inner


def norm_rows(x_ref, gain, shift, out_ref):
    @pl.loop(0, x_ref.shape[0] // CHUNK, unroll=13)
    def _(i):
        rows = pl.ds(pl.multiple_of(i * CHUNK, CHUNK), CHUNK)
        out_ref[rows, :] = layer_norm(x_ref[rows, :], gain, shift).astype(out_ref.dtype)


def norm_back_rows(x_ref, gain, grad_ref, extra_ref, out_ref, low_ref, sum_ref):
    sum_ref[...] = jnp.zeros_like(sum_ref)

    @pl.loop(0, x_ref.shape[0] // CHUNK, unroll=13)
    def _(i):
        rows = pl.ds(pl.multiple_of(i * CHUNK, CHUNK), CHUNK)
        value = x_ref[rows, :]
        grad = grad_ref[rows, :]
        center = value - jnp.mean(value, axis=-1, keepdims=True)
        scale = lax.rsqrt(jnp.mean(center * center, axis=-1, keepdims=True) + norm_eps)
        hat = center * scale
        for k, term in enumerate((grad * hat, grad)):
            sum_ref[8 * k : 8 * k + 8, :] += term[:8] + term[8:]
        pull = grad * gain
        mean_one = jnp.mean(pull, axis=-1, keepdims=True)
        mean_two = jnp.mean(pull * hat, axis=-1, keepdims=True)
        result = scale * (pull - mean_one - hat * mean_two)
        if extra_ref is not None:
            result = result + extra_ref[rows, :]
        out_ref[rows, :] = result
        low_ref[rows, :] = result.astype(bf16)


def gelu_blocks(width):
    return [slice(j, j + BLOCK) for j in range(0, width, BLOCK)]


def soft_rows(scores, column):
    scores = jnp.where(column < PATCHES, scores * HEAD_DIM ** (-0.5), -jnp.inf)
    top = jnp.max(scores, axis=-1, keepdims=True)
    weight = jnp.exp(scores - top)
    return weight * (1.0 / jnp.sum(weight, axis=-1, keepdims=True))


def enter_kernel(
    pixels_ref, stem_ref, embed_w_ref, token_ref, own_ref, other_ref,
    hidden_ref, slope_ref, embed_ref, normed_ref, tri_ref, ctx_ref,
):
    for cols in gelu_blocks(C_STEM):
        value, slope = gelu_pair(matmul(pixels_ref[...], stem_ref[:, cols]))
        hidden_ref[:, cols] = value.astype(bf16)
        slope_ref[:, cols] = slope.astype(bf16)
    slices = pixels_ref.shape[0] // PAD
    for cols in gelu_blocks(D):
        value = matmul(hidden_ref[...], embed_w_ref[:, cols])
        for s in range(slices):
            rows = slice(s * PAD, (s + 1) * PAD)
            embed_ref[rows, cols] = value[rows] + token_ref[:PAD, cols]
    gain, shift = token_ref[PATCHES : PATCHES + 1, :], token_ref[PATCHES + 1 : PATCHES + 2, :]
    norm_rows(embed_ref, gain, shift, normed_ref)
    width = tri_ref.shape[2]
    heads = width // (3 * HEAD_DIM)
    stride = width + width // 3
    column = lax.broadcasted_iota(jnp.int32, (PAD, PAD), 1)
    for p in range(tri_ref.shape[0]):
        start = (p % 2) * stride
        weight_ref = (own_ref, other_ref)[p // 2]
        tri_ref[p] = matmul(normed_ref[...], weight_ref[:, start : start + width]).astype(bf16)

    @pl.loop(0, tri_ref.shape[0])
    def _(p):
        for s in range(slices):
            rows = slice(s * PAD, (s + 1) * PAD)
            for h in range(heads):
                base = h * 3 * HEAD_DIM
                queries = tri_ref[p, rows, base : base + HEAD_DIM]
                keys_low = tri_ref[p, rows, base + HEAD_DIM : base + 2 * HEAD_DIM]
                values = tri_ref[p, rows, base + 2 * HEAD_DIM : base + 3 * HEAD_DIM]
                attend = soft_rows(matmul_t(queries, keys_low), column)
                context = matmul(attend.astype(bf16), values)
                ctx_ref[p, rows, h * HEAD_DIM : (h + 1) * HEAD_DIM] = context.astype(bf16)


def enter(pixels, stem_b, embed_b, tokens, attn_all, width):
    rows = pixels.shape[0]
    parts = 4
    return pl.pallas_call(
        enter_kernel,
        in_specs=[FULL] * 6,
        out_specs=[FULL] * 6,
        out_shape=[
            jax.ShapeDtypeStruct((rows, C_STEM), bf16),
            jax.ShapeDtypeStruct((rows, C_STEM), bf16),
            jax.ShapeDtypeStruct((rows, D), f32),
            jax.ShapeDtypeStruct((rows, D), bf16),
            jax.ShapeDtypeStruct((parts, rows, width), bf16),
            jax.ShapeDtypeStruct((parts, rows, width // 3), bf16),
        ],
        compiler_params=params(),
        cost_estimate=cost(20),
        name="enter",
    )(pixels, stem_b, embed_b, tokens, *attn_all)


def middle_kernel(
    ctx_ref, embed_ref, token_ref, own_ref, other_ref, mlp_ref,
    resid_ref, normed2_ref, slope_ref, inner_ref, resid2_ref, final_ref,
):
    p = pl.program_id(0)

    @pl.when(p == 0)
    def _():
        part = ctx_ref.shape[2]
        stride = 4 * part
        for q in range(ctx_ref.shape[0]):
            start = (q % 2) * stride + 3 * part
            weight_ref = (own_ref, other_ref)[q // 2]
            term = matmul_t(ctx_ref[q], weight_ref[:, start : start + part])
            if q == 0:
                resid_ref[...] = embed_ref[...] + term
            else:
                resid_ref[...] += term
        gain, shift = token_ref[PATCHES + 2 : PATCHES + 3, :], token_ref[PATCHES + 3 : PATCHES + 4, :]
        norm_rows(resid_ref, gain, shift, normed2_ref)
        resid2_ref[...] = resid_ref[...]

    each = mlp_ref.shape[2] // 2
    for cols in gelu_blocks(each):
        value, slope = gelu_pair(matmul(normed2_ref[...], mlp_ref[0, :, cols]))
        inner_ref[0, :, cols] = value.astype(bf16)
        slope_ref[0, :, cols] = slope.astype(bf16)
    resid2_ref[...] += matmul_t(inner_ref[0], mlp_ref[0, :, each:])

    @pl.when(p == pl.num_programs(0) - 1)
    def _():
        gain, shift = token_ref[PATCHES + 4 : PATCHES + 5, :], token_ref[PATCHES + 5 : PATCHES + 6, :]
        norm_rows(resid2_ref, gain, shift, final_ref)


def whole_of(value):
    return pl.BlockSpec(value.shape, lambda *_: (0,) * len(value.shape))


def part_of(value):
    rest = len(value.shape) - 1
    return pl.BlockSpec((1,) + tuple(value.shape[1:]), lambda i, *_: (i,) + (0,) * rest)


def middle(context, embed, tokens, attn_all, mlp_all):
    rows = embed.shape[0]
    parts, _, width = mlp_all.shape
    each = width // 2
    outs = [
        jax.ShapeDtypeStruct((rows, D), f32),
        jax.ShapeDtypeStruct((rows, D), bf16),
        jax.ShapeDtypeStruct((parts, rows, each), bf16),
        jax.ShapeDtypeStruct((parts, rows, each), bf16),
        jax.ShapeDtypeStruct((rows, D), f32),
        jax.ShapeDtypeStruct((rows, D), bf16),
    ]
    values = (context, embed, tokens, *attn_all)
    return pl.pallas_call(
        middle_kernel,
        grid=(parts,),
        in_specs=[whole_of(value) for value in values] + [part_of(mlp_all)],
        out_specs=[(part_of if len(out.shape) == 3 else whole_of)(out) for out in outs],
        out_shape=outs,
        compiler_params=params(),
        cost_estimate=cost(26),
        name="middle",
    )(*values, mlp_all)


def class_probs(logits_ref, rows, group):
    width = CLASSES * LANES
    values = [
        logits_ref[rows, group * width + c * LANES : group * width + (c + 1) * LANES]
        for c in range(CLASSES)
    ]
    top = values[0]
    for value in values[1:]:
        top = jnp.maximum(top, value)
    weights = [jnp.exp(value - top) for value in values]
    total = weights[0]
    for weight in weights[1:]:
        total = total + weight
    scale = 1.0 / total
    return values, [weight * scale for weight in weights], top + jnp.log(total)


SPLIT_A = 4 * CHAN_B
SPLIT_B = SPLIT_A + 16 * CHAN_C
SKIPW = SPLIT_B + 64 * CHAN_D


def leave_kernel(
    core_ref, hidden_ref, final_ref, skip_own_ref, skip_other_ref, dec_ref, one_ref, two_ref, three_ref, head_ref, label_ref,
    slope0_ref, level0_ref, slope_ref, level1_ref, level2_ref, level3_ref, logits_ref, stats_ref,
    skips,
):
    value, slope = gelu_pair(matmul(final_ref[...], dec_ref[...]))
    level0_ref[...] = value.astype(bf16)
    slope0_ref[...] = slope

    half = skip_own_ref.shape[1]
    core = core_ref[0]
    for which, weight_ref in ((core, skip_own_ref), (1 - core, skip_other_ref)):
        for j in range(0, half, BLOCK):
            cols = pl.ds(pl.multiple_of(which * half + j, LANES), BLOCK)
            skips[:, cols] = matmul(hidden_ref[...], weight_ref[:, j : j + BLOCK])

    def stage(source, weight, out_ref, cols, skip_cols):
        pre = matmul(source, weight) + skips[:, skip_cols : skip_cols + BLOCK]
        value, slope = gelu_pair(pre)
        out_ref[:, cols : cols + BLOCK] = value.astype(bf16)
        slope_ref[:, skip_cols : skip_cols + BLOCK] = slope.astype(bf16)

    for i in range(2):
        stage(level0_ref[...], one_ref[:, i * BLOCK : (i + 1) * BLOCK], level1_ref, i * BLOCK, i * BLOCK)
    for i in range(4):
        stage(
            level1_ref[:, i * CHAN_B : (i + 1) * CHAN_B], two_ref[...], level2_ref, i * BLOCK,
            SPLIT_A + i * BLOCK,
        )
    for i in range(4):
        stage(
            level2_ref[:, i * BLOCK : (i + 1) * BLOCK], three_ref[...], level3_ref, i * BLOCK,
            SPLIT_B + i * BLOCK,
        )
    inner = head_ref.shape[0]
    width = head_ref.shape[1]
    groups = level3_ref.shape[1] // inner
    for g in range(groups):
        logits_ref[:, g * width : (g + 1) * width] = matmul(
            level3_ref[:, g * inner : (g + 1) * inner], head_ref[...]
        )
    stats_ref[...] = jnp.zeros_like(stats_ref)
    slices = stats_ref.shape[0]
    per_slice = PAD // CHUNK

    @pl.loop(0, slices)
    def _(s):
        @pl.loop(0, per_slice)
        def _(i):
            start = pl.multiple_of(s * PAD + i * CHUNK, CHUNK)
            rows = pl.ds(start, CHUNK)
            row_id = lax.broadcasted_iota(jnp.int32, (CHUNK, LANES), 0) + i * CHUNK
            inside = (row_id < PATCHES).astype(f32)
            for g in range(groups):
                values, probs, log_total = class_probs(logits_ref, rows, g)
                label = label_ref[rows, g * LANES : (g + 1) * LANES]
                cross = jnp.zeros((CHUNK, LANES), f32)
                for c in range(CLASSES):
                    hot = (label == c).astype(f32)
                    cross = cross + hot * (log_total - values[c])
                    for k, term in enumerate((hot * probs[c], inside * probs[c], hot)):
                        spot = 8 * (3 * c + k)
                        stats_ref[s, spot : spot + 8, :] += term[:8] + term[8:]
                spot = 8 * 3 * CLASSES
                stats_ref[s, spot : spot + 8, :] += cross[:8] + cross[8:]


def leave(core, hidden, final_low, skip_all, dec_b, one_b, two_b, three_four, big_head, labels):
    rows = hidden.shape[0]
    slices = rows // PAD
    stat_rows = 8 * (3 * CLASSES + 1)
    return pl.pallas_call(
        leave_kernel,
        in_specs=[SCALAR] + [FULL] * 10,
        out_specs=[FULL] * 8,
        out_shape=[
            jax.ShapeDtypeStruct((rows, CHAN_A), f32),
            jax.ShapeDtypeStruct((rows, CHAN_A), bf16),
            jax.ShapeDtypeStruct((rows, SKIPW), bf16),
            jax.ShapeDtypeStruct((rows, 4 * CHAN_B), bf16),
            jax.ShapeDtypeStruct((rows, 16 * CHAN_C), bf16),
            jax.ShapeDtypeStruct((rows, 64 * CHAN_D), bf16),
            jax.ShapeDtypeStruct((rows, CLASSES * PIXELS), f32),
            jax.ShapeDtypeStruct((slices, stat_rows, LANES), f32),
        ],
        scratch_shapes=[pltpu.VMEM((rows, SKIPW), f32)],
        compiler_params=params(),
        cost_estimate=cost(16),
        name="leave",
    )(core, hidden, final_low, *skip_all, dec_b, one_b, two_b, three_four, big_head, labels)


def leave_back_kernel(
    coef_ref, logits_ref, label_ref, slope_ref, head_ref, three_ref, two_ref,
    g_logits_ref, g_skips_ref,
):
    inner = head_ref.shape[0]
    width = head_ref.shape[1]
    groups = 64 * CHAN_D // inner
    slices = logits_ref.shape[0] // PAD

    @pl.loop(0, slices)
    def _(s):
        cross_scale = coef_ref[s, 2 * CLASSES]

        @pl.loop(0, PAD // CHUNK)
        def _(i):
            start = pl.multiple_of(s * PAD + i * CHUNK, CHUNK)
            rows = pl.ds(start, CHUNK)
            row_id = lax.broadcasted_iota(jnp.int32, (CHUNK, LANES), 0) + i * CHUNK
            inside = (row_id < PATCHES).astype(f32)
            for g in range(groups):
                _, probs, _ = class_probs(logits_ref, rows, g)
                label = label_ref[rows, g * LANES : (g + 1) * LANES]
                mean = jnp.zeros((CHUNK, LANES), f32)
                pulls = []
                for c in range(CLASSES):
                    pull = jnp.where(label == c, coef_ref[s, c], 0.0) + coef_ref[s, CLASSES + c]
                    pulls.append(pull)
                    mean = mean + probs[c] * pull
                mean = mean - cross_scale
                for c in range(CLASSES):
                    grad = probs[c] * (pulls[c] - mean)
                    grad = grad - jnp.where(label == c, cross_scale, 0.0)
                    spot = g * width + c * LANES
                    g_logits_ref[rows, spot : spot + LANES] = (grad * inside).astype(bf16)

    for i in range(4):
        g, part = (i * BLOCK) // inner, (i * BLOCK) % inner
        grad = matmul_t(g_logits_ref[:, g * width : (g + 1) * width], head_ref[part : part + BLOCK, :])
        cols = slice(SPLIT_B + i * BLOCK, SPLIT_B + (i + 1) * BLOCK)
        g_skips_ref[:, cols] = (grad * slope_ref[:, cols].astype(f32)).astype(bf16)
    for i in range(4):
        source = g_skips_ref[:, SPLIT_B + i * BLOCK : SPLIT_B + (i + 1) * BLOCK]
        cols = slice(SPLIT_A + i * BLOCK, SPLIT_A + (i + 1) * BLOCK)
        g_skips_ref[:, cols] = (matmul_t(source, three_ref[...]) * slope_ref[:, cols].astype(f32)).astype(bf16)
    for i in range(4):
        source = g_skips_ref[:, SPLIT_A + i * BLOCK : SPLIT_A + (i + 1) * BLOCK]
        cols = slice(i * CHAN_B, (i + 1) * CHAN_B)
        g_skips_ref[:, cols] = (matmul_t(source, two_ref[...]) * slope_ref[:, cols].astype(f32)).astype(bf16)


def leave_back(coef, logits, labels, slope, big_head, three_four, two_b):
    rows = logits.shape[0]
    return pl.pallas_call(
        leave_back_kernel,
        in_specs=[SCALAR] + [FULL] * 6,
        out_specs=[FULL] * 2,
        out_shape=[
            jax.ShapeDtypeStruct((rows, CLASSES * PIXELS), bf16),
            jax.ShapeDtypeStruct((rows, SKIPW), bf16),
        ],
        compiler_params=params(),
        cost_estimate=cost(10),
        name="leave_back",
    )(coef, logits, labels, slope, big_head, three_four, two_b)


def skip_grad_kernel(core_ref, hidden_ref, g_skips_ref, send_ref, keep_ref):
    half = send_ref.shape[1]
    core = core_ref[0]
    for which, out_ref in ((1 - core, send_ref), (core, keep_ref)):
        for j in range(0, half, half // 2):
            cols = pl.ds(pl.multiple_of(which * half + j, LANES), half // 2)
            out_ref[:, j : j + half // 2] = t_matmul(hidden_ref[...], g_skips_ref[:, cols]).astype(
                bf16
            )


def skip_grad(core, hidden, g_skips):
    shape = (hidden.shape[1], g_skips.shape[1] // 2)
    return pl.pallas_call(
        skip_grad_kernel,
        in_specs=[SCALAR] + [FULL] * 2,
        out_specs=[FULL] * 2,
        out_shape=[jax.ShapeDtypeStruct(shape, bf16)] * 2,
        compiler_params=params(),
        cost_estimate=cost(6),
        name="skip_grad",
    )(core, hidden, g_skips)


def turn_kernel(
    g_skips_ref, one_ref, slope0_ref, dec_ref, resid2_ref, token_ref,
    g_pre0_ref, g_resid2_ref, low_ref, sums_ref, g_final,
):
    grad = matmul_t(g_skips_ref[:, :SPLIT_A], one_ref[...])
    g_pre0_ref[...] = (grad * slope0_ref[...]).astype(bf16)
    g_final[...] = matmul_t(g_pre0_ref[...], dec_ref[...])
    norm_back_rows(
        resid2_ref, token_ref[PATCHES + 4 : PATCHES + 5, :], g_final, None, g_resid2_ref, low_ref, sums_ref
    )


def turn(g_skips, one_b, slope0, dec_b, resid2, tokens, after=()):
    rows = resid2.shape[0]
    kernel, waits = run_after(turn_kernel, 6, after)
    return pl.pallas_call(
        kernel,
        in_specs=[FULL] * 6 + waits,
        out_specs=[FULL] * 4,
        out_shape=[
            jax.ShapeDtypeStruct((rows, CHAN_A), bf16),
            jax.ShapeDtypeStruct((rows, D), f32),
            jax.ShapeDtypeStruct((rows, D), bf16),
            jax.ShapeDtypeStruct((16, D), f32),
        ],
        scratch_shapes=[pltpu.VMEM((rows, D), f32)],
        compiler_params=params(),
        cost_estimate=cost(11),
        name="turn",
    )(g_skips, one_b, slope0, dec_b, resid2, tokens, *after)


FLAT_DEC = D * CHAN_A // LANES
FLAT_ONE = FLAT_DEC + CHAN_A * 4 * CHAN_B // LANES
FLAT_TWO = FLAT_ONE + CHAN_B * 4 * CHAN_C // LANES
FLAT_THREE = FLAT_TWO + CHAN_C * 4 * CHAN_D // LANES


def decoder_grad_kernel(
    level3_ref, g_logits_ref, level2_ref, level1_ref, g_skips_ref, level0_ref, final_ref, g_pre0_ref,
    out_ref, flat_ref, square_ref,
):
    size = out_ref.shape[1]
    flat = (FLAT_THREE * LANES + 4 * CLASSES * CHAN_D) // size
    inner, width = GROUP * CHAN_D, CLASSES * LANES
    tail = flat_ref.shape[0] - FLAT_THREE
    flat_ref[FLAT_THREE:, :] = jnp.zeros((tail, LANES), f32)

    def spread(value, base, count):
        for j in range(count):
            flat_ref[pl.ds(base + j, value.shape[0], stride=count), :] = value[
                :, j * LANES : (j + 1) * LANES
            ]

    spread(t_matmul(final_ref[...], g_pre0_ref[...]), 0, CHAN_A // LANES)
    spread(t_matmul(level0_ref[...], g_skips_ref[:, :SPLIT_A]), FLAT_DEC, SPLIT_A // LANES)
    three = jnp.zeros((CHAN_C, 4 * CHAN_D), f32)
    two = jnp.zeros((CHAN_B, 4 * CHAN_C), f32)
    for i in range(4):
        big = t_matmul(
            level2_ref[:, i * BLOCK : (i + 1) * BLOCK],
            g_skips_ref[:, SPLIT_B + i * BLOCK : SPLIT_B + (i + 1) * BLOCK],
        )
        for k in range(4):
            at = slice(k * CHAN_C, (k + 1) * CHAN_C)
            three += big[at, at]
        two += t_matmul(
            level1_ref[:, i * CHAN_B : (i + 1) * CHAN_B],
            g_skips_ref[:, SPLIT_A + i * BLOCK : SPLIT_A + (i + 1) * BLOCK],
        )
    spread(two, FLAT_ONE, 4 * CHAN_C // LANES)
    square_ref[...] = three
    flat_ref[FLAT_TWO:FLAT_THREE, :] = jnp.concatenate(
        [square_ref[pl.ds(j, CHAN_C // 2, stride=2), :] for j in range(2)], axis=1
    )
    head = jnp.zeros((CHAN_D, width), f32)
    row = lax.broadcasted_iota(jnp.int32, (CHAN_D, width), 0)
    across = lax.broadcasted_iota(jnp.int32, (CHAN_D, width), 1)
    parent = (across // 4) % GROUP
    for g in range(level3_ref.shape[1] // inner):
        big = t_matmul(
            level3_ref[:, g * inner : (g + 1) * inner], g_logits_ref[:, g * width : (g + 1) * width]
        )
        for k in range(GROUP):
            head += jnp.where(parent == k, big[k * CHAN_D : (k + 1) * CHAN_D, :], 0.0)
    column = lax.broadcasted_iota(jnp.int32, (width, LANES), 0)
    target = lax.broadcasted_iota(jnp.int32, (width, LANES), 1)
    pick = target == (column % 4) * CLASSES + column // (GROUP * 4)
    small = jnp.dot(head, pick.astype(f32), precision=highest, preferred_element_type=f32)
    lane = lax.broadcasted_iota(jnp.int32, (1, LANES), 1)
    lines = [jnp.zeros((1, LANES), f32) for _ in range(8)]
    for k in range(CHAN_D):
        line, start = divmod(k * 4 * CLASSES, LANES)
        value = small[k : k + 1, :]
        if start:
            value = pltpu.roll(value, start, 1)
        lines[line] = lines[line] + jnp.where(lane >= start, value, 0.0)
        if start + 4 * CLASSES > LANES:
            lines[line + 1] = lines[line + 1] + jnp.where(
                lane < start + 4 * CLASSES - LANES, value, 0.0
            )
    flat_ref[FLAT_THREE : FLAT_THREE + 8, :] = jnp.concatenate(lines, axis=0)

    rows = out_ref.shape[2]
    line_id = lax.broadcasted_iota(jnp.int32, (rows, LANES), 0)
    lane_id = lax.broadcasted_iota(jnp.int32, (rows, LANES), 1)
    for d in range(size):
        for c in range(2):
            first, start = divmod(d * flat + c * rows * LANES, LANES)
            value = flat_ref[first : first + rows, :]
            if start:
                after = flat_ref[first + 1 : first + 1 + rows, :]
                value = jnp.where(
                    lane_id < LANES - start,
                    pltpu.roll(value, LANES - start, 1),
                    pltpu.roll(after, LANES - start, 1),
                )
            inside = (line_id + c * rows) * LANES + lane_id < flat
            out_ref[c, d] = jnp.where(inside, value, 0.0).astype(bf16)


def decoder_grad(
    level3, g_logits, level2, level1, g_skips, level0, final_low, g_pre0, size, rows, after=()
):
    kernel, waits = run_after(decoder_grad_kernel, 8, after)
    flat = (FLAT_THREE * LANES + 4 * CLASSES * CHAN_D) // size
    lines = (size - 1) * flat // LANES + 2 * rows + 8
    lines = -(-max(lines, FLAT_THREE + 8) // 8) * 8
    return pl.pallas_call(
        kernel,
        in_specs=[FULL] * 8 + waits,
        out_specs=FULL,
        out_shape=jax.ShapeDtypeStruct((2, size, rows, LANES), bf16),
        scratch_shapes=[pltpu.VMEM((lines, LANES), f32), pltpu.VMEM((CHAN_C, 4 * CHAN_D), f32)],
        compiler_params=params(),
        cost_estimate=cost(7),
        name="decoder_grad",
    )(level3, g_logits, level2, level1, g_skips, level0, final_low, g_pre0, *after)


def first_grad_kernel(
    core_ref, pixels_ref, g_stem_ref, hidden_ref, low_ref, pos_ref, sums1_ref, sums2_ref, sumsf_ref,
    dec_ref, send_ref, keep_ref, token_ref,
):
    core = core_ref[0]
    size = send_ref.shape[0]
    stem_rows, embed_rows, token_rows = PIXELS // size, C_STEM // size, D // size
    token_ref[...] = jnp.zeros_like(token_ref)
    token_ref[:PATCHES, :] = pos_ref[:PATCHES, :]
    for i, sums_ref in enumerate((sums1_ref, sums2_ref, sumsf_ref)):
        for k in range(2):
            at = PATCHES + 2 * i + k
            token_ref[at : at + 1, :] = jnp.sum(
                sums_ref[8 * k : 8 * k + 8, :], axis=0, keepdims=True
            )
    for which, out_ref in ((1 - core, send_ref), (core, keep_ref)):
        spot = 0
        half = C_STEM // 2
        for j in range(0, half, BLOCK):
            cols = pl.ds(pl.multiple_of(which * half + j, LANES), BLOCK)
            part = t_matmul(pixels_ref[...], g_stem_ref[:, cols]).astype(bf16)
            for k in range(0, BLOCK, LANES):
                for d in range(size):
                    out_ref[d, spot : spot + stem_rows, :] = part[
                        d * stem_rows : (d + 1) * stem_rows, k : k + LANES
                    ]
                spot += stem_rows
        half = D // 2
        cols = pl.ds(pl.multiple_of(which * half, LANES), half)
        part = t_matmul(hidden_ref[...], low_ref[:, cols]).astype(bf16)
        for k in range(0, half, LANES):
            for d in range(size):
                out_ref[d, spot : spot + embed_rows, :] = part[
                    d * embed_rows : (d + 1) * embed_rows, k : k + LANES
                ]
            spot += embed_rows
        turned = token_ref[pl.ds(pl.multiple_of(which * LANES, LANES), LANES), :].T.astype(bf16)
        for d in range(size):
            out_ref[d, spot : spot + token_rows, :] = turned[d * token_rows : (d + 1) * token_rows]
            out_ref[d, spot + token_rows :, :] = dec_ref[which, d]


def first_grad(core, pixels, g_stem, hidden, low, pos, sums1, sums2, sumsf, dec, rows, after=()):
    kernel, waits = run_after(first_grad_kernel, 10, after)
    shape = (dec.shape[1], rows, LANES)
    return pl.pallas_call(
        kernel,
        in_specs=[SCALAR] + [FULL] * 9 + waits,
        out_specs=[FULL] * 2,
        out_shape=[jax.ShapeDtypeStruct(shape, bf16)] * 2,
        scratch_shapes=[pltpu.VMEM((2 * LANES, D), f32)],
        compiler_params=params(),
        cost_estimate=cost(6),
        name="first_grad",
    )(core, pixels, g_stem, hidden, low, pos, sums1, sums2, sumsf, dec, *after)


def unpack_kernel(core_ref, own_ref, other_ref, stem_ref, embed_ref, token_ref, turned_ref):
    core = core_ref[0]
    size = own_ref.shape[0]
    stem_rows, embed_rows, token_rows = PIXELS // size, C_STEM // size, D // size
    for which, block_ref in ((core, own_ref), (1 - core, other_ref)):
        spot = 0
        for target_ref, rows, half in (
            (stem_ref, stem_rows, C_STEM // 2),
            (embed_ref, embed_rows, D // 2),
            (turned_ref, token_rows, LANES),
        ):
            for k in range(0, half, LANES):
                cols = pl.ds(pl.multiple_of(which * half + k, LANES), LANES)
                for d in range(size):
                    target_ref[d * rows : (d + 1) * rows, cols] = block_ref[
                        d, spot : spot + rows, :
                    ].astype(target_ref.dtype)
                spot += rows
    token_ref[...] = turned_ref[...].T


def unpack(core, own, other):
    return pl.pallas_call(
        unpack_kernel,
        in_specs=[SCALAR] + [FULL] * 2,
        out_specs=[FULL] * 3,
        out_shape=[
            jax.ShapeDtypeStruct((PIXELS, C_STEM), bf16),
            jax.ShapeDtypeStruct((C_STEM, D), bf16),
            jax.ShapeDtypeStruct((2 * LANES, D), f32),
        ],
        scratch_shapes=[pltpu.VMEM((D, 2 * LANES), f32)],
        compiler_params=params(),
        cost_estimate=cost(4),
        name="unpack",
    )(core, own, other)


def pack_kernel(core_ref, stem_ref, embed_ref, token_ref, dec_ref, out_ref):
    core = core_ref[0]
    spot = 0
    for source_ref in (stem_ref, embed_ref, token_ref):
        rows, half = source_ref.shape[0], source_ref.shape[1] // 2
        for k in range(0, half, LANES):
            cols = pl.ds(pl.multiple_of(core * half + k, LANES), LANES)
            out_ref[spot : spot + rows, :] = source_ref[:, cols].astype(bf16)
            spot += rows
    out_ref[spot:, :] = dec_ref[core].astype(bf16)


def pack(core, stem_w, embed_w, token_t, dec, rows):
    return pl.pallas_call(
        pack_kernel,
        in_specs=[SCALAR] + [FULL] * 4,
        out_specs=FULL,
        out_shape=jax.ShapeDtypeStruct((rows, LANES), bf16),
        compiler_params=params(),
        cost_estimate=cost(2),
        name="pack",
    )(core, stem_w, embed_w, token_t, dec)


def middle_back_kernel(
    low2_ref, mlp_ref, slope_ref, resid_ref, token_ref, g_resid2_ref, own_ref, other_ref,
    g_pre_ref, g_resid_ref, low_ref, g_ctx_ref, sums_ref, g_normed,
):
    p = pl.program_id(0)
    each = mlp_ref.shape[2] // 2
    for cols in gelu_blocks(each):
        down = mlp_ref[0, :, each + cols.start : each + cols.stop]
        grad = matmul(low2_ref[...], down) * slope_ref[0, :, cols].astype(f32)
        g_pre_ref[0, :, cols] = grad.astype(bf16)
    term = matmul_t(g_pre_ref[0], mlp_ref[0, :, :each])

    @pl.when(p == 0)
    def _():
        g_normed[...] = term

    @pl.when(p > 0)
    def _():
        g_normed[...] += term

    @pl.when(p == pl.num_programs(0) - 1)
    def _():
        norm_back_rows(
            resid_ref, token_ref[PATCHES + 2 : PATCHES + 3, :], g_normed, g_resid2_ref,
            g_resid_ref, low_ref, sums_ref,
        )
        part = g_ctx_ref.shape[2]
        for q in range(g_ctx_ref.shape[0]):
            start = (q % 2) * 4 * part + 3 * part
            weight_ref = (own_ref, other_ref)[q // 2]
            g_ctx_ref[q] = matmul(low_ref[...], weight_ref[:, start : start + part]).astype(bf16)


def middle_back(low2, mlp_all, slope, resid, tokens, g_resid2, attn_all, after=()):
    kernel, waits = run_after(middle_back_kernel, 8, after)
    rows = resid.shape[0]
    parts, _, each = slope.shape
    part = attn_all[0].shape[1] // 8
    outs = [
        jax.ShapeDtypeStruct((parts, rows, each), bf16),
        jax.ShapeDtypeStruct((rows, D), f32),
        jax.ShapeDtypeStruct((rows, D), bf16),
        jax.ShapeDtypeStruct((parts, rows, part), bf16),
        jax.ShapeDtypeStruct((16, D), f32),
    ]
    values = (resid, tokens, g_resid2, *attn_all)
    return pl.pallas_call(
        kernel,
        grid=(parts,),
        in_specs=[whole_of(low2), part_of(mlp_all), part_of(slope)]
        + [whole_of(value) for value in values]
        + waits,
        out_specs=[part_of(outs[0])] + [whole_of(out) for out in outs[1:]],
        out_shape=outs,
        scratch_shapes=[pltpu.VMEM((rows, D), f32)],
        compiler_params=params(),
        cost_estimate=cost(21),
        name="middle_back",
    )(low2, mlp_all, slope, *values, *after)


def half_grad_kernel(core_ref, left_ref, right_ref, send_ref, keep_ref):
    core = core_ref[0]
    each = right_ref.shape[2]
    for which, out_ref in ((1 - core, send_ref), (core, keep_ref)):
        for x in range(2):
            out_ref[:, x * each : (x + 1) * each] = t_matmul(
                left_ref[...], right_ref[2 * x + which]
            ).astype(bf16)


def half_grad(core, left, right, after=()):
    kernel, waits = run_after(half_grad_kernel, 3, after)
    shape = (left.shape[1], 2 * right.shape[2])
    return pl.pallas_call(
        kernel,
        in_specs=[SCALAR] + [FULL] * 2 + waits,
        out_specs=[FULL] * 2,
        out_shape=[jax.ShapeDtypeStruct(shape, bf16)] * 2,
        compiler_params=params(),
        cost_estimate=cost(6),
        name="half_grad",
    )(core, left, right, *after)


def attn_back_kernel(tri_ref, g_ctx_ref, g_tri_ref):
    slices = tri_ref.shape[1] // PAD
    heads = tri_ref.shape[2] // (3 * HEAD_DIM)
    column = lax.broadcasted_iota(jnp.int32, (PAD, PAD), 1)
    for s in range(slices):
        rows = slice(s * PAD, (s + 1) * PAD)
        for h in range(heads):
            base = h * 3 * HEAD_DIM
            queries = tri_ref[0, rows, base : base + HEAD_DIM]
            keys_low = tri_ref[0, rows, base + HEAD_DIM : base + 2 * HEAD_DIM]
            values = tri_ref[0, rows, base + 2 * HEAD_DIM : base + 3 * HEAD_DIM]
            gctx = g_ctx_ref[0, rows, h * HEAD_DIM : (h + 1) * HEAD_DIM]
            attend = soft_rows(matmul_t(queries, keys_low), column)
            g_attend = matmul_t(gctx, values)
            g_values = t_matmul(attend.astype(bf16), gctx)
            inner = jnp.sum(attend * g_attend, axis=-1, keepdims=True)
            g_scores = attend * (g_attend - inner) * HEAD_DIM ** (-0.5)
            g_low = g_scores.astype(bf16)
            g_tri_ref[0, rows, base : base + HEAD_DIM] = matmul(g_low, keys_low).astype(bf16)
            g_tri_ref[0, rows, base + HEAD_DIM : base + 2 * HEAD_DIM] = t_matmul(
                g_low, queries
            ).astype(bf16)
            g_tri_ref[0, rows, base + 2 * HEAD_DIM : base + 3 * HEAD_DIM] = g_values.astype(bf16)


def attn_back(triple, g_ctx, after=()):
    parts, rows, width = triple.shape
    whole = lambda size: pl.BlockSpec((1, rows, size), lambda i: (i, 0, 0))
    kernel, waits = run_after(attn_back_kernel, 2, after)
    return pl.pallas_call(
        kernel,
        grid=(parts,),
        in_specs=[whole(width), whole(width // 3)] + waits,
        out_specs=whole(width),
        out_shape=jax.ShapeDtypeStruct(triple.shape, bf16),
        compiler_params=params(),
        cost_estimate=cost(15),
        name="attn_back",
    )(triple, g_ctx, *after)


def attn_grad_kernel(normed_ref, g_tri_ref, low_ref, ctx_ref, send_ref, keep_ref):
    width = g_tri_ref.shape[2]
    stride = width + width // 3
    for which, out_ref in ((1, send_ref), (0, keep_ref)):
        for x in range(2):
            part = 2 * which + x
            at = x * stride
            out_ref[:, at : at + width] = t_matmul(normed_ref[...], g_tri_ref[part]).astype(
                out_ref.dtype
            )
            out_ref[:, at + width : at + stride] = t_matmul(low_ref[...], ctx_ref[part]).astype(
                out_ref.dtype
            )


def attn_grad(normed, g_tri, low, context, after=()):
    shape = (D, 2 * (g_tri.shape[2] + context.shape[2]))
    kernel, waits = run_after(attn_grad_kernel, 4, after)
    return pl.pallas_call(
        kernel,
        in_specs=[FULL] * 4 + waits,
        out_specs=[FULL] * 2,
        out_shape=[jax.ShapeDtypeStruct(shape, bf16)] * 2,
        compiler_params=params(),
        cost_estimate=cost(7),
        name="attn_grad",
    )(normed, g_tri, low, context, *after)


def enter_back_kernel(
    core_ref, g_tri_ref, own_ref, other_ref, embed_ref, token_ref, g_resid_ref, embed_w_ref,
    g_skips_ref, skip_own_ref, skip_other_ref, slope_ref, low_ref, g_stem_ref, g_pos_ref, sums_ref, g_normed, g_embed,
):
    width = g_tri_ref.shape[2]
    stride = width + width // 3
    for p in range(g_tri_ref.shape[0]):
        start = (p % 2) * stride
        weight_ref = (own_ref, other_ref)[p // 2]
        term = matmul_t(g_tri_ref[p], weight_ref[:, start : start + width])
        if p == 0:
            g_normed[...] = term
        else:
            g_normed[...] += term
    norm_back_rows(
        embed_ref, token_ref[PATCHES : PATCHES + 1, :], g_normed, g_resid_ref, g_embed, low_ref, sums_ref
    )
    pos = g_embed[:PAD, :]
    for s in range(1, embed_ref.shape[0] // PAD):
        pos = pos + g_embed[s * PAD : (s + 1) * PAD, :]
    g_pos_ref[...] = pos
    half = skip_own_ref.shape[1]
    core = core_ref[0]
    for cols in gelu_blocks(C_STEM):
        grad = matmul_t(low_ref[...], embed_w_ref[cols, :])
        for which, weight_ref in ((core, skip_own_ref), (1 - core, skip_other_ref)):
            part = pl.ds(pl.multiple_of(which * half, LANES), half)
            grad += matmul_t(g_skips_ref[:, part], weight_ref[cols, :])
        g_stem_ref[:, cols] = (grad * slope_ref[:, cols].astype(f32)).astype(bf16)


def enter_back(core, g_tri, attn_all, embed, tokens, g_resid, embed_b, g_skips, skip_all, slope, after=()):
    rows = embed.shape[0]
    kernel, waits = run_after(enter_back_kernel, 12, after)
    return pl.pallas_call(
        kernel,
        in_specs=[SCALAR] + [FULL] * 11 + waits,
        out_specs=[FULL] * 4,
        out_shape=[
            jax.ShapeDtypeStruct((rows, D), bf16),
            jax.ShapeDtypeStruct((rows, C_STEM), bf16),
            jax.ShapeDtypeStruct((PAD, D), f32),
            jax.ShapeDtypeStruct((16, D), f32),
        ],
        scratch_shapes=[pltpu.VMEM((rows, D), f32), pltpu.VMEM((rows, D), f32)],
        compiler_params=params(),
        cost_estimate=cost(21),
        name="enter_back",
    )(core, g_tri, *attn_all, embed, tokens, g_resid, embed_b, g_skips, *skip_all, slope, *after)


def split_decoder(flat):
    edge_one = D * CHAN_A
    edge_two = edge_one + CHAN_A * 4 * CHAN_B
    edge_three = edge_two + CHAN_B * 4 * CHAN_C
    edge_four = edge_three + CHAN_C * 4 * CHAN_D
    return (
        flat[:edge_one].reshape(D, CHAN_A),
        flat[edge_one:edge_two].reshape(CHAN_A, 4 * CHAN_B),
        flat[edge_two:edge_three].reshape(CHAN_B, 4 * CHAN_C),
        flat[edge_three:edge_four].reshape(CHAN_C, 4 * CHAN_D),
        flat[edge_four:].reshape(CHAN_D, 4 * CLASSES),
    )


def same_block(rows, columns, inner, outer):
    row = lax.broadcasted_iota(jnp.int32, (rows, columns), 0) // inner
    column = lax.broadcasted_iota(jnp.int32, (rows, columns), 1) // outer
    return row == column


def block_diag(weight, parents):
    inner, outer = weight.shape
    mask = same_block(parents * inner, parents * outer, inner, outer)
    tiled = jnp.tile(weight, (parents, parents))
    return jnp.where(mask, tiled, jnp.zeros_like(tiled))


def head_masks():
    wide = CLASSES * GROUP * 4
    column = lax.broadcasted_iota(jnp.int32, (4 * CLASSES, wide), 1)
    source = lax.broadcasted_iota(jnp.int32, (4 * CLASSES, wide), 0)
    pick = source == (column % 4) * CLASSES + column // (GROUP * 4)
    row = lax.broadcasted_iota(jnp.int32, (GROUP * CHAN_D, wide), 0)
    across = lax.broadcasted_iota(jnp.int32, (GROUP * CHAN_D, wide), 1)
    mask = row // CHAN_D == (across // 4) % GROUP
    return pick, mask


def big_head_of(head_b):
    pick, mask = head_masks()
    spread = matmul(head_b, pick.astype(bf16)).astype(bf16)
    tiled = jnp.tile(spread, (GROUP, 1))
    return jnp.where(mask, tiled, jnp.zeros_like(tiled))


def stack_columns(value, width):
    count = value.shape[-1] // width
    return jnp.concatenate(
        [value[..., i * width : (i + 1) * width] for i in range(count)], axis=-2
    )


def unstack_columns(value, count):
    rows = value.shape[-2] // count
    return jnp.concatenate(
        [value[..., i * rows : (i + 1) * rows, :] for i in range(count)], axis=-1
    )


def pad_to(value, axis, size):
    widths = [(0, 0)] * value.ndim
    widths[axis] = (0, size - value.shape[axis])
    return jnp.pad(value, widths)


class Shared:
    def __init__(self, stem_w, embed_w, token_params, decoder_w):
        self.stem_rows = stem_w.shape[0]
        self.embed_rows = embed_w.shape[0]
        self.token_rows = token_params.shape[1]
        self.flat = decoder_w.shape[0]
        self.flat_rows = -(-self.flat // (2 * LANES * 16)) * 16
        self.stem_count = C_STEM // 2 // LANES
        self.embed_count = D // 2 // LANES
        self.cuts = [0]
        for rows in (
            self.stem_rows * self.stem_count,
            self.embed_rows * self.embed_count,
            self.token_rows,
            self.flat_rows,
        ):
            self.cuts.append(self.cuts[-1] + rows)

    def half_flat(self, flat):
        padded = pad_to(flat, flat.ndim - 1, 2 * self.flat_rows * LANES)
        return padded.reshape(flat.shape[:-1] + (2, self.flat_rows, LANES))

    def pieces(self, value):
        one, two, three, four = (
            value[..., a:b, :] for a, b in zip(self.cuts[:-1], self.cuts[1:], strict=True)
        )
        return (
            unstack_columns(one, self.stem_count),
            unstack_columns(two, self.embed_count),
            three,
            four,
        )


def half_columns(value, core, axis=-1):
    axis = axis % value.ndim
    size = value.shape[axis] // 2
    return lax.dynamic_slice_in_dim(value, core * size, size, axis)


def adamw(weight, grad, first, second, rate):
    first_new = beta_one * first + (1.0 - beta_one) * grad
    second_new = beta_two * second + (1.0 - beta_two) * grad * grad
    first_hat = first_new / (1.0 - beta_one**STEP)
    second_hat = second_new / (1.0 - beta_two**STEP)
    new_weight = weight - rate * (
        first_hat / (jnp.sqrt(second_hat) + adam_eps) + decay_rate * weight
    )
    return (new_weight, first_new, second_new)


def body(
    images,
    labels,
    background,
    patients,
    *state,
):
    masters, firsts, seconds = state[:9], state[9:18], state[18:]
    stem_w, embed_w, token_params, qkv_w, out_w, mlp_in_w, mlp_out_w, skip_w, decoder_w = masters
    n_dp = lax.axis_size("dp")
    n_mp = lax.axis_size("mp")
    mp_id = lax.axis_index("mp")
    core = mp_id & 1
    slices = images.shape[0] // n_mp
    rows = slices * PAD
    shared = Shared(stem_w, embed_w, token_params, decoder_w)
    attn_cut = qkv_w.shape[1]

    core_id = core.reshape(1)
    token_t = pad_to(token_params.T, 1, 2 * LANES)
    aligned = shared.stem_rows % 16 == 0 and shared.token_rows % 16 == 0
    mlp_block = jnp.concatenate([mlp_in_w, mlp_out_w.T], axis=1).astype(bf16)
    mlp_all = lax.all_gather(mlp_block, ("mp", "dp"), axis=0, tiled=True).reshape(n_mp, D, -1)
    if aligned:
        first_block = pack(
            core_id, stem_w, embed_w, token_t, shared.half_flat(decoder_w), shared.cuts[-1]
        )
    else:
        dec_half = lax.dynamic_index_in_dim(shared.half_flat(decoder_w), core, 0, keepdims=False)
        first_block = jnp.concatenate(
            [
                stack_columns(half_columns(stem_w, core), LANES),
                stack_columns(half_columns(embed_w, core), LANES),
                half_columns(token_t, core),
                dec_half,
            ],
            axis=0,
        ).astype(bf16)
    attn_block = jnp.concatenate([qkv_w, out_w.T], axis=1).astype(bf16)
    skip_block = half_columns(skip_w, core).astype(bf16)

    first, split, skip = Gather(first_block), Gather(attn_block), Gather(skip_block)
    order = list(reversed(range(log_two(n_dp))))
    for bit in order[3:]:
        for part in (first, split, skip):
            part.step("dp", bit)
    top, middle_bit, last = order[:3]
    first.start("dp", top)
    split.start("dp", top)
    token = first.finish()
    first.start("dp", last)
    token = split.finish(after=(token,))
    split.start("dp", middle_bit)
    skip.value = run_gate(skip.value, token)
    skip.start("dp", top)
    token = first.finish(after=(token,))
    first.start("dp", middle_bit)
    token = split.finish(after=(token,))
    split.start("dp", last)
    token = skip.finish(after=(token,))
    skip.start("dp", middle_bit)
    token = split.finish(after=(token,))
    split.start("mp", 1)
    token = first.finish(after=(token,))
    first_own = first.value
    token = skip.finish(after=(token,))
    skip.start("dp", last)
    token = split.finish(after=(token,))
    attn_weights = split.value
    first_pair = [
        value.reshape(n_dp, -1, LANES) for value in (first_own, swap(first_own, "mp", 0))
    ]
    by_core = lambda pair: [
        jnp.where(core == 0, pair[0], pair[1]), jnp.where(core == 0, pair[1], pair[0])
    ]
    dec_parts = by_core([value[:, shared.cuts[3] :] for value in first_pair])
    if aligned:
        stem_b, embed_b, table = unpack(core_id, *first_pair)
    else:
        both = [shared.pieces(value) for value in by_core(first_pair)]
        side = lambda k: jnp.concatenate([both[0][k], both[1][k]], axis=-1)
        stem_b = side(0).reshape(PIXELS, C_STEM)
        embed_b = side(1).reshape(C_STEM, D)
        table = side(2).reshape(D, 2 * LANES).T.astype(f32)
    dec_flat = jnp.stack(dec_parts, axis=1).reshape(n_dp, -1)[:, : shared.flat].reshape(-1)
    dec_b, one_b, two_b, three_b, head_b = split_decoder(dec_flat)

    attn_all = (attn_weights, swap(attn_weights, "mp", 0))

    take = lambda value: lax.dynamic_slice_in_dim(value, mp_id * slices, slices, 0)
    pixels = pad_to(take(images), 1, PAD).reshape(rows, PIXELS)
    label_own = jnp.pad(take(labels), ((0, 0), (0, PAD - PATCHES), (0, 0)), constant_values=-1)
    label_own = label_own.reshape(rows, PIXELS)
    keep = (1 - take(background)).astype(f32)
    owner = (take(patients)[:, None] == jnp.arange(PATIENTS, dtype=jnp.int32)).astype(f32)

    hidden, slope_stem, embed, normed, triple, context = enter(
        pixels, stem_b, embed_b, table, attn_all, attn_cut
    )
    skip_weights = skip.finish(after=(hidden,))
    skip_all = (skip_weights, swap(skip_weights, "mp", 0))
    resid, normed2, slope_mlp, inner, resid2, final_low = middle(
        context, embed, table, attn_all, mlp_all
    )
    three_four = block_diag(three_b, 4)
    big_head = big_head_of(head_b)
    slope0, level0, slope_skips, level1, level2, level3, logits, stats = leave(
        core_id, hidden, final_low, skip_all, dec_b, one_b, two_b, three_four, big_head, label_own
    )

    sums = jnp.sum(stats.reshape(slices, 3 * CLASSES + 1, 8 * LANES), axis=-1)
    class_sums = sums[:, : 3 * CLASSES]
    pat_sums = jnp.sum(owner[:, :, None] * class_sums[:, None, :], axis=0)
    cross_sum = jnp.sum(keep * sums[:, 3 * CLASSES])
    packed = jnp.concatenate(
        [pat_sums.reshape(-1), cross_sum[None], jnp.sum(keep)[None]]
    )
    packed = pad_to(packed, 0, 4 * LANES).reshape(4, LANES)
    packed = butterfly(packed).reshape(-1)
    pat_all = packed[: PATIENTS * 3 * CLASSES].reshape(PATIENTS, CLASSES, 3)
    ce_total = packed[PATIENTS * 3 * CLASSES]
    pixel_count = packed[PATIENTS * 3 * CLASSES + 1] * (PATCHES * PIXELS)
    pat_over, pat_pred, pat_true = pat_all[..., 0], pat_all[..., 1], pat_all[..., 2]
    denominator = pat_pred + pat_true + dice_eps
    dice = (2.0 * pat_over + dice_eps) / denominator
    count_floor = jnp.maximum(pixel_count, 1.0)
    loss = ce_total / count_floor + 1.0 - jnp.mean(dice)
    cells = PATIENTS * CLASSES
    over_coef = -2.0 / (cells * denominator)
    pred_coef = (2.0 * pat_over + dice_eps) / (cells * denominator * denominator)
    pick_own = lambda table: jnp.sum(owner[:, :, None] * table[None], axis=1)
    coef = jnp.concatenate(
        [pick_own(over_coef), pick_own(pred_coef), (keep / count_floor)[:, None]], axis=1
    )

    def x_sum(value):
        value = lax.reduce_precision(value, 8, 7).astype(bf16)
        return value.astype(f32) + swap(value, "mp", 1).astype(f32)

    def core_pair(send, own):
        return Scatter(own, swap(send, "mp", 0))

    grad_logits, grad_skips = leave_back(
        coef, logits, label_own, slope_skips, big_head, three_four, two_b
    )
    skip_send, skip_keep = skip_grad(core_id, hidden, grad_skips)
    grad_pre0, grad_resid2, grad_resid2_low, sums_f = turn(
        grad_skips, one_b, slope0, dec_b, resid2, table, after=(skip_send,)
    )
    low_bits = list(range(log_two(n_dp)))
    skip_part = core_pair(skip_send, skip_keep)
    token = skip_part.step("dp", low_bits[0], bf16, after=(grad_pre0,))
    down_send, down_keep = half_grad(core_id, grad_resid2_low, inner, after=(token,))
    grad_pre, grad_resid, grad_resid_low, grad_context, sums_2 = middle_back(
        grad_resid2_low, mlp_all, slope_mlp, resid, table, grad_resid2, attn_all,
        after=(down_send,),
    )
    down = core_pair(down_send, down_keep)
    token = down.step("dp", low_bits[0], bf16, after=(grad_pre,))
    token = skip_part.step("dp", low_bits[1], after=(token,))
    in_send, in_keep = half_grad(core_id, normed2, grad_pre, after=(token,))
    grad_triple = attn_back(triple, grad_context, after=(in_send,))
    into = core_pair(in_send, in_keep)
    token = into.step("mp", 1, bf16, after=(grad_triple,))
    token = skip_part.step("dp", low_bits[2], after=(token,))
    attn_send, attn_keep = attn_grad(
        normed, grad_triple, grad_resid_low, context, after=(token,)
    )
    token = down.step("dp", low_bits[1], after=(attn_send,))
    decoder_halves = decoder_grad(
        level3, grad_logits, level2, level1, grad_skips, level0, final_low, grad_pre0,
        n_dp, shared.flat_rows, after=(token,),
    )
    token = decoder_halves
    grad_embed_low, grad_pre_stem, grad_pos, sums_1 = enter_back(
        core_id, grad_triple, attn_all, embed, table, grad_resid, embed_b, grad_skips, skip_all,
        slope_stem, after=(token,),
    )
    attn = core_pair(attn_send, attn_keep)
    token = attn.step("mp", 1, bf16, after=(grad_embed_low,))
    token = into.step("dp", low_bits[0], after=(token,))
    token = down.step("dp", low_bits[2], after=(token,))
    if aligned:
        first_send, first_keep = first_grad(
            core_id, pixels, grad_pre_stem, hidden, grad_embed_low, grad_pos, sums_1, sums_2,
            sums_f, decoder_halves, shared.cuts[-1], after=(token,),
        )
    else:
        gains = jnp.concatenate([sums_1, sums_2, sums_f], axis=0).reshape(6, 8, D).sum(axis=1)
        grad_token = pad_to(jnp.concatenate([grad_pos[:PATCHES], gains], axis=0).T, 1, 2 * LANES)

        def first_half(which):
            blocks = lambda value: value.reshape(n_dp, -1, value.shape[-1])
            stem_part = t_matmul(pixels, half_columns(grad_pre_stem, which))
            embed_part = t_matmul(hidden, half_columns(grad_embed_low, which))
            return jnp.concatenate(
                [
                    stack_columns(blocks(stem_part), LANES),
                    stack_columns(blocks(embed_part), LANES),
                    blocks(half_columns(grad_token, which)),
                    lax.dynamic_index_in_dim(decoder_halves, which, 0, keepdims=False).astype(f32),
                ],
                axis=1,
            ).astype(bf16)

        first_send, first_keep = first_half(1 - core), first_half(core)
    wide = lambda value: value.reshape(-1, LANES)
    first = core_pair(wide(first_send), wide(first_keep))
    token = into.step("dp", low_bits[1], after=(first_send,))
    token = first.step("dp", low_bits[0], after=(token,))
    token = down.step("mp", 1, after=(token,))
    token = attn.step("dp", low_bits[0], after=(token,))
    token = into.step("dp", low_bits[2], after=(token,))
    token = first.step("dp", low_bits[1], after=(token,))
    token = attn.step("dp", low_bits[1], after=(token,))
    token = first.step("dp", low_bits[2], after=(token,))
    token = attn.step("dp", low_bits[2], after=(token,))
    for bit in low_bits[3:]:
        for part in (skip_part, down, into, first, attn):
            part.step("dp", bit)
    down_own, in_own, attn_own = down.total(), into.total(), attn.total()
    first_half_sum = x_sum(first.total())
    skip_half = x_sum(skip_part.total())

    square = lambda value: jnp.sum(value * value)
    n_copies = n_mp // 2
    local = (
        square(down_own)
        + square(in_own)
        + square(attn_own)
        + (square(skip_half) + square(first_half_sum)) / n_copies
    )
    total = butterfly(jnp.broadcast_to(local, (8, LANES)))[0, 0]
    grad_norm = jnp.sqrt(total)
    factor = jnp.minimum(1.0, clip_limit / (grad_norm + 1e-06))

    red_skip = jnp.concatenate(by_core([skip_half, swap(skip_half, "mp", 0)]), axis=1)
    own = [shared.pieces(part) for part in by_core([first_half_sum, swap(first_half_sum, "mp", 0)])]
    red_stem = jnp.concatenate([own[0][0], own[1][0]], axis=-1)
    red_embed = jnp.concatenate([own[0][1], own[1][1]], axis=-1)
    red_token = jnp.concatenate([own[0][2], own[1][2]], axis=-1)[:, : PATCHES + 6].T
    red_decoder = jnp.concatenate([own[0][3], own[1][3]], axis=0).reshape(-1)[: shared.flat]
    red_qkv = attn_own[:, :attn_cut]
    red_out = attn_own[:, attn_cut:].T
    red_in = in_own
    red_down = down_own.T
    reduced = (
        red_stem, red_embed, red_token, red_qkv, red_out, red_in, red_down, red_skip, red_decoder,
    )
    rates = [learn_rate] * 9
    rates[2] = token_rate
    results = [
        adamw(weight, grad * factor, first, second, rate)
        for weight, grad, first, second, rate in zip(
            masters, reduced, firsts, seconds, rates, strict=True
        )
    ]
    news = [item[0] for item in results]
    moms = [item[1] for item in results]
    secs = [item[2] for item in results]
    return (loss, pixel_count, grad_norm, *news, *moms, *secs)


def solution(mesh):
    weights = (
        P("dp", None),
        P("dp", None),
        P(None, "dp"),
        P("dp", "mp"),
        P("mp", "dp"),
        P("dp", "mp"),
        P("mp", "dp"),
        P("dp", None),
        P("dp"),
    )
    placed = (P("dp", None, None), P("dp", None, None), P("dp"), P("dp")) + weights * 3
    outs = (P(), P(), P()) + weights * 3
    return jax.shard_map(body, mesh=mesh, in_specs=placed, out_specs=outs, check_vma=False)
```

time: 685 us -> 549 us (0.80)
  Pallas kernels: 30.1 us -> 230 us
  waiting for transfers between devices: 252 us -> 147 us
  matrix products: 100 us -> 0.16 us
  local copies, waits for them, and re-layouts: 133 us -> 54.8 us
  other arithmetic: 109 us -> 39.4 us
  between operations: 13.3 us -> 24.6 us
    pallas_call x4 -> x45, Pallas kernels: 30.1 us -> 230 us  [the longest x18 55 us: step(): pl.pallas_call(kernel, grid=(steps,), in_specs=[SCALAR] + [block(shape)]...]
    ppermute x50, waiting for transfers between devices: 252 us -> 147 us  [swap(): return lax.ppermute(value, axis, [(i, i ^ 1 << bit) for i in range(size)])]
    dot_general x29 -> x0, matrix products: 59.8 us -> none  [the longest x18 35.5 us: t_matmul(): lax.dot_general(left, right, (((0,), (0,)), ((), ())), preferred_element_...]
    dot_general x12 -> x1, matrix products: 40.3 us -> 0.16 us  [matmul(): return jnp.dot(left, right, preferred_element_type=f32)]
    another operation x32 -> x5, other arithmetic: 20.2 us -> 2.38 us  [the longest x2 1.25 us: body(): jnp.stack(dec_parts, axis=1).reshape(n_dp, -1)[:, :shared.flat].reshape(-1)]
    slice x18 -> x5, local copies, waits for them, and re-layouts: 19.6 us -> 1.97 us  [the longest x4 1.92 us: pieces(): value[..., a:b, :]]
    select_n x6 -> x3, other arithmetic: 17.4 us -> 3.37 us  [the longest x1 1.77 us: body(): jnp.where(core == 0, pair[1], pair[0])]
    add x16 -> x2, other arithmetic: 14 us -> 0.12 us  [x_sum(): return value.astype(f32) + swap(value, 'mp', 1).astype(f32)]
  transfers between devices with their start and end apart: 50 -> 51, of which waited for: 31 -> 24; matrix products, arithmetic and copies ran while one was open for 28% -> 7% of each run, Pallas kernels for 1% -> 34%
where the time goes in v2:
time: 549 us; the launch traced here: 541 us
  Pallas kernels  230 us (42%)
  waiting for transfers between devices  147 us (27%)
  local copies, waits for them, and re-layouts  54.8 us (10%)
  starting transfers between devices  45.9 us (8%)
  other arithmetic  39.4 us (7%)
  between operations  24.6 us (4%)
    ppermute x50, waiting for transfers between devices, swap(): return lax.ppermute(value, axis, [(i, i ^ 1 << bit) for i in range(size)])  147 us
    pallas_call x18, Pallas kernels, step(): pl.pallas_call(kernel, grid=(steps,), in_specs=[SCALAR] + [block(shape)]...  55 us
    ppermute x50, starting transfers between devices, swap(): return lax.ppermute(value, axis, [(i, i ^ 1 << bit) for i in range(size)])  45.9 us
    unnamed x175, local copies, waits for them, and re-layouts  36.2 us
    pallas_call x10, Pallas kernels, finish(): pl.pallas_call(kernel, in_specs=[SCALAR] + [FULL] * 2 + waits, out_specs=...  23.7 us
    pallas_call x1, Pallas kernels, leave(): pl.pallas_call(leave_kernel, in_specs=[SCALAR] + [FULL] * 10, out_specs=[...  16.5 us
    pallas_call x1, Pallas kernels, middle(): pl.pallas_call(middle_kernel, grid=(parts,), in_specs=[whole_of(value) fo...  16.1 us
    pallas_call x1, Pallas kernels, attn_back(): pl.pallas_call(kernel, grid=(parts,), in_specs=[whole(width), whole(width...  15.4 us
  transfers between devices with their start and end apart: 51, of which 24 were waited for; matrix products, arithmetic and copies ran while one was open for 7% of the time, Pallas kernels for 34%

profile of v2, /device:TPU:0, one launch (start us, length us, event | category | flops | bytes accessed | tf_op | source)
XLA Modules:
  0.0 541.5 jit_solution(17191429954130782141)
XLA Ops:
  13.4 4.0 collective-permute-start
  17.8 18.8 %collective-permute-done = bf16[800,128]{1,0:T(8,128)(2,1)S(1)} collective-permute-done((bf16[800,128]{1,0:T(8,128)(2,1)}, bf16[800,128]{1,0:T(8,128)(2,1)S(1)}, u32[]{:S(2)}, u32[]{:S(2)}) %collective-permute-start) | collective-permute-done | bytes 204832 | tf_op jit(solution)/shard_map/ppermute | solution.py:86
  44.9 6.7 %collective-permute-done.1 = bf16[1600,128]{1,0:T(8,128)(2,1)S(1)} collective-permute-done((bf16[1600,128]{1,0:T(8,128)(2,1)}, bf16[1600,128]{1,0:T(8,128)(2,1)S(1)}, u32[]{:S(2)}, u32[]{:S(2)}) %collective-permute-start.1) | collective-permute-done | bytes 409632 | tf_op jit(solution)/shard_map/ppermute | solution.py:86
  57.9 5.4 %collective-permute-done.4 = bf16[192,768]{1,0:T(8,128)(2,1)S(1)} collective-permute-done((bf16[192,768]{1,0:T(8,128)(2,1)}, bf16[192,768]{1,0:T(8,128)(2,1)S(1)}, u32[]{:S(2)}, u32[]{:S(2)}) %collective-permute-start.4) | collective-permute-done | bytes 294944 | tf_op jit(solution)/shard_map/ppermute | solution.py:86
  71.5 28.7 %collective-permute-done.6 = bf16[128,1280]{1,0:T(8,128)(2,1)S(1)} collective-permute-done((bf16[128,1280]{1,0:T(8,128)(2,1)}, bf16[128,1280]{1,0:T(8,128)(2,1)S(1)}, u32[]{:S(2)}, u32[]{:S(2)}) %collective-permute-start.6) | collective-permute-done | bytes 327712 | tf_op jit(solution)/shard_map/ppermute | solution.py:86
  117.2 15.0 %collective-permute-done.9 = bf16[256,1280]{1,0:T(8,128)(2,1)S(1)} collective-permute-done((bf16[256,1280]{1,0:T(8,128)(2,1)S(1)}, bf16[256,1280]{1,0:T(8,128)(2,1)S(1)}, u32[]{:S(2)}, u32[]{:S(2)}) %collective-permute-start.9) | collective-permute-done | bytes 655392 | tf_op jit(solution)/shard_map/ppermute | solution.py:86
  153.2 4.0 unpack.1
  157.2 14.9 %enter.1 = (bf16[416,1024]{1,0:T(8,128)(2,1)}, bf16[416,1024]{1,0:T(8,128)(2,1)}, f32[416,768]{1,0:T(8,128)}, bf16[416,768]{1,0:T(8,128)(2,1)}, bf16[4,416,576]{...) custom-call(bf16[416,256]{1,0:T(8,128)(2,1)} %bitcast.256, bf16[256,1024]{1,0:T(8,128)(2,1)} %get-tuple-element.114.stem_ref, ...), custom_call_target="tpu_custom_call" | custom-call | flops 60000002048 | bytes 180000000 | tf_op jit(solution)/shard_map/enter/pallas_call | solution.py:319
  175.7 16.1 %middle.1 = (f32[416,768]{1,0:T(8,128)}, bf16[416,768]{1,0:T(8,128)(2,1)}, bf16[4,416,768]{2,1,0:T(8,128)(2,1)}, bf16[4,416,768]{2,1,0:T(8,128)(2,1)}, f32[416,768]{1,0:T(8,128)}, /*index=5*/bf16[416,768]{1,0:T(8,128)(2,1)}) custom-call(bf16[4,416,192]{2,1,0:T(8,128)(2,1)} %get-tuple-element.118.ctx_ref.refs_3_, ...), custom_call_target="tpu_custom_call" | custom-call | flops 77999996928 | bytes 234000000 | tf_op jit(solution)/shard_map/middle/pallas_call | solution.py:394
  191.8 16.5 %leave.1 = (f32[416,256]{1,0:T(8,128)}, bf16[416,256]{1,0:T(8,128)(2,1)}, bf16[416,2560]{1,0:T(8,128)(2,1)}, bf16[416,512]{1,0:T(8,128)(2,1)}, bf16[416,1024]{1,...) custom-call(s32[1]{0:T(128)} %bitcast.core_ref.refs_0_, ...), custom_call_target="tpu_custom_call" | custom-call | flops 48000000000 | bytes 144000000 | tf_op jit(solution)/shard_map/leave/pallas_call | solution.py:499
  234.9 9.4 %leave_back.1 = (bf16[416,2304]{1,0:T(8,128)(2,1)}, bf16[416,2560]{1,0:T(8,128)(2,1)}) custom-call(f32[2,19]{1,0:T(2,128)} %pad_maximum_fusion.5.coef_ref, f32[416,2304]{1,0:T(8,128)} %get-tuple-element.122.logits_ref, s32[416,256]{1,0:T(8,128)} %bitcast.242, bf16[416,2560]{1,0:T(8,128)(2,1)} %get-tuple-element.123.slope_ref, ...), custom_call_target="tpu_custom_call" | custom-call | flops 30000001024 | bytes 90000000 | tf_op jit(solution)/shard_map/leave_back/pallas_call | solution.py:572
  244.3 6.8 %skip_grad.1 = (bf16[1024,1280]{1,0:T(8,128)(2,1)}, bf16[1024,1280]{1,0:T(8,128)(2,1)}) custom-call(s32[1]{0:T(128)} %bitcast.core_ref.refs_0_, bf16[416,1024]{1,0:T(8,128)(2,1)} %get-tuple-element.117.refs_3_.hidden_ref, bf16[416,2560]{1,0:T(8,128)(2,1)} %get-tuple-element.124.g_skips_ref.refs_0_.refs_4_.refs_8_), custom_call_target="tpu_custom_call" | custom-call | flops 17999998976 | bytes 54000000 | tf_op jit(solution)/shard_map/skip_grad/pallas_call | solution.py:599
  251.1 5.5 %turn.1 = (bf16[416,256]{1,0:T(8,128)(2,1)}, f32[416,768]{1,0:T(8,128)}, bf16[416,768]{1,0:T(8,128)(2,1)}, f32[16,768]{1,0:T(8,128)}) custom-call(bf16[416,2560]{1,0:T(8,128)(2,1)} %get-tuple-element.124.g_skips_ref.refs_0_.refs_4_.refs_8_, bf16[256,512]{1,0:T(8,128)(2,1)} %reshape.459.one_ref.refs_1_, f32[416,256]{1,0:T(8,128)} %get-tuple-element.125.refs_2_, ...), custom_call_target="tpu_custom_call" | custom-call | flops 32999999488 | bytes 99000000 | tf_op jit(solution)/shard_map/turn/pallas_call | solution.py:625
  258.1 4.5 scatter_step.18
  264.2 6.0 %half_grad.2 = (bf16[768,1536]{1,0:T(8,128)(2,1)}, bf16[768,1536]{1,0:T(8,128)(2,1)}) custom-call(s32[1]{0:T(128)} %bitcast.core_ref.refs_0_, bf16[416,768]{1,0:T(8,128)(2,1)} %get-tuple-element.128.refs_1_.refs_0_, bf16[4,416,768]{2,1,0:T(8,128)(2,1)} %get-tuple-element.129.refs_2_, bf16[512,1280]{1,0:T(8,128)(2,1)} %bitcast.266), custom_call_target="tpu_custom_call" | custom-call | flops 17999998976 | bytes 54000000 | tf_op jit(solution)/shard_map/half_grad/pallas_call | solution.py:943
  270.4 14.5 %middle_back.1 = (bf16[4,416,768]{2,1,0:T(8,128)(2,1)}, f32[416,768]{1,0:T(8,128)}, bf16[416,768]{1,0:T(8,128)(2,1)}, bf16[4,416,192]{2,1,0:T(8,128)(2,1)}, f32[16,768]{1,0:T(8,128)}) custom-call(bf16[416,768]{1,0:T(8,128)(2,1)} %get-tuple-element.128.refs_1_.refs_0_, bf16[4,768,1536]{2,1,0:T(8,128)(2,1)} %bitcast.264, ...), custom_call_target="tpu_custom_call" | custom-call | flops 62999998464 | bytes 189000000 | tf_op jit(solution)/shard_map/middle_back/pallas_call | solution.py:915
  286.3 4.3 scatter_step.19
  299.6 6.1 %half_grad.3 = (bf16[768,1536]{1,0:T(8,128)(2,1)}, bf16[768,1536]{1,0:T(8,128)(2,1)}) custom-call(s32[1]{0:T(128)} %bitcast.core_ref.refs_0_, bf16[416,768]{1,0:T(8,128)(2,1)} %get-tuple-element.144.refs_1_, bf16[4,416,768]{2,1,0:T(8,128)(2,1)} %get-tuple-element.138.refs_3_.refs_2_, bf16[256,1280]{1,0:T(8,128)(2,1)} %bitcast.268), custom_call_target="tpu_custom_call" | custom-call | flops 17999998976 | bytes 54000000 | tf_op jit(solution)/shard_map/half_grad/pallas_call | solution.py:943
  305.7 15.4 %attn_back.1.refs_3_.refs_1_ = bf16[4,416,576]{2,1,0:T(8,128)(2,1)} custom-call(bf16[4,416,576]{2,1,0:T(8,128)(2,1)} %get-tuple-element.142.refs_0_, bf16[4,416,192]{2,1,0:T(8,128)(2,1)} %get-tuple-element.143.refs_1_, bf16[768,1536]{1,0:T(8,128)(2,1)} %get-tuple-element.147.refs_2_), custom_call_target="tpu_custom_call" | custom-call | flops 44999999488 | bytes 135000000 | tf_op jit(solution)/shard_map/attn_back/pallas_call | solution.py:983
  322.5 4.3 scatter_step.21
  331.6 7.2 %attn_grad.1 = (bf16[768,1536]{1,0:T(8,128)(2,1)}, bf16[768,1536]{1,0:T(8,128)(2,1)}) custom-call(bf16[416,768]{1,0:T(8,128)(2,1)} %get-tuple-element.141.refs_0_, bf16[4,416,576]{2,1,0:T(8,128)(2,1)} %attn_back.1.refs_3_.refs_1_, bf16[416,768]{1,0:T(8,128)(2,1)} %get-tuple-element.148.refs_2_, bf16[4,416,192]{2,1,0:T(8,128)(2,1)} %get-tuple-element.118.ctx_ref.refs_3_, ...), custom_call_target="tpu_custom_call" | custom-call | flops 20999999488 | bytes 63000000 | tf_op jit(solution)/shard_map/attn_grad/pallas_call | solution.py:1013
  344.0 6.9 %decoder_grad.1.refs_12_.refs_9_ = bf16[2,8,192,128]{3,2,1,0:T(8,128)(2,1)} custom-call(bf16[416,1024]{1,0:T(8,128)(2,1)} %get-tuple-element.160.refs_0_, bf16[416,2304]{1,0:T(8,128)(2,1)} %get-tuple-element.161.refs_1_, bf16[416,1024]{1,0:T(8,128)(2,1)} %get-tuple-element.162.refs_2_, bf16[416,512]{1,0:T(8,128)(2,1)} %get-tuple-element.163.refs_3_, ...), custom_call_target="tpu_custom_call" | custom-call | flops 20999999488 | bytes 63000000 | tf_op jit(solution)/shard_map/decoder_grad/pallas_call | solution.py:738
  350.9 14.2 %enter_back.1 = (bf16[416,768]{1,0:T(8,128)(2,1)}, bf16[416,1024]{1,0:T(8,128)(2,1)}, f32[208,768]{1,0:T(8,128)}, f32[16,768]{1,0:T(8,128)}) custom-call(s32[1]{0:T(128)} %bitcast.core_ref.refs_0_, bf16[4,416,576]{2,1,0:T(8,128)(2,1)} %attn_back.1.refs_3_.refs_1_, bf16[768,1536]{1,0:T(8,128)(2,1)} %gather_step.18.own_ref.refs_6_.refs_2_, ...), custom_call_target="tpu_custom_call" | custom-call | flops 62999998464 | bytes 189000000 | tf_op jit(solution)/shard_map/enter_back/pallas_call | solution.py:1058
  366.6 4.4 scatter_step.24
  372.0 3.7 scatter_step.25
  379.0 5.7 %first_grad.1 = (bf16[8,800,128]{2,1,0:T(8,128)(2,1)}, bf16[8,800,128]{2,1,0:T(8,128)(2,1)}) custom-call(s32[1]{0:T(128)} %bitcast.core_ref.refs_0_, bf16[416,256]{1,0:T(8,128)(2,1)} %bitcast.257, bf16[416,1024]{1,0:T(8,128)(2,1)} %get-tuple-element.170.refs_2_, bf16[416,1024]{1,0:T(8,128)(2,1)} %get-tuple-element.117.refs_3_.hidden_ref, ...), custom_call_target="tpu_custom_call" | custom-call | flops 17999998976 | bytes 54000000 | tf_op jit(solution)/shard_map/first_grad/pallas_call | solution.py:795
  387.3 13.1 %collective-permute-done.29 = bf16[384,768]{1,0:T(8,128)(2,1)S(1)} collective-permute-done((bf16[384,768]{1,0:T(8,128)(2,1)S(1)}, bf16[384,768]{1,0:T(8,128)(2,1)S(1)}, u32[]{:S(2)}, u32[]{:S(2)}) %collective-permute-start.29) | collective-permute-done | bytes 589856 | tf_op jit(solution)/shard_map/ppermute | solution.py:86
  404.6 4.1 scatter_step.28
  414.2 11.6 %collective-permute-done.27.refs_2_ = bf16[96,1536]{1,0:T(8,128)(2,1)S(1)} collective-permute-done((bf16[96,1536]{1,0:T(8,128)(2,1)}, bf16[96,1536]{1,0:T(8,128)(2,1)S(1)}, u32[]{:S(2)}, u32[]{:S(2)}) %collective-permute-start.27) | collective-permute-done | bytes 294944 | tf_op jit(solution)/shard_map/ppermute | solution.py:86
  429.5 3.7 scatter_step.30
  440.1 7.8 %collective-permute-done.34 = bf16[384,768]{1,0:T(8,128)(2,1)S(1)} collective-permute-done((bf16[384,768]{1,0:T(8,128)(2,1)}, bf16[384,768]{1,0:T(8,128)(2,1)S(1)}, u32[]{:S(2)}, u32[]{:S(2)}) %collective-permute-start.34) | collective-permute-done | bytes 589856 | tf_op jit(solution)/shard_map/ppermute | solution.py:86
  460.1 4.9 collective-permute-done.41
  (397 shorter events, 222.5 us)
Async XLA Ops:
  7.2 168.5 %all-gather.2.cloned.1.call-start = ((), (), s32[]{:S(2)}) async-start(), calls=%async_computation | async-start | bytes 9732096 | tf_op jit(solution)/shard_map/all_gather | solution.py:1213
  13.4 23.2 %collective-permute-start = (bf16[800,128]{1,0:T(8,128)(2,1)}, bf16[800,128]{1,0:T(8,128)(2,1)S(1)}, u32[]{:S(2)}, u32[]{:S(2)}) collective-permute-start(bf16[800,128]{1,0:T(8,128)(2,1)} %pack.1), channel_id=1, source_target_pairs={{0,16},{4,20},{8,24},{12,28},{16,0},{20,4},{24,8},{28,12},{1,17},{... | collective-permute-start | bytes 614408 | tf_op jit(solution)/shard_map/ppermute | solution.py:86
  17.7 24.7 %collective-permute-start.2 = (bf16[96,768]{1,0:T(8,128)(2,1)S(1)}, bf16[96,768]{1,0:T(8,128)(2,1)S(1)}, u32[]{:S(2)}, u32[]{:S(2)}) collective-permute-start(bf16[96,768]{1,0:T(8,128)(2,1)S(1)} %pad_maximum_fusion.3), channel_id=1, source_target_pairs={{0,16},{4,20},{8,24},{12,28},{16,0},{20,4},{24,8},{28,12},{1,17},{... | collective-permute-start | bytes 442376 | tf_op jit(solution)/shard_map/ppermute | solution.py:86
  39.1 12.5 %collective-permute-start.1 = (bf16[1600,128]{1,0:T(8,128)(2,1)}, bf16[1600,128]{1,0:T(8,128)(2,1)S(1)}, u32[]{:S(2)}, u32[]{:S(2)}) collective-permute-start(bf16[1600,128]{1,0:T(8,128)(2,1)} %bitcast.245), channel_id=1, source_target_pairs={{0,4},{4,0},{8,12},{12,8},{16,20},{20,16},{24,28},{28,24},{1,5},{5... | collective-permute-start | bytes 1228808 | tf_op jit(solution)/shard_map/ppermute | solution.py:86
  44.9 18.4 %collective-permute-start.4 = (bf16[192,768]{1,0:T(8,128)(2,1)}, bf16[192,768]{1,0:T(8,128)(2,1)S(1)}, u32[]{:S(2)}, u32[]{:S(2)}) collective-permute-start(bf16[192,768]{1,0:T(8,128)(2,1)} %bitcast.195), channel_id=1, source_target_pairs={{0,8},{4,12},{8,0},{12,4},{16,24},{20,28},{24,16},{28,20},{1,9},{5... | collective-permute-start | bytes 884744 | tf_op jit(solution)/shard_map/ppermute | solution.py:86
  54.4 56.8 %collective-permute-start.3 = (bf16[3200,128]{1,0:T(8,128)(2,1)}, bf16[3200,128]{1,0:T(8,128)(2,1)S(1)}, u32[]{:S(2)}, u32[]{:S(2)}) collective-permute-start(bf16[3200,128]{1,0:T(8,128)(2,1)} %bitcast.183), channel_id=1, source_target_pairs={{0,8},{4,12},{8,0},{12,4},{16,24},{20,28},{24,16},{28,20},{1,9},{5... | collective-permute-start | bytes 2457608 | tf_op jit(solution)/shard_map/ppermute | solution.py:86
  65.9 37.0 %collective-permute-start.5 = (bf16[384,768]{1,0:T(8,128)(2,1)}, bf16[384,768]{1,0:T(8,128)(2,1)S(1)}, u32[]{:S(2)}, u32[]{:S(2)}) collective-permute-start(bf16[384,768]{1,0:T(8,128)(2,1)} %bitcast.189), channel_id=1, source_target_pairs={{0,4},{4,0},{8,12},{12,8},{16,20},{20,16},{24,28},{28,24},{1,5},{5... | collective-permute-start | bytes 1769480 | tf_op jit(solution)/shard_map/ppermute | solution.py:86
  67.8 32.5 %collective-permute-start.6 = (bf16[128,1280]{1,0:T(8,128)(2,1)}, bf16[128,1280]{1,0:T(8,128)(2,1)S(1)}, u32[]{:S(2)}, u32[]{:S(2)}) collective-permute-start(bf16[128,1280]{1,0:T(8,128)(2,1)} %gate.1), channel_id=1, source_target_pairs={{0,16},{4,20},{8,24},{12,28},{16,0},{20,4},{24,8},{28,12},{1,17},{... | collective-permute-start | bytes 983048 | tf_op jit(solution)/shard_map/ppermute | solution.py:86
  106.1 29.4 %collective-permute-start.8 = (bf16[768,768]{1,0:T(8,128)(2,1)}, bf16[768,768]{1,0:T(8,128)(2,1)}, u32[]{:S(2)}, u32[]{:S(2)}) collective-permute-start(bf16[768,768]{1,0:T(8,128)(2,1)} %bitcast.176), channel_id=1, source_target_pairs={{0,2},{1,3},{2,0},{3,1},{4,6},{5,7},{6,4},{7,5},{8,10},{9,11},{10,... | collective-permute-start | bytes 3538952 | tf_op jit(solution)/shard_map/ppermute | solution.py:86
  114.9 26.4 %collective-permute-start.7 = (bf16[6400,128]{1,0:T(8,128)(2,1)}, bf16[6400,128]{1,0:T(8,128)(2,1)}, u32[]{:S(2)}, u32[]{:S(2)}) collective-permute-start(bf16[6400,128]{1,0:T(8,128)(2,1)} %bitcast.179), channel_id=1, source_target_pairs={{0,1},{1,0},{2,3},{3,2},{4,5},{5,4},{6,7},{7,6},{8,9},{9,8},{10,11... | collective-permute-start | bytes 4915208 | tf_op jit(solution)/shard_map/ppermute | solution.py:86
  115.0 17.2 %collective-permute-start.9 = (bf16[256,1280]{1,0:T(8,128)(2,1)S(1)}, bf16[256,1280]{1,0:T(8,128)(2,1)S(1)}, u32[]{:S(2)}, u32[]{:S(2)}) collective-permute-start(bf16[256,1280]{1,0:T(8,128)(2,1)S(1)} %bitcast.188), channel_id=1, source_target_pairs={{0,8},{4,12},{8,0},{12,4},{16,24},{20,28},{24,16},{28,20},{1,9},{5... | collective-permute-start | bytes 1966088 | tf_op jit(solution)/shard_map/ppermute | solution.py:86
  138.7 18.6 %collective-permute-start.10 = (bf16[768,1536]{1,0:T(8,128)(2,1)}, bf16[768,1536]{1,0:T(8,128)(2,1)}, u32[]{:S(2)}, u32[]{:S(2)}) collective-permute-start(bf16[768,1536]{1,0:T(8,128)(2,1)} %gather_step.18.own_ref.refs_6_.refs_2_), channel_id=1, source_target_pairs={{0,1},{1,0},{2,3},{3,2},{4,5},{5,4},{6,7},{7,6},{8,9},{9,8},{10,11... | collective-permute-start | bytes 7077896 | tf_op jit(solution)/shard_map/ppermute | solution.py:86
  141.0 31.3 %collective-permute-start.11 = (bf16[512,1280]{1,0:T(8,128)(2,1)S(1)}, bf16[512,1280]{1,0:T(8,128)(2,1)}, u32[]{:S(2)}, u32[]{:S(2)}) collective-permute-start(bf16[512,1280]{1,0:T(8,128)(2,1)S(1)} %bitcast.175), channel_id=1, source_target_pairs={{0,4},{4,0},{8,12},{12,8},{16,20},{20,16},{24,28},{28,24},{1,5},{5... | collective-permute-start | bytes 3932168 | tf_op jit(solution)/shard_map/ppermute | solution.py:86
  175.7 16.1 %collective-permute-start.12 = (bf16[1024,1280]{1,0:T(8,128)(2,1)}, bf16[1024,1280]{1,0:T(8,128)(2,1)}, u32[]{:S(2)}, u32[]{:S(2)}) collective-permute-start(bf16[1024,1280]{1,0:T(8,128)(2,1)} %bitcast.199), channel_id=1, source_target_pairs={{0,1},{1,0},{2,3},{3,2},{4,5},{5,4},{6,7},{7,6},{8,9},{9,8},{10,11... | collective-permute-start | bytes 7864328 | tf_op jit(solution)/shard_map/ppermute | solution.py:86
  262.6 31.7 %collective-permute-start.21 = (bf16[512,1280]{1,0:T(8,128)(2,1)}, bf16[512,1280]{1,0:T(8,128)(2,1)S(1)}, u32[]{:S(2)}, u32[]{:S(2)}) collective-permute-start(bf16[512,1280]{1,0:T(8,128)(2,1)} %bitcast.265), channel_id=1, source_target_pairs={{0,4},{4,0},{8,12},{12,8},{16,20},{20,16},{24,28},{28,24},{1,5},{5... | collective-permute-start | bytes 3932168 | tf_op jit(solution)/shard_map/ppermute | solution.py:86
  270.1 14.7 %collective-permute-start.19 = (bf16[768,1536]{1,0:T(8,128)(2,1)}, bf16[768,1536]{1,0:T(8,128)(2,1)S(1)}, u32[]{:S(2)}, u32[]{:S(2)}) collective-permute-start(bf16[768,1536]{1,0:T(8,128)(2,1)} %get-tuple-element.134.refs_8_), channel_id=1, source_target_pairs={{0,1},{1,0},{2,3},{3,2},{4,5},{5,4},{6,7},{7,6},{8,9},{9,8},{10,11... | collective-permute-start | bytes 7077896 | tf_op jit(solution)/shard_map/ppermute | solution.py:86
  290.6 48.5 %collective-permute-start.20 = (bf16[384,1536]{1,0:T(8,128)(2,1)}, bf16[384,1536]{1,0:T(8,128)(2,1)S(1)}, u32[]{:S(2)}, u32[]{:S(2)}) collective-permute-start(bf16[384,1536]{1,0:T(8,128)(2,1)} %bitcast.222), channel_id=1, source_target_pairs={{0,4},{4,0},{8,12},{12,8},{16,20},{20,16},{24,28},{28,24},{1,5},{5... | collective-permute-start | bytes 3538952 | tf_op jit(solution)/shard_map/ppermute | solution.py:86
  298.4 29.8 %collective-permute-start.22 = (bf16[256,1280]{1,0:T(8,128)(2,1)}, bf16[256,1280]{1,0:T(8,128)(2,1)S(1)}, u32[]{:S(2)}, u32[]{:S(2)}) collective-permute-start(bf16[256,1280]{1,0:T(8,128)(2,1)} %bitcast.267), channel_id=1, source_target_pairs={{0,8},{4,12},{8,0},{12,4},{16,24},{20,28},{24,16},{28,20},{1,9},{5... | collective-permute-start | bytes 1966088 | tf_op jit(solution)/shard_map/ppermute | solution.py:86
  305.7 15.4 %collective-permute-start.23 = (bf16[768,1536]{1,0:T(8,128)(2,1)}, bf16[768,1536]{1,0:T(8,128)(2,1)S(1)}, u32[]{:S(2)}, u32[]{:S(2)}) collective-permute-start(bf16[768,1536]{1,0:T(8,128)(2,1)} %get-tuple-element.147.refs_2_), channel_id=1, source_target_pairs={{0,1},{1,0},{2,3},{3,2},{4,5},{5,4},{6,7},{7,6},{8,9},{9,8},{10,11... | collective-permute-start | bytes 7077896 | tf_op jit(solution)/shard_map/ppermute | solution.py:86
  326.8 44.2 %collective-permute-start.25 = (bf16[768,768]{1,0:T(8,128)(2,1)}, bf16[768,768]{1,0:T(8,128)(2,1)S(1)}, u32[]{:S(2)}, u32[]{:S(2)}) collective-permute-start(bf16[768,768]{1,0:T(8,128)(2,1)} %get-tuple-element.151.refs_3_), channel_id=1, source_target_pairs={{0,2},{1,3},{2,0},{3,1},{4,6},{5,7},{6,4},{7,5},{8,10},{9,11},{10,... | collective-permute-start | bytes 3538952 | tf_op jit(solution)/shard_map/ppermute | solution.py:86
  338.9 26.3 %collective-permute-start.26 = (bf16[768,1536]{1,0:T(8,128)(2,1)}, bf16[768,1536]{1,0:T(8,128)(2,1)S(1)}, u32[]{:S(2)}, u32[]{:S(2)}) collective-permute-start(bf16[768,1536]{1,0:T(8,128)(2,1)} %get-tuple-element.153.refs_3_), channel_id=1, source_target_pairs={{0,1},{1,0},{2,3},{3,2},{4,5},{5,4},{6,7},{7,6},{8,9},{9,8},{10,11... | collective-permute-start | bytes 7077896 | tf_op jit(solution)/shard_map/ppermute | solution.py:86
  342.9 32.9 %collective-permute-start.24 = (bf16[192,1536]{1,0:T(8,128)(2,1)}, bf16[192,1536]{1,0:T(8,128)(2,1)S(1)}, u32[]{:S(2)}, u32[]{:S(2)}) collective-permute-start(bf16[192,1536]{1,0:T(8,128)(2,1)} %bitcast.270), channel_id=1, source_target_pairs={{0,8},{4,12},{8,0},{12,4},{16,24},{20,28},{24,16},{28,20},{1,9},{5... | collective-permute-start | bytes 1769480 | tf_op jit(solution)/shard_map/ppermute | solution.py:86
  384.6 18.8 %collective-permute-start.28 = (bf16[6400,128]{1,0:T(8,128)(2,1)}, bf16[6400,128]{1,0:T(8,128)(2,1)S(1)}, u32[]{:S(2)}, u32[]{:S(2)}) collective-permute-start(bf16[6400,128]{1,0:T(8,128)(2,1)} %bitcast.206), channel_id=1, source_target_pairs={{0,1},{1,0},{2,3},{3,2},{4,5},{5,4},{6,7},{7,6},{8,9},{9,8},{10,11... | collective-permute-start | bytes 4915208 | tf_op jit(solution)/shard_map/ppermute | solution.py:86
  384.7 15.7 %collective-permute-start.29 = (bf16[384,768]{1,0:T(8,128)(2,1)S(1)}, bf16[384,768]{1,0:T(8,128)(2,1)S(1)}, u32[]{:S(2)}, u32[]{:S(2)}) collective-permute-start(bf16[384,768]{1,0:T(8,128)(2,1)S(1)} %bitcast.233), channel_id=1, source_target_pairs={{0,4},{4,0},{8,12},{12,8},{16,20},{20,16},{24,28},{28,24},{1,5},{5... | collective-permute-start | bytes 1769480 | tf_op jit(solution)/shard_map/ppermute | solution.py:86
  386.1 42.4 %collective-permute-start.32 = (bf16[768,768]{1,0:T(8,128)(2,1)S(1)}, bf16[768,768]{1,0:T(8,128)(2,1)S(1)}, u32[]{:S(2)}, u32[]{:S(2)}) collective-permute-start(bf16[768,768]{1,0:T(8,128)(2,1)S(1)} %copy-done.22), channel_id=1, source_target_pairs={{0,2},{1,3},{2,0},{3,1},{4,6},{5,7},{6,4},{7,5},{8,10},{9,11},{10,... | collective-permute-start | bytes 3538952 | tf_op jit(solution)/shard_map/ppermute | solution.py:86
  386.8 25.7 %collective-permute-start.39 = (bf16[128,1280]{1,0:T(8,128)(2,1)S(1)}, bf16[128,1280]{1,0:T(8,128)(2,1)S(1)}, u32[]{:S(2)}, u32[]{:S(2)}) collective-permute-start(bf16[128,1280]{1,0:T(8,128)(2,1)S(1)} %bitcast.273), channel_id=1, source_target_pairs={{0,16},{4,20},{8,24},{12,28},{16,0},{20,4},{24,8},{28,12},{1,17},{... | collective-permute-start | bytes 983048 | tf_op jit(solution)/shard_map/ppermute | solution.py:86
  408.7 27.8 %collective-permute-start.35 = (bf16[3200,128]{1,0:T(8,128)(2,1)}, bf16[3200,128]{1,0:T(8,128)(2,1)S(1)}, u32[]{:S(2)}, u32[]{:S(2)}) collective-permute-start(bf16[3200,128]{1,0:T(8,128)(2,1)} %bitcast.226), channel_id=1, source_target_pairs={{0,4},{4,0},{8,12},{12,8},{16,20},{20,16},{24,28},{28,24},{1,5},{5... | collective-permute-start | bytes 2457608 | tf_op jit(solution)/shard_map/ppermute | solution.py:86
  410.1 15.7 %collective-permute-start.27 = (bf16[96,1536]{1,0:T(8,128)(2,1)}, bf16[96,1536]{1,0:T(8,128)(2,1)S(1)}, u32[]{:S(2)}, u32[]{:S(2)}) collective-permute-start(bf16[96,1536]{1,0:T(8,128)(2,1)} %bitcast.73.refs_10_), channel_id=1, source_target_pairs={{0,16},{4,20},{8,24},{12,28},{16,0},{20,4},{24,8},{28,12},{1,17},{... | collective-permute-start | bytes 884744 | tf_op jit(solution)/shard_map/ppermute | solution.py:86
  410.7 23.1 %collective-permute-start.31 = (bf16[192,768]{1,0:T(8,128)(2,1)S(1)}, bf16[192,768]{1,0:T(8,128)(2,1)S(1)}, u32[]{:S(2)}, u32[]{:S(2)}) collective-permute-start(bf16[192,768]{1,0:T(8,128)(2,1)S(1)} %bitcast.253), channel_id=1, source_target_pairs={{0,8},{4,12},{8,0},{12,4},{16,24},{20,28},{24,16},{28,20},{1,9},{5... | collective-permute-start | bytes 884744 | tf_op jit(solution)/shard_map/ppermute | solution.py:86
  413.6 26.3 %collective-permute-start.40 = (bf16[128,1280]{1,0:T(8,128)(2,1)S(1)}, bf16[128,1280]{1,0:T(8,128)(2,1)S(1)}, u32[]{:S(2)}, u32[]{:S(2)}) collective-permute-start(bf16[128,1280]{1,0:T(8,128)(2,1)S(1)} %fusion.5), channel_id=1, source_target_pairs={{0,2},{1,3},{2,0},{3,1},{4,6},{5,7},{6,4},{7,5},{8,10},{9,11},{10,... | collective-permute-start | bytes 983048 | tf_op jit(solution)/shard_map/ppermute | solution.py:86
  433.2 14.7 %collective-permute-start.34 = (bf16[384,768]{1,0:T(8,128)(2,1)}, bf16[384,768]{1,0:T(8,128)(2,1)S(1)}, u32[]{:S(2)}, u32[]{:S(2)}) collective-permute-start(bf16[384,768]{1,0:T(8,128)(2,1)} %bitcast.238), channel_id=1, source_target_pairs={{0,4},{4,0},{8,12},{12,8},{16,20},{20,16},{24,28},{28,24},{1,5},{5... | collective-permute-start | bytes 1769480 | tf_op jit(solution)/shard_map/ppermute | solution.py:86
  440.0 26.9 %collective-permute-start.49 = (f32[128,1280]{1,0:T(8,128)S(1)}, f32[128,1280]{1,0:T(8,128)S(1)}, u32[]{:S(2)}, u32[]{:S(2)}) collective-permute-start(f32[128,1280]{1,0:T(8,128)S(1)} %convert_add_fusion), channel_id=1, source_target_pairs={{0,1},{1,0},{2,3},{3,2},{4,5},{5,4},{6,7},{7,6},{8,9},{9,8},{10,11... | collective-permute-start | bytes 1966088 | tf_op jit(solution)/shard_map/ppermute | solution.py:86
  (99 other events, 602.8 us)
Sparse Core Ops, SparseCore 0:
  11.6 104.1 all-gather.1

commit v3 on v2

--- a/solution.py
+++ b/solution.py
@@ -69,7 +69,7 @@
 
 
 def params():
-    return pltpu.CompilerParams(vmem_limit_bytes=58 * MIB)
+    return pltpu.CompilerParams(vmem_limit_bytes=32 * MIB)
 
 
 def run_after(kernel, count, after):
@@ -219,9 +219,20 @@
 
 
 def butterfly(value):
-    for axis, bits in (("mp", 2), ("dp", log_two(lax.axis_size("dp")))):
-        for bit in range(bits):
-            value = value + swap(value, axis, bit)
+    def hop(value, moves):
+        size = lax.axis_size("dp") * lax.axis_size("mp")
+        get = lambda move: lax.ppermute(value, ("dp", "mp"), [(i, i ^ move) for i in range(size)])
+        if len(moves) == 1:
+            return value + get(moves[0])
+        one, two = moves
+        first, second, third = get(one), get(two), get(one | two)
+        return (value + first) + (second + third)
+
+    value = hop(value, (1,))
+    bits = log_two(lax.axis_size("dp"))
+    moves = [2] + [4 << bit for bit in range(bits)]
+    for i in range(0, len(moves), 2):
+        value = hop(value, tuple(moves[i : i + 2]))
     return value
 
 
@@ -1361,15 +1372,15 @@
         level3, grad_logits, level2, level1, grad_skips, level0, final_low, grad_pre0,
         n_dp, shared.flat_rows, after=(token,),
     )
-    token = decoder_halves
+    attn = core_pair(attn_send, attn_keep)
+    token = attn.step("mp", 1, bf16, after=(decoder_halves,))
     grad_embed_low, grad_pre_stem, grad_pos, sums_1 = enter_back(
         core_id, grad_triple, attn_all, embed, table, grad_resid, embed_b, grad_skips, skip_all,
         slope_stem, after=(token,),
     )
-    attn = core_pair(attn_send, attn_keep)
-    token = attn.step("mp", 1, bf16, after=(grad_embed_low,))
-    token = into.step("dp", low_bits[0], after=(token,))
+    token = into.step("dp", low_bits[0], after=(grad_embed_low,))
     token = down.step("dp", low_bits[2], after=(token,))
+    token = attn.step("dp", low_bits[0], after=(token,))
     if aligned:
         first_send, first_keep = first_grad(
             core_id, pixels, grad_pre_stem, hidden, grad_embed_low, grad_pos, sums_1, sums_2,
@@ -1396,15 +1407,14 @@
         first_send, first_keep = first_half(1 - core), first_half(core)
     wide = lambda value: value.reshape(-1, LANES)
     first = core_pair(wide(first_send), wide(first_keep))
-    token = into.step("dp", low_bits[1], after=(first_send,))
-    token = first.step("dp", low_bits[0], after=(token,))
+    token = first.step("dp", low_bits[0], after=(first_send,))
+    token = into.step("dp", low_bits[1], after=(token,))
     token = down.step("mp", 1, after=(token,))
-    token = attn.step("dp", low_bits[0], after=(token,))
+    token = attn.step("dp", low_bits[1], after=(token,))
+    token = first.step("dp", low_bits[1], after=(token,))
     token = into.step("dp", low_bits[2], after=(token,))
-    token = first.step("dp", low_bits[1], after=(token,))
-    token = attn.step("dp", low_bits[1], after=(token,))
+    token = attn.step("dp", low_bits[2], after=(token,))
     token = first.step("dp", low_bits[2], after=(token,))
-    token = attn.step("dp", low_bits[2], after=(token,))
     for bit in low_bits[3:]:
         for part in (skip_part, down, into, first, attn):
             part.step("dp", bit)

time: 549 us -> 521 us (0.949)
  Pallas kernels: 230 us -> 114 us
  waiting for transfers between devices: 147 us -> 206 us
  starting transfers between devices: 45.9 us -> 67.2 us
  local copies, waits for them, and re-layouts: 54.8 us -> 67.5 us
  other arithmetic: 39.4 us -> 33 us
    pallas_call x18, Pallas kernels: 55 us -> 5.66 us  [step(): pl.pallas_call(kernel, grid=(steps,), in_specs=[SCALAR] + [block(shape)]...]
    ppermute x50 -> x40, waiting for transfers between devices: 147 us -> 191 us  [swap(): return lax.ppermute(value, axis, [(i, i ^ 1 << bit) for i in range(size)])]
    ppermute x0 -> x14, starting transfers between devices: none -> 16.1 us  [hop(): lax.ppermute(value, ('dp', 'mp'), [(i, i ^ move) for i in range(size)])]
    ppermute x0 -> x14, waiting for transfers between devices: none -> 15.3 us  [hop(): lax.ppermute(value, ('dp', 'mp'), [(i, i ^ move) for i in range(size)])]
    pallas_call x10, Pallas kernels: 23.7 us -> 8.67 us  [finish(): pl.pallas_call(kernel, in_specs=[SCALAR] + [FULL] * 2 + waits, out_specs=...]
    pallas_call x2, Pallas kernels: 12 us -> 5.3 us  [half_grad(): pl.pallas_call(kernel, in_specs=[SCALAR] + [FULL] * 2 + waits, out_specs=...]
    unnamed x175 -> x253, local copies, waits for them, and re-layouts: 36.2 us -> 42.3 us
    ppermute x50 -> x40, starting transfers between devices: 45.9 us -> 51 us  [swap(): return lax.ppermute(value, axis, [(i, i ^ 1 << bit) for i in range(size)])]
  transfers between devices with their start and end apart: 51 -> 55, of which waited for: 24 -> 32; matrix products, arithmetic and copies ran while one was open for 7% -> 7% of each run, Pallas kernels for 34% -> 18%
where the time goes in v3:
time: 521 us; the launch traced here: 514 us
  waiting for transfers between devices  206 us (40%)
  Pallas kernels  114 us (22%)
  local copies, waits for them, and re-layouts  67.5 us (13%)
  starting transfers between devices  67.2 us (13%)
  other arithmetic  33 us (6%)
  between operations  25.3 us (5%)
    ppermute x40, waiting for transfers between devices, swap(): return lax.ppermute(value, axis, [(i, i ^ 1 << bit) for i in range(size)])  191 us
    ppermute x40, starting transfers between devices, swap(): return lax.ppermute(value, axis, [(i, i ^ 1 << bit) for i in range(size)])  51 us
    unnamed x253, local copies, waits for them, and re-layouts  42.3 us
    ppermute x14, starting transfers between devices, hop(): lax.ppermute(value, ('dp', 'mp'), [(i, i ^ move) for i in range(size)])  16.1 us
    ppermute x14, waiting for transfers between devices, hop(): lax.ppermute(value, ('dp', 'mp'), [(i, i ^ move) for i in range(size)])  15.3 us
    pallas_call x1, Pallas kernels, attn_back(): pl.pallas_call(kernel, grid=(parts,), in_specs=[whole(width), whole(width...  13.5 us
    pallas_call x1, Pallas kernels, enter(): pl.pallas_call(enter_kernel, in_specs=[FULL] * 6, out_specs=[FULL] * 6, o...  13.3 us
    sub x9, other arithmetic, adamw(): weight - rate * (first_hat / (jnp.sqrt(second_hat) + adam_eps) + decay_ra...  12.9 us
  transfers between devices with their start and end apart: 55, of which 32 were waited for; matrix products, arithmetic and copies ran while one was open for 7% of the time, Pallas kernels for 18%

profile of v3, /device:TPU:0, one launch (start us, length us, event | category | flops | bytes accessed | tf_op | source)
XLA Modules:
  0.0 513.9 jit_solution(10639016657626050384)
XLA Ops:
  10.3 4.1 collective-permute-start
  16.1 14.0 %collective-permute-done = bf16[800,128]{1,0:T(8,128)(2,1)S(1)} collective-permute-done((bf16[800,128]{1,0:T(8,128)(2,1)S(1)}, bf16[800,128]{1,0:T(8,128)(2,1)S(1)}, u32[]{:S(2)}, u32[]{:S(2)}) %collective-permute-start) | collective-permute-done | bytes 204832 | tf_op jit(solution)/shard_map/ppermute | solution.py:86
  39.2 3.4 collective-permute-start.3
  48.7 6.6 %collective-permute-start.6 = (bf16[128,1280]{1,0:T(8,128)(2,1)}, bf16[128,1280]{1,0:T(8,128)(2,1)S(1)}, u32[]{:S(2)}, u32[]{:S(2)}) collective-permute-start(bf16[128,1280]{1,0:T(8,128)(2,1)} %gate.1), channel_id=1, source_target_pairs={{0,16},{4,20},{8,24},{12,28},{16,0},{20,4},{24,8},{28,12},{1,17},{... | collective-permute-start | bytes 983048 | tf_op jit(solution)/shard_map/ppermute | solution.py:86
  55.3 27.5 %collective-permute-done.6 = bf16[128,1280]{1,0:T(8,128)(2,1)S(1)} collective-permute-done((bf16[128,1280]{1,0:T(8,128)(2,1)}, bf16[128,1280]{1,0:T(8,128)(2,1)S(1)}, u32[]{:S(2)}, u32[]{:S(2)}) %collective-permute-start.6) | collective-permute-done | bytes 327712 | tf_op jit(solution)/shard_map/ppermute | solution.py:86
  91.4 3.8 collective-permute-start.9
  98.2 24.5 %collective-permute-done.9 = bf16[256,1280]{1,0:T(8,128)(2,1)S(1)} collective-permute-done((bf16[256,1280]{1,0:T(8,128)(2,1)S(1)}, bf16[256,1280]{1,0:T(8,128)(2,1)S(1)}, u32[]{:S(2)}, u32[]{:S(2)}) %collective-permute-start.9) | collective-permute-done | bytes 655392 | tf_op jit(solution)/shard_map/ppermute | solution.py:86
  135.0 3.7 slice.144
  154.9 13.3 %enter.1 = (bf16[416,1024]{1,0:T(8,128)(2,1)S(1)}, bf16[416,1024]{1,0:T(8,128)(2,1)S(1)}, f32[416,768]{1,0:T(8,128)S(1)}, bf16[416,768]{1,0:T(8,128)(2,1)S(1)}, ...) custom-call(bf16[416,256]{1,0:T(8,128)(2,1)S(1)} %bitcast.243, ...), custom_call_target="tpu_custom_call" | custom-call | flops 60000002048 | bytes 180000000 | tf_op jit(solution)/shard_map/enter/pallas_call | solution.py:330
  176.3 12.7 %middle.1 = (f32[416,768]{1,0:T(8,128)S(1)}, bf16[416,768]{1,0:T(8,128)(2,1)S(1)}, bf16[4,416,768]{2,1,0:T(8,128)(2,1)S(1)}, bf16[4,416,768]{2,1,0:T(8,128)(2,1)...) custom-call(bf16[4,416,192]{2,1,0:T(8,128)(2,1)S(1)} %copy-done.48, f32[416,768]{1,0:T(8,128)S(1)} %copy-done.75, ...), custom_call_target="tpu_custom_call" | custom-call | flops 77999996928 | bytes 234000000 | tf_op jit(solution)/shard_map/middle/pallas_call | solution.py:405
  195.0 12.1 %leave.1 = (f32[416,256]{1,0:T(8,128)S(1)}, bf16[416,256]{1,0:T(8,128)(2,1)S(1)}, bf16[416,2560]{1,0:T(8,128)(2,1)S(1)}, bf16[416,512]{1,0:T(8,128)(2,1)S(1)}, b...) custom-call(s32[1]{0:T(128)} %bitcast.core_ref.refs_0_, ...), custom_call_target="tpu_custom_call" | custom-call | flops 48000000000 | bytes 144000000 | tf_op jit(solution)/shard_map/leave/pallas_call | solution.py:510
  230.4 3.3 collective-permute-done.19
  240.4 5.6 %leave_back.1 = (bf16[416,2304]{1,0:T(8,128)(2,1)S(1)}, bf16[416,2560]{1,0:T(8,128)(2,1)S(1)}) custom-call(f32[2,19]{1,0:T(2,128)S(1)} %pad_maximum_fusion.5.coef_ref, f32[416,2304]{1,0:T(8,128)S(1)} %copy-done.38, s32[416,256]{1,0:T(8,128)S(1)} %bitcast.226, bf16[416,2560]{1,0:T(8,128)(2,1)S(1)} %copy-done.40, bf16[512,1152]{1,0:T(8,128)(2,1)S(1)} %copy-done.6, ...), custom_call_target="tpu_custom_call" | custom-call | flops 30000001024 | bytes 90000000 | tf_op jit(solution)/shard_map/leave_back/pallas_call | solution.py:583
  246.1 3.5 skip_grad.1
  251.4 3.2 collective-permute-done.20
  259.5 11.0 %middle_back.1 = (bf16[4,416,768]{2,1,0:T(8,128)(2,1)S(1)}, f32[416,768]{1,0:T(8,128)S(1)}, bf16[416,768]{1,0:T(8,128)(2,1)S(1)}, bf16[4,416,192]{2,1,0:T(8,128)(2,1)S(1)}, f32[16,768]{1,0:T(8,128)S(1)}) custom-call(bf16[416,768]{1,0:T(8,128)(2,1)S(1)} %get-tuple-element.128.refs_1_.refs_0_, bf16[4,768,1536]{2,1,0:T(8,128)(2,1)} %bitcast.272, ...), custom_call_target="tpu_custom_call" | custom-call | flops 62999998464 | bytes 189000000 | tf_op jit(solution)/shard_map/middle_back/pallas_call | solution.py:926
  274.4 12.5 %collective-permute-done.23 = bf16[512,1280]{1,0:T(8,128)(2,1)S(1)} collective-permute-done((bf16[512,1280]{1,0:T(8,128)(2,1)S(1)}, bf16[512,1280]{1,0:T(8,128)(2,1)S(1)}, u32[]{:S(2)}, u32[]{:S(2)}) %collective-permute-start.23) | collective-permute-done | bytes 1310752 | tf_op jit(solution)/shard_map/ppermute | solution.py:86
  290.8 13.5 %attn_back.1.refs_3_.refs_1_ = bf16[4,416,576]{2,1,0:T(8,128)(2,1)S(1)} custom-call(bf16[4,416,576]{2,1,0:T(8,128)(2,1)S(1)} %copy-done.61, bf16[4,416,192]{2,1,0:T(8,128)(2,1)S(1)} %copy-done.67, bf16[768,1536]{1,0:T(8,128)(2,1)S(1)} %get-tuple-element.147.refs_2_), custom_call_target="tpu_custom_call" | custom-call | flops 44999999488 | bytes 135000000 | tf_op jit(solution)/shard_map/attn_back/pallas_call | solution.py:994
  306.5 3.6 attn_grad.1
  314.4 3.0 decoder_grad.1.refs_3_.refs_9_
  324.8 10.3 %enter_back.1 = (bf16[416,768]{1,0:T(8,128)(2,1)S(1)}, bf16[416,1024]{1,0:T(8,128)(2,1)S(1)}, f32[208,768]{1,0:T(8,128)S(1)}, f32[16,768]{1,0:T(8,128)S(1)}) custom-call(s32[1]{0:T(128)} %bitcast.core_ref.refs_0_, bf16[4,416,576]{2,1,0:T(8,128)(2,1)S(1)} %attn_back.1.refs_3_.refs_1_, bf16[768,1536]{1,0:T(8,128)(2,1)} %gather_step.18.own_ref.refs_6_.refs_2_, ...), custom_call_target="tpu_custom_call" | custom-call | flops 62999998464 | bytes 189000000 | tf_op jit(solution)/shard_map/enter_back/pallas_call | solution.py:1069
  335.1 4.3 collective-permute-done.27
  339.9 24.0 %collective-permute-done.31 = bf16[768,768]{1,0:T(8,128)(2,1)S(1)} collective-permute-done((bf16[768,768]{1,0:T(8,128)(2,1)S(1)}, bf16[768,768]{1,0:T(8,128)(2,1)S(1)}, u32[]{:S(2)}, u32[]{:S(2)}) %collective-permute-start.31) | collective-permute-done | bytes 1179680 | tf_op jit(solution)/shard_map/ppermute | solution.py:86
  367.1 3.1 collective-permute-done.32
  374.7 16.8 %collective-permute-done.40 = bf16[128,1280]{1,0:T(8,128)(2,1)S(1)} collective-permute-done((bf16[128,1280]{1,0:T(8,128)(2,1)S(1)}, bf16[128,1280]{1,0:T(8,128)(2,1)S(1)}, u32[]{:S(2)}, u32[]{:S(2)}) %collective-permute-start.40) | collective-permute-done | bytes 327712 | tf_op jit(solution)/shard_map/ppermute | solution.py:86
  393.1 11.3 %collective-permute-done.30 = bf16[384,768]{1,0:T(8,128)(2,1)S(1)} collective-permute-done((bf16[384,768]{1,0:T(8,128)(2,1)S(1)}, bf16[384,768]{1,0:T(8,128)(2,1)S(1)}, u32[]{:S(2)}, u32[]{:S(2)}) %collective-permute-start.30) | collective-permute-done | bytes 589856 | tf_op jit(solution)/shard_map/ppermute | solution.py:86
  406.2 10.1 %collective-permute-done.36 = bf16[384,768]{1,0:T(8,128)(2,1)S(1)} collective-permute-done((bf16[384,768]{1,0:T(8,128)(2,1)S(1)}, bf16[384,768]{1,0:T(8,128)(2,1)S(1)}, u32[]{:S(2)}, u32[]{:S(2)}) %collective-permute-start.36) | collective-permute-done | bytes 589856 | tf_op jit(solution)/shard_map/ppermute | solution.py:86
  420.0 6.4 %collective-permute-done.38 = bf16[192,768]{1,0:T(8,128)(2,1)S(1)} collective-permute-done((bf16[192,768]{1,0:T(8,128)(2,1)S(1)}, bf16[192,768]{1,0:T(8,128)(2,1)S(1)}, u32[]{:S(2)}, u32[]{:S(2)}) %collective-permute-start.38) | collective-permute-done | bytes 294944 | tf_op jit(solution)/shard_map/ppermute | solution.py:86
  426.5 7.0 %collective-permute-done.42 = bf16[1600,128]{1,0:T(8,128)(2,1)S(1)} collective-permute-done((bf16[1600,128]{1,0:T(8,128)(2,1)S(1)}, bf16[1600,128]{1,0:T(8,128)(2,1)S(1)}, u32[]{:S(2)}, u32[]{:S(2)}) %collective-permute-start.42) | collective-permute-done | bytes 409632 | tf_op jit(solution)/shard_map/ppermute | solution.py:86
  435.4 8.9 %collective-permute-done.43 = bf16[800,128]{1,0:T(8,128)(2,1)S(1)} collective-permute-done((bf16[800,128]{1,0:T(8,128)(2,1)S(1)}, bf16[800,128]{1,0:T(8,128)(2,1)S(1)}, u32[]{:S(2)}, u32[]{:S(2)}) %collective-permute-start.43) | collective-permute-done | bytes 204832 | tf_op jit(solution)/shard_map/ppermute | solution.py:86
  454.6 8.9 %collective-permute-done.37 = bf16[96,768]{1,0:T(8,128)(2,1)S(1)} collective-permute-done((bf16[96,768]{1,0:T(8,128)(2,1)S(1)}, bf16[96,768]{1,0:T(8,128)(2,1)S(1)}, u32[]{:S(2)}, u32[]{:S(2)}) %collective-permute-start.37) | collective-permute-done | bytes 147488 | tf_op jit(solution)/shard_map/ppermute | solution.py:86
  483.5 3.2 collective-permute-done.51
  (478 shorter events, 189.3 us)
Async XLA Ops:
  7.3 165.4 %all-gather.2.cloned.1.call-start = ((), (), s32[]{:S(2)}) async-start(), calls=%async_computation | async-start | bytes 9732096 | tf_op jit(solution)/shard_map/all_gather | solution.py:1224
  10.3 19.7 %collective-permute-start = (bf16[800,128]{1,0:T(8,128)(2,1)S(1)}, bf16[800,128]{1,0:T(8,128)(2,1)S(1)}, u32[]{:S(2)}, u32[]{:S(2)}) collective-permute-start(bf16[800,128]{1,0:T(8,128)(2,1)S(1)} %pack.1), channel_id=1, source_target_pairs={{0,16},{4,20},{8,24},{12,28},{16,0},{20,4},{24,8},{28,12},{1,17},{... | collective-permute-start | bytes 614408 | tf_op jit(solution)/shard_map/ppermute | solution.py:86
  15.3 19.4 %collective-permute-start.2 = (bf16[96,768]{1,0:T(8,128)(2,1)S(1)}, bf16[96,768]{1,0:T(8,128)(2,1)S(1)}, u32[]{:S(2)}, u32[]{:S(2)}) collective-permute-start(bf16[96,768]{1,0:T(8,128)(2,1)S(1)} %pad_maximum_fusion.3), channel_id=1, source_target_pairs={{0,16},{4,20},{8,24},{12,28},{16,0},{20,4},{24,8},{28,12},{1,17},{... | collective-permute-start | bytes 442376 | tf_op jit(solution)/shard_map/ppermute | solution.py:86
  39.2 49.4 %collective-permute-start.3 = (bf16[3200,128]{1,0:T(8,128)(2,1)}, bf16[3200,128]{1,0:T(8,128)(2,1)}, u32[]{:S(2)}, u32[]{:S(2)}) collective-permute-start(bf16[3200,128]{1,0:T(8,128)(2,1)} %bitcast.18.refs_3_), channel_id=1, source_target_pairs={{0,8},{4,12},{8,0},{12,4},{16,24},{20,28},{24,16},{28,20},{1,9},{5... | collective-permute-start | bytes 2457608 | tf_op jit(solution)/shard_map/ppermute | solution.py:86
  45.1 38.8 %collective-permute-start.5 = (bf16[384,768]{1,0:T(8,128)(2,1)S(1)}, bf16[384,768]{1,0:T(8,128)(2,1)S(1)}, u32[]{:S(2)}, u32[]{:S(2)}) collective-permute-start(bf16[384,768]{1,0:T(8,128)(2,1)S(1)} %bitcast.180), channel_id=1, source_target_pairs={{0,4},{4,0},{8,12},{12,8},{16,20},{20,16},{24,28},{28,24},{1,5},{5... | collective-permute-start | bytes 1769480 | tf_op jit(solution)/shard_map/ppermute | solution.py:86
  48.7 34.1 %collective-permute-start.6 = (bf16[128,1280]{1,0:T(8,128)(2,1)}, bf16[128,1280]{1,0:T(8,128)(2,1)S(1)}, u32[]{:S(2)}, u32[]{:S(2)}) collective-permute-start(bf16[128,1280]{1,0:T(8,128)(2,1)} %gate.1), channel_id=1, source_target_pairs={{0,16},{4,20},{8,24},{12,28},{16,0},{20,4},{24,8},{28,12},{1,17},{... | collective-permute-start | bytes 983048 | tf_op jit(solution)/shard_map/ppermute | solution.py:86
  86.9 37.1 %collective-permute-start.8 = (bf16[768,768]{1,0:T(8,128)(2,1)S(1)}, bf16[768,768]{1,0:T(8,128)(2,1)}, u32[]{:S(2)}, u32[]{:S(2)}) collective-permute-start(bf16[768,768]{1,0:T(8,128)(2,1)S(1)} %bitcast.174), channel_id=1, source_target_pairs={{0,2},{1,3},{2,0},{3,1},{4,6},{5,7},{6,4},{7,5},{8,10},{9,11},{10,... | collective-permute-start | bytes 3538952 | tf_op jit(solution)/shard_map/ppermute | solution.py:86
  91.4 37.9 %collective-permute-start.7 = (bf16[6400,128]{1,0:T(8,128)(2,1)}, bf16[6400,128]{1,0:T(8,128)(2,1)}, u32[]{:S(2)}, u32[]{:S(2)}) collective-permute-start(bf16[6400,128]{1,0:T(8,128)(2,1)} %bitcast.30.refs_3_), channel_id=1, source_target_pairs={{0,1},{1,0},{2,3},{3,2},{4,5},{5,4},{6,7},{7,6},{8,9},{9,8},{10,11... | collective-permute-start | bytes 4915208 | tf_op jit(solution)/shard_map/ppermute | solution.py:86
  91.4 31.2 %collective-permute-start.9 = (bf16[256,1280]{1,0:T(8,128)(2,1)S(1)}, bf16[256,1280]{1,0:T(8,128)(2,1)S(1)}, u32[]{:S(2)}, u32[]{:S(2)}) collective-permute-start(bf16[256,1280]{1,0:T(8,128)(2,1)S(1)} %bitcast.178), channel_id=1, source_target_pairs={{0,8},{4,12},{8,0},{12,4},{16,24},{20,28},{24,16},{28,20},{1,9},{5... | collective-permute-start | bytes 1966088 | tf_op jit(solution)/shard_map/ppermute | solution.py:86
  126.9 28.0 %collective-permute-start.10 = (bf16[768,1536]{1,0:T(8,128)(2,1)}, bf16[768,1536]{1,0:T(8,128)(2,1)}, u32[]{:S(2)}, u32[]{:S(2)}) collective-permute-start(bf16[768,1536]{1,0:T(8,128)(2,1)} %gather_step.18.own_ref.refs_6_.refs_2_), channel_id=1, source_target_pairs={{0,1},{1,0},{2,3},{3,2},{4,5},{5,4},{6,7},{7,6},{8,9},{9,8},{10,11... | collective-permute-start | bytes 7077896 | tf_op jit(solution)/shard_map/ppermute | solution.py:86
  127.9 41.3 %collective-permute-start.11 = (bf16[512,1280]{1,0:T(8,128)(2,1)S(1)}, bf16[512,1280]{1,0:T(8,128)(2,1)S(1)}, u32[]{:S(2)}, u32[]{:S(2)}) collective-permute-start(bf16[512,1280]{1,0:T(8,128)(2,1)S(1)} %bitcast.172), channel_id=1, source_target_pairs={{0,4},{4,0},{8,12},{12,8},{16,20},{20,16},{24,28},{28,24},{1,5},{5... | collective-permute-start | bytes 3932168 | tf_op jit(solution)/shard_map/ppermute | solution.py:86
  172.4 22.5 %collective-permute-start.12 = (bf16[1024,1280]{1,0:T(8,128)(2,1)}, bf16[1024,1280]{1,0:T(8,128)(2,1)}, u32[]{:S(2)}, u32[]{:S(2)}) collective-permute-start(bf16[1024,1280]{1,0:T(8,128)(2,1)} %bitcast.40.skip_own_ref.refs_9_), channel_id=1, source_target_pairs={{0,1},{1,0},{2,3},{3,2},{4,5},{5,4},{6,7},{7,6},{8,9},{9,8},{10,11... | collective-permute-start | bytes 7864328 | tf_op jit(solution)/shard_map/ppermute | solution.py:86
  255.2 31.7 %collective-permute-start.23 = (bf16[512,1280]{1,0:T(8,128)(2,1)S(1)}, bf16[512,1280]{1,0:T(8,128)(2,1)S(1)}, u32[]{:S(2)}, u32[]{:S(2)}) collective-permute-start(bf16[512,1280]{1,0:T(8,128)(2,1)S(1)} %bitcast.248), channel_id=1, source_target_pairs={{0,4},{4,0},{8,12},{12,8},{16,20},{20,16},{24,28},{28,24},{1,5},{5... | collective-permute-start | bytes 3932168 | tf_op jit(solution)/shard_map/ppermute | solution.py:86
  259.4 12.9 %collective-permute-start.21 = (bf16[768,1536]{1,0:T(8,128)(2,1)S(1)}, bf16[768,1536]{1,0:T(8,128)(2,1)S(1)}, u32[]{:S(2)}, u32[]{:S(2)}) collective-permute-start(bf16[768,1536]{1,0:T(8,128)(2,1)S(1)} %get-tuple-element.134.refs_8_), channel_id=1, source_target_pairs={{0,1},{1,0},{2,3},{3,2},{4,5},{5,4},{6,7},{7,6},{8,9},{9,8},{10,11... | collective-permute-start | bytes 7077896 | tf_op jit(solution)/shard_map/ppermute | solution.py:86
  273.3 38.7 %collective-permute-start.22 = (bf16[384,1536]{1,0:T(8,128)(2,1)S(1)}, bf16[384,1536]{1,0:T(8,128)(2,1)S(1)}, u32[]{:S(2)}, u32[]{:S(2)}) collective-permute-start(bf16[384,1536]{1,0:T(8,128)(2,1)S(1)} %bitcast.209), channel_id=1, source_target_pairs={{0,4},{4,0},{8,12},{12,8},{16,20},{20,16},{24,28},{28,24},{1,5},{5... | collective-permute-start | bytes 3538952 | tf_op jit(solution)/shard_map/ppermute | solution.py:86
  287.4 17.5 %collective-permute-start.24 = (bf16[256,1280]{1,0:T(8,128)(2,1)S(1)}, bf16[256,1280]{1,0:T(8,128)(2,1)S(1)}, u32[]{:S(2)}, u32[]{:S(2)}) collective-permute-start(bf16[256,1280]{1,0:T(8,128)(2,1)S(1)} %bitcast.250), channel_id=1, source_target_pairs={{0,8},{4,12},{8,0},{12,4},{16,24},{20,28},{24,16},{28,20},{1,9},{5... | collective-permute-start | bytes 1966088 | tf_op jit(solution)/shard_map/ppermute | solution.py:86
  290.7 13.6 %collective-permute-start.25 = (bf16[768,1536]{1,0:T(8,128)(2,1)S(1)}, bf16[768,1536]{1,0:T(8,128)(2,1)S(1)}, u32[]{:S(2)}, u32[]{:S(2)}) collective-permute-start(bf16[768,1536]{1,0:T(8,128)(2,1)S(1)} %get-tuple-element.147.refs_2_), channel_id=1, source_target_pairs={{0,1},{1,0},{2,3},{3,2},{4,5},{5,4},{6,7},{7,6},{8,9},{9,8},{10,11... | collective-permute-start | bytes 7077896 | tf_op jit(solution)/shard_map/ppermute | solution.py:86
  310.6 28.8 %collective-permute-start.27 = (bf16[768,768]{1,0:T(8,128)(2,1)S(1)}, bf16[768,768]{1,0:T(8,128)(2,1)S(1)}, u32[]{:S(2)}, u32[]{:S(2)}) collective-permute-start(bf16[768,768]{1,0:T(8,128)(2,1)S(1)} %get-tuple-element.151.refs_3_), channel_id=1, source_target_pairs={{0,2},{1,3},{2,0},{3,1},{4,6},{5,7},{6,4},{7,5},{8,10},{9,11},{10,... | collective-permute-start | bytes 3538952 | tf_op jit(solution)/shard_map/ppermute | solution.py:86
  312.4 27.3 %collective-permute-start.26 = (bf16[192,1536]{1,0:T(8,128)(2,1)S(1)}, bf16[192,1536]{1,0:T(8,128)(2,1)S(1)}, u32[]{:S(2)}, u32[]{:S(2)}) collective-permute-start(bf16[192,1536]{1,0:T(8,128)(2,1)S(1)} %bitcast.254), channel_id=1, source_target_pairs={{0,8},{4,12},{8,0},{12,4},{16,24},{20,28},{24,16},{28,20},{1,9},{5... | collective-permute-start | bytes 1769480 | tf_op jit(solution)/shard_map/ppermute | solution.py:86
  318.3 45.5 %collective-permute-start.31 = (bf16[768,768]{1,0:T(8,128)(2,1)S(1)}, bf16[768,768]{1,0:T(8,128)(2,1)S(1)}, u32[]{:S(2)}, u32[]{:S(2)}) collective-permute-start(bf16[768,768]{1,0:T(8,128)(2,1)S(1)} %get-tuple-element.165.refs_12_), channel_id=1, source_target_pairs={{0,2},{1,3},{2,0},{3,1},{4,6},{5,7},{6,4},{7,5},{8,10},{9,11},{10,... | collective-permute-start | bytes 3538952 | tf_op jit(solution)/shard_map/ppermute | solution.py:86
  366.7 24.8 %collective-permute-start.40 = (bf16[128,1280]{1,0:T(8,128)(2,1)S(1)}, bf16[128,1280]{1,0:T(8,128)(2,1)S(1)}, u32[]{:S(2)}, u32[]{:S(2)}) collective-permute-start(bf16[128,1280]{1,0:T(8,128)(2,1)S(1)} %bitcast.258), channel_id=1, source_target_pairs={{0,16},{4,20},{8,24},{12,28},{16,0},{20,4},{24,8},{28,12},{1,17},{... | collective-permute-start | bytes 983048 | tf_op jit(solution)/shard_map/ppermute | solution.py:86
  370.6 47.3 %collective-permute-start.35 = (bf16[3200,128]{1,0:T(8,128)(2,1)S(1)}, bf16[3200,128]{1,0:T(8,128)(2,1)S(1)}, u32[]{:S(2)}, u32[]{:S(2)}) collective-permute-start(bf16[3200,128]{1,0:T(8,128)(2,1)S(1)} %bitcast.211), channel_id=1, source_target_pairs={{0,4},{4,0},{8,12},{12,8},{16,20},{20,16},{24,28},{28,24},{1,5},{5... | collective-permute-start | bytes 2457608 | tf_op jit(solution)/shard_map/ppermute | solution.py:86
  372.2 32.2 %collective-permute-start.30 = (bf16[384,768]{1,0:T(8,128)(2,1)S(1)}, bf16[384,768]{1,0:T(8,128)(2,1)S(1)}, u32[]{:S(2)}, u32[]{:S(2)}) collective-permute-start(bf16[384,768]{1,0:T(8,128)(2,1)S(1)} %bitcast.218), channel_id=1, source_target_pairs={{0,4},{4,0},{8,12},{12,8},{16,20},{20,16},{24,28},{28,24},{1,5},{5... | collective-permute-start | bytes 1769480 | tf_op jit(solution)/shard_map/ppermute | solution.py:86
  372.7 33.4 %collective-permute-start.29 = (bf16[96,1536]{1,0:T(8,128)(2,1)S(1)}, bf16[96,1536]{1,0:T(8,128)(2,1)S(1)}, u32[]{:S(2)}, u32[]{:S(2)}) collective-permute-start(bf16[96,1536]{1,0:T(8,128)(2,1)S(1)} %bitcast.238), channel_id=1, source_target_pairs={{0,16},{4,20},{8,24},{12,28},{16,0},{20,4},{24,8},{28,12},{1,17},{... | collective-permute-start | bytes 884744 | tf_op jit(solution)/shard_map/ppermute | solution.py:86
  373.0 43.3 %collective-permute-start.36 = (bf16[384,768]{1,0:T(8,128)(2,1)S(1)}, bf16[384,768]{1,0:T(8,128)(2,1)S(1)}, u32[]{:S(2)}, u32[]{:S(2)}) collective-permute-start(bf16[384,768]{1,0:T(8,128)(2,1)S(1)} %bitcast.253), channel_id=1, source_target_pairs={{0,4},{4,0},{8,12},{12,8},{16,20},{20,16},{24,28},{28,24},{1,5},{5... | collective-permute-start | bytes 1769480 | tf_op jit(solution)/shard_map/ppermute | solution.py:86
  391.6 27.4 %collective-permute-start.41 = (bf16[128,1280]{1,0:T(8,128)(2,1)S(1)}, bf16[128,1280]{1,0:T(8,128)(2,1)S(1)}, u32[]{:S(2)}, u32[]{:S(2)}) collective-permute-start(bf16[128,1280]{1,0:T(8,128)(2,1)S(1)} %fusion.5), channel_id=1, source_target_pairs={{0,2},{1,3},{2,0},{3,1},{4,6},{5,7},{6,4},{7,5},{8,10},{9,11},{10,... | collective-permute-start | bytes 983048 | tf_op jit(solution)/shard_map/ppermute | solution.py:86
  404.6 15.3 %collective-permute-start.34 = (bf16[192,768]{1,0:T(8,128)(2,1)S(1)}, bf16[192,768]{1,0:T(8,128)(2,1)S(1)}, u32[]{:S(2)}, u32[]{:S(2)}) collective-permute-start(bf16[192,768]{1,0:T(8,128)(2,1)S(1)} %bitcast.240), channel_id=1, source_target_pairs={{0,8},{4,12},{8,0},{12,4},{16,24},{20,28},{24,16},{28,20},{1,9},{5... | collective-permute-start | bytes 884744 | tf_op jit(solution)/shard_map/ppermute | solution.py:86
  418.4 15.1 %collective-permute-start.42 = (bf16[1600,128]{1,0:T(8,128)(2,1)S(1)}, bf16[1600,128]{1,0:T(8,128)(2,1)S(1)}, u32[]{:S(2)}, u32[]{:S(2)}) collective-permute-start(bf16[1600,128]{1,0:T(8,128)(2,1)S(1)} %bitcast.228), channel_id=1, source_target_pairs={{0,8},{4,12},{8,0},{12,4},{16,24},{20,28},{24,16},{28,20},{1,9},{5... | collective-permute-start | bytes 1228808 | tf_op jit(solution)/shard_map/ppermute | solution.py:86
  419.9 26.0 %collective-permute-start.53 = (f32[128,1280]{1,0:T(8,128)}, f32[128,1280]{1,0:T(8,128)}, u32[]{:S(2)}, u32[]{:S(2)}) collective-permute-start(f32[128,1280]{1,0:T(8,128)} %convert_add_fusion), channel_id=1, source_target_pairs={{0,1},{1,0},{2,3},{3,2},{4,5},{5,4},{6,7},{7,6},{8,9},{9,8},{10,11... | collective-permute-start | bytes 1966088 | tf_op jit(solution)/shard_map/ppermute | solution.py:86
  449.3 16.1 %collective-permute-start.39 = (bf16[96,768]{1,0:T(8,128)(2,1)S(1)}, bf16[96,768]{1,0:T(8,128)(2,1)S(1)}, u32[]{:S(2)}, u32[]{:S(2)}) collective-permute-start(bf16[96,768]{1,0:T(8,128)(2,1)S(1)} %bitcast.247), channel_id=1, source_target_pairs={{0,16},{4,20},{8,24},{12,28},{16,0},{20,4},{24,8},{28,12},{1,17},{... | collective-permute-start | bytes 442376 | tf_op jit(solution)/shard_map/ppermute | solution.py:86
  449.3 14.1 %collective-permute-start.37 = (bf16[96,768]{1,0:T(8,128)(2,1)S(1)}, bf16[96,768]{1,0:T(8,128)(2,1)S(1)}, u32[]{:S(2)}, u32[]{:S(2)}) collective-permute-start(bf16[96,768]{1,0:T(8,128)(2,1)S(1)} %bitcast.264), channel_id=1, source_target_pairs={{0,16},{4,20},{8,24},{12,28},{16,0},{20,4},{24,8},{28,12},{1,17},{... | collective-permute-start | bytes 442376 | tf_op jit(solution)/shard_map/ppermute | solution.py:86
  452.3 16.0 %collective-permute-start.52 = (f32[800,128]{1,0:T(8,128)S(1)}, f32[800,128]{1,0:T(8,128)S(1)}, u32[]{:S(2)}, u32[]{:S(2)}) collective-permute-start(f32[800,128]{1,0:T(8,128)S(1)} %convert_add_fusion.1), channel_id=1, source_target_pairs={{0,1},{1,0},{2,3},{3,2},{4,5},{5,4},{6,7},{7,6},{8,9},{9,8},{10,11... | collective-permute-start | bytes 1228808 | tf_op jit(solution)/shard_map/ppermute | solution.py:86
  (141 other events, 792.1 us)
Sparse Core Ops, SparseCore 0:
  11.6 113.1 all-gather.1

commit v4 on v3

--- a/solution.py
+++ b/solution.py
@@ -64,7 +64,7 @@
 
 def cost(micros):
     return pl.CostEstimate(
-        flops=int(micros * 3e9), bytes_accessed=int(micros * 9e6), transcendentals=0
+        flops=int(micros * 2e9), bytes_accessed=int(micros * 6e6), transcendentals=0
     )
 
 
@@ -340,7 +340,7 @@
             jax.ShapeDtypeStruct((parts, rows, width // 3), bf16),
         ],
         compiler_params=params(),
-        cost_estimate=cost(20),
+        cost_estimate=cost(13),
         name="enter",
     )(pixels, stem_b, embed_b, tokens, *attn_all)
 
@@ -409,7 +409,7 @@
         out_specs=[(part_of if len(out.shape) == 3 else whole_of)(out) for out in outs],
         out_shape=outs,
         compiler_params=params(),
-        cost_estimate=cost(26),
+        cost_estimate=cost(13),
         name="middle",
     )(*values, mlp_all)
 
@@ -523,7 +523,7 @@
         ],
         scratch_shapes=[pltpu.VMEM((rows, SKIPW), f32)],
         compiler_params=params(),
-        cost_estimate=cost(16),
+        cost_estimate=cost(12),
         name="leave",
     )(core, hidden, final_low, *skip_all, dec_b, one_b, two_b, three_four, big_head, labels)
 
@@ -589,7 +589,7 @@
             jax.ShapeDtypeStruct((rows, SKIPW), bf16),
         ],
         compiler_params=params(),
-        cost_estimate=cost(10),
+        cost_estimate=cost(6),
         name="leave_back",
     )(coef, logits, labels, slope, big_head, three_four, two_b)
 
@@ -613,7 +613,7 @@
         out_specs=[FULL] * 2,
         out_shape=[jax.ShapeDtypeStruct(shape, bf16)] * 2,
         compiler_params=params(),
-        cost_estimate=cost(6),
+        cost_estimate=cost(3.5),
         name="skip_grad",
     )(core, hidden, g_skips)
 
@@ -645,7 +645,7 @@
         ],
         scratch_shapes=[pltpu.VMEM((rows, D), f32)],
         compiler_params=params(),
-        cost_estimate=cost(11),
+        cost_estimate=cost(3),
         name="turn",
     )(g_skips, one_b, slope0, dec_b, resid2, tokens, *after)
 
@@ -753,7 +753,7 @@
         out_shape=jax.ShapeDtypeStruct((2, size, rows, LANES), bf16),
         scratch_shapes=[pltpu.VMEM((lines, LANES), f32), pltpu.VMEM((CHAN_C, 4 * CHAN_D), f32)],
         compiler_params=params(),
-        cost_estimate=cost(7),
+        cost_estimate=cost(3),
         name="decoder_grad",
     )(level3, g_logits, level2, level1, g_skips, level0, final_low, g_pre0, *after)
 
@@ -810,7 +810,7 @@
         out_shape=[jax.ShapeDtypeStruct(shape, bf16)] * 2,
         scratch_shapes=[pltpu.VMEM((2 * LANES, D), f32)],
         compiler_params=params(),
-        cost_estimate=cost(6),
+        cost_estimate=cost(2),
         name="first_grad",
     )(core, pixels, g_stem, hidden, low, pos, sums1, sums2, sumsf, dec, *after)
 
@@ -848,7 +848,7 @@
         ],
         scratch_shapes=[pltpu.VMEM((D, 2 * LANES), f32)],
         compiler_params=params(),
-        cost_estimate=cost(4),
+        cost_estimate=cost(3),
         name="unpack",
     )(core, own, other)
 
@@ -933,7 +933,7 @@
         out_shape=outs,
         scratch_shapes=[pltpu.VMEM((rows, D), f32)],
         compiler_params=params(),
-        cost_estimate=cost(21),
+        cost_estimate=cost(11),
         name="middle_back",
     )(low2, mlp_all, slope, *values, *after)
 
@@ -957,7 +957,7 @@
         out_specs=[FULL] * 2,
         out_shape=[jax.ShapeDtypeStruct(shape, bf16)] * 2,
         compiler_params=params(),
-        cost_estimate=cost(6),
+        cost_estimate=cost(2.7),
         name="half_grad",
     )(core, left, right, *after)
 
@@ -998,7 +998,7 @@
         out_specs=whole(width),
         out_shape=jax.ShapeDtypeStruct(triple.shape, bf16),
         compiler_params=params(),
-        cost_estimate=cost(15),
+        cost_estimate=cost(13.5),
         name="attn_back",
     )(triple, g_ctx, *after)
 
@@ -1027,7 +1027,7 @@
         out_specs=[FULL] * 2,
         out_shape=[jax.ShapeDtypeStruct(shape, bf16)] * 2,
         compiler_params=params(),
-        cost_estimate=cost(7),
+        cost_estimate=cost(3.6),
         name="attn_grad",
     )(normed, g_tri, low, context, *after)
 
@@ -1078,7 +1078,7 @@
         ],
         scratch_shapes=[pltpu.VMEM((rows, D), f32), pltpu.VMEM((rows, D), f32)],
         compiler_params=params(),
-        cost_estimate=cost(21),
+        cost_estimate=cost(10.4),
         name="enter_back",
     )(core, g_tri, *attn_all, embed, tokens, g_resid, embed_b, g_skips, *skip_all, slope, *after)
 
@@ -1349,38 +1349,37 @@
         grad_skips, one_b, slope0, dec_b, resid2, table, after=(skip_send,)
     )
     low_bits = list(range(log_two(n_dp)))
+    bit_y, bit_one, bit_two = low_bits[:3]
     skip_part = core_pair(skip_send, skip_keep)
-    token = skip_part.step("dp", low_bits[0], bf16, after=(grad_pre0,))
+    token = skip_part.step("dp", bit_y, bf16, after=(grad_pre0,))
     down_send, down_keep = half_grad(core_id, grad_resid2_low, inner, after=(token,))
     grad_pre, grad_resid, grad_resid_low, grad_context, sums_2 = middle_back(
         grad_resid2_low, mlp_all, slope_mlp, resid, table, grad_resid2, attn_all,
         after=(down_send,),
     )
     down = core_pair(down_send, down_keep)
-    token = down.step("dp", low_bits[0], bf16, after=(grad_pre,))
-    token = skip_part.step("dp", low_bits[1], after=(token,))
+    token = down.step("dp", bit_y, bf16, after=(grad_pre,))
     in_send, in_keep = half_grad(core_id, normed2, grad_pre, after=(token,))
     grad_triple = attn_back(triple, grad_context, after=(in_send,))
     into = core_pair(in_send, in_keep)
     token = into.step("mp", 1, bf16, after=(grad_triple,))
-    token = skip_part.step("dp", low_bits[2], after=(token,))
+    token = skip_part.step("dp", bit_one, after=(token,))
     attn_send, attn_keep = attn_grad(
         normed, grad_triple, grad_resid_low, context, after=(token,)
     )
-    token = down.step("dp", low_bits[1], after=(attn_send,))
     decoder_halves = decoder_grad(
         level3, grad_logits, level2, level1, grad_skips, level0, final_low, grad_pre0,
-        n_dp, shared.flat_rows, after=(token,),
-    )
-    attn = core_pair(attn_send, attn_keep)
-    token = attn.step("mp", 1, bf16, after=(decoder_halves,))
+        n_dp, shared.flat_rows, after=(attn_send,),
+    )
     grad_embed_low, grad_pre_stem, grad_pos, sums_1 = enter_back(
         core_id, grad_triple, attn_all, embed, table, grad_resid, embed_b, grad_skips, skip_all,
-        slope_stem, after=(token,),
-    )
-    token = into.step("dp", low_bits[0], after=(grad_embed_low,))
-    token = down.step("dp", low_bits[2], after=(token,))
-    token = attn.step("dp", low_bits[0], after=(token,))
+        slope_stem, after=(decoder_halves,),
+    )
+    attn = core_pair(attn_send, attn_keep)
+    token = attn.step("mp", 1, bf16, after=(grad_embed_low,))
+    token = down.step("dp", bit_one, after=(token,))
+    token = skip_part.step("dp", bit_two, after=(token,))
+    token = into.step("dp", bit_y, after=(token,))
     if aligned:
         first_send, first_keep = first_grad(
             core_id, pixels, grad_pre_stem, hidden, grad_embed_low, grad_pos, sums_1, sums_2,
@@ -1407,20 +1406,26 @@
         first_send, first_keep = first_half(1 - core), first_half(core)
     wide = lambda value: value.reshape(-1, LANES)
     first = core_pair(wide(first_send), wide(first_keep))
-    token = first.step("dp", low_bits[0], after=(first_send,))
-    token = into.step("dp", low_bits[1], after=(token,))
+    token = first_send
+    token = first.step("dp", bit_y, after=(token,))
+    token = down.step("dp", bit_two, after=(token,))
+    token = into.step("dp", bit_one, after=(token,))
+    for bit in low_bits[3:]:
+        skip_part.step("dp", bit)
+    skip_half = run_gate(skip_part.total(), token)
+    skip_half = x_sum(skip_half)
+    token = attn.step("dp", bit_y, after=(token,))
+    token = into.step("dp", bit_two, after=(token,))
     token = down.step("mp", 1, after=(token,))
-    token = attn.step("dp", low_bits[1], after=(token,))
-    token = first.step("dp", low_bits[1], after=(token,))
-    token = into.step("dp", low_bits[2], after=(token,))
-    token = attn.step("dp", low_bits[2], after=(token,))
-    token = first.step("dp", low_bits[2], after=(token,))
+    token = first.step("dp", bit_one, after=(token,))
+    token = attn.step("dp", bit_one, after=(token,))
+    token = first.step("dp", bit_two, after=(token,))
+    token = attn.step("dp", bit_two, after=(token,))
     for bit in low_bits[3:]:
-        for part in (skip_part, down, into, first, attn):
+        for part in (down, into, first, attn):
             part.step("dp", bit)
     down_own, in_own, attn_own = down.total(), into.total(), attn.total()
     first_half_sum = x_sum(first.total())
-    skip_half = x_sum(skip_part.total())
 
     square = lambda value: jnp.sum(value * value)
     n_copies = n_mp // 2

time: 521 us -> 472 us (0.906)
  waiting for transfers between devices: 206 us -> 137 us
  Pallas kernels: 114 us -> 130 us
  starting transfers between devices: 67.2 us -> 58.5 us
  other arithmetic: 33 us -> 41 us
    ppermute x40, waiting for transfers between devices: 191 us -> 123 us  [swap(): return lax.ppermute(value, axis, [(i, i ^ 1 << bit) for i in range(size)])]
    pallas_call x18, Pallas kernels: 5.66 us -> 19.7 us  [step(): pl.pallas_call(kernel, grid=(steps,), in_specs=[SCALAR] + [block(shape)]...]
    ppermute x40, starting transfers between devices: 51 us -> 42.6 us  [swap(): return lax.ppermute(value, axis, [(i, i ^ 1 << bit) for i in range(size)])]
    unnamed x253 -> x301, local copies, waits for them, and re-layouts: 42.3 us -> 43.8 us
  transfers between devices with their start and end apart: 55 -> 55, of which waited for: 32 -> 27; matrix products, arithmetic and copies ran while one was open for 7% -> 11% of each run, Pallas kernels for 18% -> 22%
where the time goes in v4:
time: 472 us; the launch traced here: 465 us
  waiting for transfers between devices  137 us (29%)
  Pallas kernels  130 us (28%)
  local copies, waits for them, and re-layouts  71.5 us (15%)
  starting transfers between devices  58.5 us (12%)
  other arithmetic  41 us (9%)
  between operations  25.5 us (5%)
    ppermute x40, waiting for transfers between devices, swap(): return lax.ppermute(value, axis, [(i, i ^ 1 << bit) for i in range(size)])  123 us
    unnamed x301, local copies, waits for them, and re-layouts  43.8 us
    ppermute x40, starting transfers between devices, swap(): return lax.ppermute(value, axis, [(i, i ^ 1 << bit) for i in range(size)])  42.6 us
    pallas_call x18, Pallas kernels, step(): pl.pallas_call(kernel, grid=(steps,), in_specs=[SCALAR] + [block(shape)]...  19.7 us
    ppermute x14, starting transfers between devices, hop(): lax.ppermute(value, ('dp', 'mp'), [(i, i ^ move) for i in range(size)])  15.9 us
    ppermute x14, waiting for transfers between devices, hop(): lax.ppermute(value, ('dp', 'mp'), [(i, i ^ move) for i in range(size)])  13.6 us
    pallas_call x1, Pallas kernels, attn_back(): pl.pallas_call(kernel, grid=(parts,), in_specs=[whole(width), whole(width...  13.5 us
    pallas_call x1, Pallas kernels, enter(): pl.pallas_call(enter_kernel, in_specs=[FULL] * 6, out_specs=[FULL] * 6, o...  13.3 us
  transfers between devices with their start and end apart: 55, of which 27 were waited for; matrix products, arithmetic and copies ran while one was open for 11% of the time, Pallas kernels for 22%

profile of v4, /device:TPU:0, one launch (start us, length us, event | category | flops | bytes accessed | tf_op | source)
XLA Modules:
  0.0 464.9 jit_solution(1372224942359568734)
XLA Ops:
  10.3 4.1 collective-permute-start
  15.6 14.5 %collective-permute-done = bf16[800,128]{1,0:T(8,128)(2,1)S(1)} collective-permute-done((bf16[800,128]{1,0:T(8,128)(2,1)S(1)}, bf16[800,128]{1,0:T(8,128)(2,1)S(1)}, u32[]{:S(2)}, u32[]{:S(2)}) %collective-permute-start) | collective-permute-done | bytes 204832 | tf_op jit(solution)/shard_map/ppermute | solution.py:86
  39.2 5.4 %collective-permute-done.4 = bf16[192,768]{1,0:T(8,128)(2,1)S(1)} collective-permute-done((bf16[192,768]{1,0:T(8,128)(2,1)S(1)}, bf16[192,768]{1,0:T(8,128)(2,1)S(1)}, u32[]{:S(2)}, u32[]{:S(2)}) %collective-permute-start.4) | collective-permute-done | bytes 294944 | tf_op jit(solution)/shard_map/ppermute | solution.py:86
  47.9 6.2 %collective-permute-start.6 = (bf16[128,1280]{1,0:T(8,128)(2,1)}, bf16[128,1280]{1,0:T(8,128)(2,1)S(1)}, u32[]{:S(2)}, u32[]{:S(2)}) collective-permute-start(bf16[128,1280]{1,0:T(8,128)(2,1)} %gate.2), channel_id=1, source_target_pairs={{0,16},{4,20},{8,24},{12,28},{16,0},{20,4},{24,8},{28,12},{1,17},{... | collective-permute-start | bytes 983048 | tf_op jit(solution)/shard_map/ppermute | solution.py:86
  54.1 3.2 collective-permute-start.3
  57.4 16.4 %collective-permute-done.6 = bf16[128,1280]{1,0:T(8,128)(2,1)S(1)} collective-permute-done((bf16[128,1280]{1,0:T(8,128)(2,1)}, bf16[128,1280]{1,0:T(8,128)(2,1)S(1)}, u32[]{:S(2)}, u32[]{:S(2)}) %collective-permute-start.6) | collective-permute-done | bytes 327712 | tf_op jit(solution)/shard_map/ppermute | solution.py:86
  79.6 21.6 %collective-permute-done.3 = bf16[3200,128]{1,0:T(8,128)(2,1)S(1)} collective-permute-done((bf16[3200,128]{1,0:T(8,128)(2,1)}, bf16[3200,128]{1,0:T(8,128)(2,1)S(1)}, u32[]{:S(2)}, u32[]{:S(2)}) %collective-permute-start.3) | collective-permute-done | bytes 819232 | tf_op jit(solution)/shard_map/ppermute | solution.py:86
  106.5 17.1 %collective-permute-done.9 = bf16[256,1280]{1,0:T(8,128)(2,1)} collective-permute-done((bf16[256,1280]{1,0:T(8,128)(2,1)S(1)}, bf16[256,1280]{1,0:T(8,128)(2,1)}, u32[]{:S(2)}, u32[]{:S(2)}) %collective-permute-start.9) | collective-permute-done | bytes 655392 | tf_op jit(solution)/shard_map/ppermute | solution.py:86
  124.8 2.9 gather_step.18.own_ref.refs_6_.refs_2_
  135.4 2.9 reshape.457
  138.3 3.8 slice.144
  155.8 2.7 unpack.1
  158.6 13.3 %enter.1 = (bf16[416,1024]{1,0:T(8,128)(2,1)S(1)}, bf16[416,1024]{1,0:T(8,128)(2,1)S(1)}, f32[416,768]{1,0:T(8,128)S(1)}, bf16[416,768]{1,0:T(8,128)(2,1)S(1)}, ...) custom-call(bf16[416,256]{1,0:T(8,128)(2,1)S(1)} %bitcast.230, ...), custom_call_target="tpu_custom_call" | custom-call | flops 25999998976 | bytes 78000000 | tf_op jit(solution)/shard_map/enter/pallas_call | solution.py:330
  180.4 12.9 %middle.1 = (f32[416,768]{1,0:T(8,128)S(1)}, bf16[416,768]{1,0:T(8,128)(2,1)S(1)}, bf16[4,416,768]{2,1,0:T(8,128)(2,1)S(1)}, bf16[4,416,768]{2,1,0:T(8,128)(2,1)...) custom-call(bf16[4,416,192]{2,1,0:T(8,128)(2,1)S(1)} %copy-done.70, f32[416,768]{1,0:T(8,128)S(1)} %copy-done.81, ...), custom_call_target="tpu_custom_call" | custom-call | flops 25999998976 | bytes 78000000 | tf_op jit(solution)/shard_map/middle/pallas_call | solution.py:405
  199.3 12.1 %leave.1 = (f32[416,256]{1,0:T(8,128)S(1)}, bf16[416,256]{1,0:T(8,128)(2,1)S(1)}, bf16[416,2560]{1,0:T(8,128)(2,1)S(1)}, bf16[416,512]{1,0:T(8,128)(2,1)S(1)}, b...) custom-call(s32[1]{0:T(128)} %bitcast.core_ref.refs_0_, ...), custom_call_target="tpu_custom_call" | custom-call | flops 24000000000 | bytes 72000000 | tf_op jit(solution)/shard_map/leave/pallas_call | solution.py:510
  230.7 2.8 collective-permute-start.18
  235.2 3.6 collective-permute-done.19
  245.6 5.4 %leave_back.1 = (bf16[416,2304]{1,0:T(8,128)(2,1)S(1)}, bf16[416,2560]{1,0:T(8,128)(2,1)S(1)}) custom-call(f32[2,19]{1,0:T(2,128)S(1)} %pad_maximum_fusion.5.coef_ref, f32[416,2304]{1,0:T(8,128)S(1)} %copy-done.64, s32[416,256]{1,0:T(8,128)S(1)} %bitcast.222, bf16[416,2560]{1,0:T(8,128)(2,1)S(1)} %copy-done.73, bf16[512,1152]{1,0:T(8,128)(2,1)S(1)} %copy-done.8, ...), custom_call_target="tpu_custom_call" | custom-call | flops 12000000000 | bytes 36000000 | tf_op jit(solution)/shard_map/leave_back/pallas_call | solution.py:583
  251.0 3.5 skip_grad.1
  256.3 3.2 collective-permute-done.20
  265.9 11.0 %middle_back.1 = (bf16[4,416,768]{2,1,0:T(8,128)(2,1)S(1)}, f32[416,768]{1,0:T(8,128)S(1)}, bf16[416,768]{1,0:T(8,128)(2,1)S(1)}, bf16[4,416,192]{2,1,0:T(8,128)(2,1)S(1)}, f32[16,768]{1,0:T(8,128)S(1)}) custom-call(bf16[416,768]{1,0:T(8,128)(2,1)S(1)} %get-tuple-element.128.refs_1_.refs_0_, bf16[4,768,1536]{2,1,0:T(8,128)(2,1)} %bitcast.247, ...), custom_call_target="tpu_custom_call" | custom-call | flops 22000001024 | bytes 66000000 | tf_op jit(solution)/shard_map/middle_back/pallas_call | solution.py:926
  282.1 13.5 %attn_back.1.refs_3_.refs_1_ = bf16[4,416,576]{2,1,0:T(8,128)(2,1)S(1)} custom-call(bf16[4,416,576]{2,1,0:T(8,128)(2,1)S(1)} %copy-done.88, bf16[4,416,192]{2,1,0:T(8,128)(2,1)S(1)} %get-tuple-element.143.refs_1_, bf16[768,1536]{1,0:T(8,128)(2,1)S(1)} %get-tuple-element.145.refs_2_), custom_call_target="tpu_custom_call" | custom-call | flops 27000000512 | bytes 81000000 | tf_op jit(solution)/shard_map/attn_back/pallas_call | solution.py:994
  299.3 4.9 %attn_grad.1 = (bf16[768,1536]{1,0:T(8,128)(2,1)}, bf16[768,1536]{1,0:T(8,128)(2,1)S(1)}) custom-call(bf16[416,768]{1,0:T(8,128)(2,1)S(1)} %copy-done.77, bf16[4,416,576]{2,1,0:T(8,128)(2,1)S(1)} %attn_back.1.refs_3_.refs_1_, bf16[416,768]{1,0:T(8,128)(2,1)S(1)} %get-tuple-element.146.refs_2_, bf16[4,416,192]{2,1,0:T(8,128)(2,1)S(1)} %copy-done.71, ...), custom_call_target="tpu_custom_call" | custom-call | flops 7200000000 | bytes 21600000 | tf_op jit(solution)/shard_map/attn_grad/pallas_call | solution.py:1024
  304.6 3.0 decoder_grad.1.refs_12_.refs_9_
  308.9 10.3 %enter_back.1 = (bf16[416,768]{1,0:T(8,128)(2,1)S(1)}, bf16[416,1024]{1,0:T(8,128)(2,1)S(1)}, f32[208,768]{1,0:T(8,128)S(1)}, f32[16,768]{1,0:T(8,128)S(1)}) custom-call(s32[1]{0:T(128)} %bitcast.core_ref.refs_0_, bf16[4,416,576]{2,1,0:T(8,128)(2,1)S(1)} %attn_back.1.refs_3_.refs_1_, bf16[768,1536]{1,0:T(8,128)(2,1)} %gather_step.18.own_ref.refs_6_.refs_2_, ...), custom_call_target="tpu_custom_call" | custom-call | flops 20800000000 | bytes 62400000 | tf_op jit(solution)/shard_map/enter_back/pallas_call | solution.py:1069
  335.5 16.3 %collective-permute-done.26 = bf16[192,1536]{1,0:T(8,128)(2,1)S(1)} collective-permute-done((bf16[192,1536]{1,0:T(8,128)(2,1)S(1)}, bf16[192,1536]{1,0:T(8,128)(2,1)S(1)}, u32[]{:S(2)}, u32[]{:S(2)}) %collective-permute-start.26) | collective-permute-done | bytes 589856 | tf_op jit(solution)/shard_map/ppermute | solution.py:86
  360.3 7.8 %collective-permute-done.32 = bf16[192,768]{1,0:T(8,128)(2,1)S(1)} collective-permute-done((bf16[192,768]{1,0:T(8,128)(2,1)S(1)}, bf16[192,768]{1,0:T(8,128)(2,1)S(1)}, u32[]{:S(2)}, u32[]{:S(2)}) %collective-permute-start.32) | collective-permute-done | bytes 294944 | tf_op jit(solution)/shard_map/ppermute | solution.py:86
  379.6 2.7 collective-permute-start.35
  384.3 2.9 collective-permute-done.39
  392.6 4.5 collective-permute-done.43
  404.4 2.7 broadcast_select_fusion.1
  407.1 5.5 %collective-permute-done.40 = bf16[96,768]{1,0:T(8,128)(2,1)S(1)} collective-permute-done((bf16[96,768]{1,0:T(8,128)(2,1)S(1)}, bf16[96,768]{1,0:T(8,128)(2,1)S(1)}, u32[]{:S(2)}, u32[]{:S(2)}) %collective-permute-start.40) | collective-permute-done | bytes 147488 | tf_op jit(solution)/shard_map/ppermute | solution.py:86
  (528 shorter events, 196.7 us)
Async XLA Ops:
  7.3 169.5 %all-gather.2.cloned.1.call-start = ((), (), s32[]{:S(2)}) async-start(), calls=%async_computation | async-start | bytes 9732096 | tf_op jit(solution)/shard_map/all_gather | solution.py:1224
  10.3 19.7 %collective-permute-start = (bf16[800,128]{1,0:T(8,128)(2,1)S(1)}, bf16[800,128]{1,0:T(8,128)(2,1)S(1)}, u32[]{:S(2)}, u32[]{:S(2)}) collective-permute-start(bf16[800,128]{1,0:T(8,128)(2,1)S(1)} %pack.1), channel_id=1, source_target_pairs={{0,16},{4,20},{8,24},{12,28},{16,0},{20,4},{24,8},{28,12},{1,17},{... | collective-permute-start | bytes 614408 | tf_op jit(solution)/shard_map/ppermute | solution.py:86
  14.7 19.9 %collective-permute-start.2 = (bf16[96,768]{1,0:T(8,128)(2,1)S(1)}, bf16[96,768]{1,0:T(8,128)(2,1)S(1)}, u32[]{:S(2)}, u32[]{:S(2)}) collective-permute-start(bf16[96,768]{1,0:T(8,128)(2,1)S(1)} %pad_maximum_fusion.3), channel_id=1, source_target_pairs={{0,16},{4,20},{8,24},{12,28},{16,0},{20,4},{24,8},{28,12},{1,17},{... | collective-permute-start | bytes 442376 | tf_op jit(solution)/shard_map/ppermute | solution.py:86
  44.6 30.2 %collective-permute-start.5 = (bf16[384,768]{1,0:T(8,128)(2,1)S(1)}, bf16[384,768]{1,0:T(8,128)(2,1)S(1)}, u32[]{:S(2)}, u32[]{:S(2)}) collective-permute-start(bf16[384,768]{1,0:T(8,128)(2,1)S(1)} %bitcast.176), channel_id=1, source_target_pairs={{0,4},{4,0},{8,12},{12,8},{16,20},{20,16},{24,28},{28,24},{1,5},{5... | collective-permute-start | bytes 1769480 | tf_op jit(solution)/shard_map/ppermute | solution.py:86
  47.9 25.8 %collective-permute-start.6 = (bf16[128,1280]{1,0:T(8,128)(2,1)}, bf16[128,1280]{1,0:T(8,128)(2,1)S(1)}, u32[]{:S(2)}, u32[]{:S(2)}) collective-permute-start(bf16[128,1280]{1,0:T(8,128)(2,1)} %gate.2), channel_id=1, source_target_pairs={{0,16},{4,20},{8,24},{12,28},{16,0},{20,4},{24,8},{28,12},{1,17},{... | collective-permute-start | bytes 983048 | tf_op jit(solution)/shard_map/ppermute | solution.py:86
  54.1 47.0 %collective-permute-start.3 = (bf16[3200,128]{1,0:T(8,128)(2,1)}, bf16[3200,128]{1,0:T(8,128)(2,1)S(1)}, u32[]{:S(2)}, u32[]{:S(2)}) collective-permute-start(bf16[3200,128]{1,0:T(8,128)(2,1)} %bitcast.18.refs_3_), channel_id=1, source_target_pairs={{0,8},{4,12},{8,0},{12,4},{16,24},{20,28},{24,16},{28,20},{1,9},{5... | collective-permute-start | bytes 2457608 | tf_op jit(solution)/shard_map/ppermute | solution.py:86
  77.8 47.0 %collective-permute-start.8 = (bf16[768,768]{1,0:T(8,128)(2,1)S(1)}, bf16[768,768]{1,0:T(8,128)(2,1)}, u32[]{:S(2)}, u32[]{:S(2)}) collective-permute-start(bf16[768,768]{1,0:T(8,128)(2,1)S(1)} %bitcast.170), channel_id=1, source_target_pairs={{0,2},{1,3},{2,0},{3,1},{4,6},{5,7},{6,4},{7,5},{8,10},{9,11},{10,... | collective-permute-start | bytes 3538952 | tf_op jit(solution)/shard_map/ppermute | solution.py:86
  79.5 44.1 %collective-permute-start.9 = (bf16[256,1280]{1,0:T(8,128)(2,1)S(1)}, bf16[256,1280]{1,0:T(8,128)(2,1)}, u32[]{:S(2)}, u32[]{:S(2)}) collective-permute-start(bf16[256,1280]{1,0:T(8,128)(2,1)S(1)} %bitcast.174), channel_id=1, source_target_pairs={{0,8},{4,12},{8,0},{12,4},{16,24},{20,28},{24,16},{28,20},{1,9},{5... | collective-permute-start | bytes 1966088 | tf_op jit(solution)/shard_map/ppermute | solution.py:86
  103.6 29.0 %collective-permute-start.7 = (bf16[6400,128]{1,0:T(8,128)(2,1)}, bf16[6400,128]{1,0:T(8,128)(2,1)}, u32[]{:S(2)}, u32[]{:S(2)}) collective-permute-start(bf16[6400,128]{1,0:T(8,128)(2,1)} %bitcast.30.refs_3_), channel_id=1, source_target_pairs={{0,1},{1,0},{2,3},{3,2},{4,5},{5,4},{6,7},{7,6},{8,9},{9,8},{10,11... | collective-permute-start | bytes 4915208 | tf_op jit(solution)/shard_map/ppermute | solution.py:86
  127.7 30.8 %collective-permute-start.10 = (bf16[768,1536]{1,0:T(8,128)(2,1)}, bf16[768,1536]{1,0:T(8,128)(2,1)}, u32[]{:S(2)}, u32[]{:S(2)}) collective-permute-start(bf16[768,1536]{1,0:T(8,128)(2,1)} %gather_step.18.own_ref.refs_6_.refs_2_), channel_id=1, source_target_pairs={{0,1},{1,0},{2,3},{3,2},{4,5},{5,4},{6,7},{7,6},{8,9},{9,8},{10,11... | collective-permute-start | bytes 7077896 | tf_op jit(solution)/shard_map/ppermute | solution.py:86
  132.6 40.2 %collective-permute-start.11 = (bf16[512,1280]{1,0:T(8,128)(2,1)S(1)}, bf16[512,1280]{1,0:T(8,128)(2,1)S(1)}, u32[]{:S(2)}, u32[]{:S(2)}) collective-permute-start(bf16[512,1280]{1,0:T(8,128)(2,1)S(1)} %bitcast.168), channel_id=1, source_target_pairs={{0,4},{4,0},{8,12},{12,8},{16,20},{20,16},{24,28},{28,24},{1,5},{5... | collective-permute-start | bytes 3932168 | tf_op jit(solution)/shard_map/ppermute | solution.py:86
  176.1 23.2 %collective-permute-start.12 = (bf16[1024,1280]{1,0:T(8,128)(2,1)}, bf16[1024,1280]{1,0:T(8,128)(2,1)}, u32[]{:S(2)}, u32[]{:S(2)}) collective-permute-start(bf16[1024,1280]{1,0:T(8,128)(2,1)} %bitcast.40.skip_own_ref.refs_9_), channel_id=1, source_target_pairs={{0,1},{1,0},{2,3},{3,2},{4,5},{5,4},{6,7},{7,6},{8,9},{9,8},{10,11... | collective-permute-start | bytes 7864328 | tf_op jit(solution)/shard_map/ppermute | solution.py:86
  264.5 33.2 %collective-permute-start.23 = (bf16[512,1280]{1,0:T(8,128)(2,1)}, bf16[512,1280]{1,0:T(8,128)(2,1)S(1)}, u32[]{:S(2)}, u32[]{:S(2)}) collective-permute-start(bf16[512,1280]{1,0:T(8,128)(2,1)} %bitcast.54.refs_3_), channel_id=1, source_target_pairs={{0,4},{4,0},{8,12},{12,8},{16,20},{20,16},{24,28},{28,24},{1,5},{5... | collective-permute-start | bytes 3932168 | tf_op jit(solution)/shard_map/ppermute | solution.py:86
  278.6 42.6 %collective-permute-start.22 = (bf16[384,1536]{1,0:T(8,128)(2,1)}, bf16[384,1536]{1,0:T(8,128)(2,1)}, u32[]{:S(2)}, u32[]{:S(2)}) collective-permute-start(bf16[384,1536]{1,0:T(8,128)(2,1)} %bitcast.58.refs_3_), channel_id=1, source_target_pairs={{0,4},{4,0},{8,12},{12,8},{16,20},{20,16},{24,28},{28,24},{1,5},{5... | collective-permute-start | bytes 3538952 | tf_op jit(solution)/shard_map/ppermute | solution.py:86
  282.0 13.6 %collective-permute-start.24 = (bf16[768,1536]{1,0:T(8,128)(2,1)S(1)}, bf16[768,1536]{1,0:T(8,128)(2,1)S(1)}, u32[]{:S(2)}, u32[]{:S(2)}) collective-permute-start(bf16[768,1536]{1,0:T(8,128)(2,1)S(1)} %get-tuple-element.145.refs_2_), channel_id=1, source_target_pairs={{0,1},{1,0},{2,3},{3,2},{4,5},{5,4},{6,7},{7,6},{8,9},{9,8},{10,11... | collective-permute-start | bytes 7077896 | tf_op jit(solution)/shard_map/ppermute | solution.py:86
  297.4 28.6 %collective-permute-start.27 = (bf16[768,768]{1,0:T(8,128)(2,1)}, bf16[768,768]{1,0:T(8,128)(2,1)S(1)}, u32[]{:S(2)}, u32[]{:S(2)}) collective-permute-start(bf16[768,768]{1,0:T(8,128)(2,1)} %get-tuple-element.149.refs_3_), channel_id=1, source_target_pairs={{0,2},{1,3},{2,0},{3,1},{4,6},{5,7},{6,4},{7,5},{8,10},{9,11},{10,... | collective-permute-start | bytes 3538952 | tf_op jit(solution)/shard_map/ppermute | solution.py:86
  298.9 23.7 %collective-permute-start.28 = (bf16[256,1280]{1,0:T(8,128)(2,1)}, bf16[256,1280]{1,0:T(8,128)(2,1)S(1)}, u32[]{:S(2)}, u32[]{:S(2)}) collective-permute-start(bf16[256,1280]{1,0:T(8,128)(2,1)} %bitcast.62.refs_4_), channel_id=1, source_target_pairs={{0,8},{4,12},{8,0},{12,4},{16,24},{20,28},{24,16},{28,20},{1,9},{5... | collective-permute-start | bytes 1966088 | tf_op jit(solution)/shard_map/ppermute | solution.py:86
  304.3 15.0 %collective-permute-start.25 = (bf16[768,1536]{1,0:T(8,128)(2,1)}, bf16[768,1536]{1,0:T(8,128)(2,1)S(1)}, u32[]{:S(2)}, u32[]{:S(2)}) collective-permute-start(bf16[768,1536]{1,0:T(8,128)(2,1)} %get-tuple-element.152.refs_8_), channel_id=1, source_target_pairs={{0,1},{1,0},{2,3},{3,2},{4,5},{5,4},{6,7},{7,6},{8,9},{9,8},{10,11... | collective-permute-start | bytes 7077896 | tf_op jit(solution)/shard_map/ppermute | solution.py:86
  329.1 28.4 %collective-permute-start.33 = (bf16[768,768]{1,0:T(8,128)(2,1)S(1)}, bf16[768,768]{1,0:T(8,128)(2,1)S(1)}, u32[]{:S(2)}, u32[]{:S(2)}) collective-permute-start(bf16[768,768]{1,0:T(8,128)(2,1)S(1)} %get-tuple-element.161.refs_3_), channel_id=1, source_target_pairs={{0,2},{1,3},{2,0},{3,1},{4,6},{5,7},{6,4},{7,5},{8,10},{9,11},{10,... | collective-permute-start | bytes 3538952 | tf_op jit(solution)/shard_map/ppermute | solution.py:86
  329.4 22.4 %collective-permute-start.26 = (bf16[192,1536]{1,0:T(8,128)(2,1)S(1)}, bf16[192,1536]{1,0:T(8,128)(2,1)S(1)}, u32[]{:S(2)}, u32[]{:S(2)}) collective-permute-start(bf16[192,1536]{1,0:T(8,128)(2,1)S(1)} %bitcast.219), channel_id=1, source_target_pairs={{0,8},{4,12},{8,0},{12,4},{16,24},{20,28},{24,16},{28,20},{1,9},{5... | collective-permute-start | bytes 1769480 | tf_op jit(solution)/shard_map/ppermute | solution.py:86
  330.5 22.2 %collective-permute-start.31 = (bf16[384,768]{1,0:T(8,128)(2,1)S(1)}, bf16[384,768]{1,0:T(8,128)(2,1)S(1)}, u32[]{:S(2)}, u32[]{:S(2)}) collective-permute-start(bf16[384,768]{1,0:T(8,128)(2,1)S(1)} %bitcast.239), channel_id=1, source_target_pairs={{0,4},{4,0},{8,12},{12,8},{16,20},{20,16},{24,28},{28,24},{1,5},{5... | collective-permute-start | bytes 1769480 | tf_op jit(solution)/shard_map/ppermute | solution.py:86
  331.8 23.6 %collective-permute-start.41 = (bf16[128,1280]{1,0:T(8,128)(2,1)S(1)}, bf16[128,1280]{1,0:T(8,128)(2,1)S(1)}, u32[]{:S(2)}, u32[]{:S(2)}) collective-permute-start(bf16[128,1280]{1,0:T(8,128)(2,1)S(1)} %bitcast.226), channel_id=1, source_target_pairs={{0,16},{4,20},{8,24},{12,28},{16,0},{20,4},{24,8},{28,12},{1,17},{... | collective-permute-start | bytes 983048 | tf_op jit(solution)/shard_map/ppermute | solution.py:86
  334.1 37.4 %collective-permute-start.37 = (bf16[3200,128]{1,0:T(8,128)(2,1)}, bf16[3200,128]{1,0:T(8,128)(2,1)}, u32[]{:S(2)}, u32[]{:S(2)}) collective-permute-start(bf16[3200,128]{1,0:T(8,128)(2,1)} %bitcast.75.refs_3_), channel_id=1, source_target_pairs={{0,4},{4,0},{8,12},{12,8},{16,20},{20,16},{24,28},{28,24},{1,5},{5... | collective-permute-start | bytes 2457608 | tf_op jit(solution)/shard_map/ppermute | solution.py:86
  352.7 17.1 %collective-permute-start.30 = (bf16[96,1536]{1,0:T(8,128)(2,1)}, bf16[96,1536]{1,0:T(8,128)(2,1)}, u32[]{:S(2)}, u32[]{:S(2)}) collective-permute-start(bf16[96,1536]{1,0:T(8,128)(2,1)} %bitcast.77.refs_3_), channel_id=1, source_target_pairs={{0,16},{4,20},{8,24},{12,28},{16,0},{20,4},{24,8},{28,12},{1,17},{... | collective-permute-start | bytes 884744 | tf_op jit(solution)/shard_map/ppermute | solution.py:86
  352.9 15.2 %collective-permute-start.32 = (bf16[192,768]{1,0:T(8,128)(2,1)S(1)}, bf16[192,768]{1,0:T(8,128)(2,1)S(1)}, u32[]{:S(2)}, u32[]{:S(2)}) collective-permute-start(bf16[192,768]{1,0:T(8,128)(2,1)S(1)} %bitcast.207), channel_id=1, source_target_pairs={{0,8},{4,12},{8,0},{12,4},{16,24},{20,28},{24,16},{28,20},{1,9},{5... | collective-permute-start | bytes 884744 | tf_op jit(solution)/shard_map/ppermute | solution.py:86
  359.0 23.6 %collective-permute-start.36 = (bf16[384,768]{1,0:T(8,128)(2,1)}, bf16[384,768]{1,0:T(8,128)(2,1)}, u32[]{:S(2)}, u32[]{:S(2)}) collective-permute-start(bf16[384,768]{1,0:T(8,128)(2,1)} %bitcast.85.refs_3_), channel_id=1, source_target_pairs={{0,4},{4,0},{8,12},{12,8},{16,20},{20,16},{24,28},{28,24},{1,5},{5... | collective-permute-start | bytes 1769480 | tf_op jit(solution)/shard_map/ppermute | solution.py:86
  374.4 12.8 %collective-permute-start.39 = (bf16[1600,128]{1,0:T(8,128)(2,1)}, bf16[1600,128]{1,0:T(8,128)(2,1)}, u32[]{:S(2)}, u32[]{:S(2)}) collective-permute-start(bf16[1600,128]{1,0:T(8,128)(2,1)} %bitcast.92.refs_3_), channel_id=1, source_target_pairs={{0,8},{4,12},{8,0},{12,4},{16,24},{20,28},{24,16},{28,20},{1,9},{5... | collective-permute-start | bytes 1228808 | tf_op jit(solution)/shard_map/ppermute | solution.py:86
  375.2 13.2 %collective-permute-start.42 = (bf16[128,1280]{1,0:T(8,128)(2,1)}, bf16[128,1280]{1,0:T(8,128)(2,1)}, u32[]{:S(2)}, u32[]{:S(2)}) collective-permute-start(bf16[128,1280]{1,0:T(8,128)(2,1)} %reduce-precision_convert_fusion), channel_id=1, source_target_pairs={{0,2},{1,3},{2,0},{3,1},{4,6},{5,7},{6,4},{7,5},{8,10},{9,11},{10,... | collective-permute-start | bytes 983048 | tf_op jit(solution)/shard_map/ppermute | solution.py:86
  379.6 18.8 %collective-permute-start.35 = (bf16[96,768]{1,0:T(8,128)(2,1)}, bf16[96,768]{1,0:T(8,128)(2,1)S(1)}, u32[]{:S(2)}, u32[]{:S(2)}) collective-permute-start(bf16[96,768]{1,0:T(8,128)(2,1)} %bitcast.86.refs_3_), channel_id=1, source_target_pairs={{0,16},{4,20},{8,24},{12,28},{16,0},{20,4},{24,8},{28,12},{1,17},{... | collective-permute-start | bytes 442376 | tf_op jit(solution)/shard_map/ppermute | solution.py:86
  382.2 17.4 %collective-permute-start.34 = (bf16[96,768]{1,0:T(8,128)(2,1)}, bf16[96,768]{1,0:T(8,128)(2,1)S(1)}, u32[]{:S(2)}, u32[]{:S(2)}) collective-permute-start(bf16[96,768]{1,0:T(8,128)(2,1)} %copy-done.35), channel_id=1, source_target_pairs={{0,2},{1,3},{2,0},{3,1},{4,6},{5,7},{6,4},{7,5},{8,10},{9,11},{10,... | collective-permute-start | bytes 442376 | tf_op jit(solution)/shard_map/ppermute | solution.py:86
  390.3 14.1 %collective-permute-start.53 = (f32[128,1280]{1,0:T(8,128)}, f32[128,1280]{1,0:T(8,128)}, u32[]{:S(2)}, u32[]{:S(2)}) collective-permute-start(f32[128,1280]{1,0:T(8,128)} %convert_add_fusion), channel_id=1, source_target_pairs={{0,1},{1,0},{2,3},{3,2},{4,5},{5,4},{6,7},{7,6},{8,9},{9,8},{10,11... | collective-permute-start | bytes 1966088 | tf_op jit(solution)/shard_map/ppermute | solution.py:86
  390.3 12.9 %collective-permute-start.38 = (bf16[192,768]{1,0:T(8,128)(2,1)}, bf16[192,768]{1,0:T(8,128)(2,1)S(1)}, u32[]{:S(2)}, u32[]{:S(2)}) collective-permute-start(bf16[192,768]{1,0:T(8,128)(2,1)} %bitcast.94.refs_3_), channel_id=1, source_target_pairs={{0,8},{4,12},{8,0},{12,4},{16,24},{20,28},{24,16},{28,20},{1,9},{5... | collective-permute-start | bytes 884744 | tf_op jit(solution)/shard_map/ppermute | solution.py:86
  (165 other events, 978.1 us)
Sparse Core Ops, SparseCore 0:
  11.6 113.9 all-gather.1

commit v5 on v4

--- a/solution.py
+++ b/solution.py
@@ -1,5 +1,6 @@
 import jax
 import jax.numpy as jnp
+import numpy as np
 from jax import lax
 from jax.experimental import pallas as pl
 from jax.experimental.pallas import tpu as pltpu
@@ -68,8 +69,8 @@
     )
 
 
-def params():
-    return pltpu.CompilerParams(vmem_limit_bytes=32 * MIB)
+def params(size=27):
+    return pltpu.CompilerParams(vmem_limit_bytes=size * MIB)
 
 
 def run_after(kernel, count, after):
@@ -148,7 +149,7 @@
             in_specs=[SCALAR] + [FULL] * 2 + waits,
             out_specs=FULL,
             out_shape=jax.ShapeDtypeStruct(out, self.value.dtype),
-            compiler_params=params(),
+            compiler_params=params(12),
             cost_estimate=cost(0.1),
             name="gather_step",
         )(my_bit(axis, bit).reshape(1), self.value.reshape(shape), other.reshape(shape), *after)
@@ -205,7 +206,7 @@
             in_specs=[SCALAR] + [block(shape)] * count + waits,
             out_specs=[block(half)] * 2,
             out_shape=[jax.ShapeDtypeStruct(half, bf16), jax.ShapeDtypeStruct(half, kept_type)],
-            compiler_params=params(),
+            compiler_params=params(12),
             cost_estimate=cost(0.1),
             name="scatter_step",
         )(my_bit(axis, bit).reshape(1), *[term.reshape(shape) for term in self.terms], *after)
@@ -409,7 +410,7 @@
         out_specs=[(part_of if len(out.shape) == 3 else whole_of)(out) for out in outs],
         out_shape=outs,
         compiler_params=params(),
-        cost_estimate=cost(13),
+        cost_estimate=cost(2),
         name="middle",
     )(*values, mlp_all)
 
@@ -1098,26 +1099,22 @@
 
 
 def same_block(rows, columns, inner, outer):
-    row = lax.broadcasted_iota(jnp.int32, (rows, columns), 0) // inner
-    column = lax.broadcasted_iota(jnp.int32, (rows, columns), 1) // outer
-    return row == column
+    return (np.arange(rows) // inner)[:, None] == (np.arange(columns) // outer)[None, :]
 
 
 def block_diag(weight, parents):
     inner, outer = weight.shape
     mask = same_block(parents * inner, parents * outer, inner, outer)
     tiled = jnp.tile(weight, (parents, parents))
-    return jnp.where(mask, tiled, jnp.zeros_like(tiled))
+    return tiled * mask.astype(bf16)
 
 
 def head_masks():
-    wide = CLASSES * GROUP * 4
-    column = lax.broadcasted_iota(jnp.int32, (4 * CLASSES, wide), 1)
-    source = lax.broadcasted_iota(jnp.int32, (4 * CLASSES, wide), 0)
-    pick = source == (column % 4) * CLASSES + column // (GROUP * 4)
-    row = lax.broadcasted_iota(jnp.int32, (GROUP * CHAN_D, wide), 0)
-    across = lax.broadcasted_iota(jnp.int32, (GROUP * CHAN_D, wide), 1)
-    mask = row // CHAN_D == (across // 4) % GROUP
+    column = np.arange(CLASSES * GROUP * 4)
+    source = np.arange(4 * CLASSES)[:, None]
+    pick = source == ((column % 4) * CLASSES + column // (GROUP * 4))[None, :]
+    row = np.arange(GROUP * CHAN_D)[:, None]
+    mask = row // CHAN_D == ((column // 4) % GROUP)[None, :]
     return pick, mask
 
 
@@ -1125,7 +1122,7 @@
     pick, mask = head_masks()
     spread = matmul(head_b, pick.astype(bf16)).astype(bf16)
     tiled = jnp.tile(spread, (GROUP, 1))
-    return jnp.where(mask, tiled, jnp.zeros_like(tiled))
+    return tiled * mask.astype(bf16)
 
 
 def stack_columns(value, width):
@@ -1264,10 +1261,6 @@
     split.start("mp", 1)
     token = first.finish(after=(token,))
     first_own = first.value
-    token = skip.finish(after=(token,))
-    skip.start("dp", last)
-    token = split.finish(after=(token,))
-    attn_weights = split.value
     first_pair = [
         value.reshape(n_dp, -1, LANES) for value in (first_own, swap(first_own, "mp", 0))
     ]
@@ -1285,6 +1278,12 @@
         table = side(2).reshape(D, 2 * LANES).T.astype(f32)
     dec_flat = jnp.stack(dec_parts, axis=1).reshape(n_dp, -1)[:, : shared.flat].reshape(-1)
     dec_b, one_b, two_b, three_b, head_b = split_decoder(dec_flat)
+    three_four = block_diag(three_b, 4)
+    big_head = big_head_of(head_b)
+    token = skip.finish(after=(token, dec_b, one_b, two_b, three_four, big_head, table))
+    skip.start("dp", last)
+    token = split.finish(after=(token,))
+    attn_weights = split.value
 
     attn_all = (attn_weights, swap(attn_weights, "mp", 0))
 
@@ -1298,13 +1297,11 @@
     hidden, slope_stem, embed, normed, triple, context = enter(
         pixels, stem_b, embed_b, table, attn_all, attn_cut
     )
-    skip_weights = skip.finish(after=(hidden,))
-    skip_all = (skip_weights, swap(skip_weights, "mp", 0))
     resid, normed2, slope_mlp, inner, resid2, final_low = middle(
         context, embed, table, attn_all, mlp_all
     )
-    three_four = block_diag(three_b, 4)
-    big_head = big_head_of(head_b)
+    skip_weights = skip.finish(after=(final_low,))
+    skip_all = (skip_weights, swap(skip_weights, "mp", 0))
     slope0, level0, slope_skips, level1, level2, level3, logits, stats = leave(
         core_id, hidden, final_low, skip_all, dec_b, one_b, two_b, three_four, big_head, label_own
     )

time: 472 us -> 459 us (0.972)
  waiting for transfers between devices: 137 us -> 124 us
  Pallas kernels: 130 us -> 124 us
    ppermute x40, waiting for transfers between devices: 123 us -> 110 us  [swap(): return lax.ppermute(value, axis, [(i, i ^ 1 << bit) for i in range(size)])]
    unnamed x301 -> x321, local copies, waits for them, and re-layouts: 43.8 us -> 52 us
  transfers between devices with their start and end apart: 55 -> 55, of which waited for: 27 -> 28; matrix products, arithmetic and copies ran while one was open for 11% -> 10% of each run, Pallas kernels for 22% -> 22%
where the time goes in v5:
time: 459 us; the launch traced here: 450 us
  waiting for transfers between devices  124 us (27%)
  Pallas kernels  124 us (27%)
  local copies, waits for them, and re-layouts  76.1 us (17%)
  starting transfers between devices  59.8 us (13%)
  other arithmetic  39.9 us (9%)
  between operations  25.6 us (6%)
    ppermute x40, waiting for transfers between devices, swap(): return lax.ppermute(value, axis, [(i, i ^ 1 << bit) for i in range(size)])  110 us
    unnamed x321, local copies, waits for them, and re-layouts  52 us
    ppermute x40, starting transfers between devices, swap(): return lax.ppermute(value, axis, [(i, i ^ 1 << bit) for i in range(size)])  43.2 us
    pallas_call x18, Pallas kernels, step(): pl.pallas_call(kernel, grid=(steps,), in_specs=[SCALAR] + [block(shape)]...  17.5 us
    ppermute x14, starting transfers between devices, hop(): lax.ppermute(value, ('dp', 'mp'), [(i, i ^ move) for i in range(size)])  16.5 us
    ppermute x14, waiting for transfers between devices, hop(): lax.ppermute(value, ('dp', 'mp'), [(i, i ^ move) for i in range(size)])  14.6 us
    pallas_call x1, Pallas kernels, attn_back(): pl.pallas_call(kernel, grid=(parts,), in_specs=[whole(width), whole(width...  13.5 us
    sub x9, other arithmetic, adamw(): weight - rate * (first_hat / (jnp.sqrt(second_hat) + adam_eps) + decay_ra...  12.9 us
  transfers between devices with their start and end apart: 55, of which 28 were waited for; matrix products, arithmetic and copies ran while one was open for 10% of the time, Pallas kernels for 22%

profile of v5, /device:TPU:0, one launch (start us, length us, event | category | flops | bytes accessed | tf_op | source)
XLA Modules:
  0.0 450.2 jit_solution(5135869813936763051)
XLA Ops:
  10.4 4.1 collective-permute-start
  16.7 13.4 %collective-permute-done = bf16[800,128]{1,0:T(8,128)(2,1)S(1)} collective-permute-done((bf16[800,128]{1,0:T(8,128)(2,1)S(1)}, bf16[800,128]{1,0:T(8,128)(2,1)S(1)}, u32[]{:S(2)}, u32[]{:S(2)}) %collective-permute-start) | collective-permute-done | bytes 204832 | tf_op jit(solution)/shard_map/ppermute | solution.py:87
  38.4 3.5 collective-permute-start.3
  41.9 3.6 collective-permute-done.4
  50.4 6.1 %collective-permute-start.6 = (bf16[128,1280]{1,0:T(8,128)(2,1)}, bf16[128,1280]{1,0:T(8,128)(2,1)S(1)}, u32[]{:S(2)}, u32[]{:S(2)}) collective-permute-start(bf16[128,1280]{1,0:T(8,128)(2,1)} %gate.2), channel_id=1, source_target_pairs={{0,16},{4,20},{8,24},{12,28},{16,0},{20,4},{24,8},{28,12},{1,17},{... | collective-permute-start | bytes 983048 | tf_op jit(solution)/shard_map/ppermute | solution.py:87
  56.4 28.6 %collective-permute-done.6 = bf16[128,1280]{1,0:T(8,128)(2,1)S(1)} collective-permute-done((bf16[128,1280]{1,0:T(8,128)(2,1)}, bf16[128,1280]{1,0:T(8,128)(2,1)S(1)}, u32[]{:S(2)}, u32[]{:S(2)}) %collective-permute-start.6) | collective-permute-done | bytes 327712 | tf_op jit(solution)/shard_map/ppermute | solution.py:87
  89.9 3.1 collective-permute-start.9
  97.7 2.9 reshape.453
  100.6 3.8 slice.144
  118.9 2.9 collective-permute-done.9
  124.5 3.2 gather_step.18.own_ref.refs_6_.refs_2_
  136.1 12.6 %enter.1 = (bf16[416,1024]{1,0:T(8,128)(2,1)S(1)}, bf16[416,1024]{1,0:T(8,128)(2,1)S(1)}, f32[416,768]{1,0:T(8,128)S(1)}, bf16[416,768]{1,0:T(8,128)(2,1)S(1)}, ...) custom-call(bf16[416,256]{1,0:T(8,128)(2,1)S(1)} %bitcast.239, bf16[256,1024]{1,0:T(8,128)(2,1)S(1)} %copy-done.94, ...), custom_call_target="tpu_custom_call" | custom-call | flops 25999998976 | bytes 78000000 | tf_op jit(solution)/shard_map/enter/pallas_call | solution.py:331
  154.7 3.7 copy-done.2
  162.0 12.0 %middle.1 = (f32[416,768]{1,0:T(8,128)S(1)}, bf16[416,768]{1,0:T(8,128)(2,1)S(1)}, bf16[4,416,768]{2,1,0:T(8,128)(2,1)S(1)}, bf16[4,416,768]{2,1,0:T(8,128)(2,1)...) custom-call(bf16[4,416,192]{2,1,0:T(8,128)(2,1)S(1)} %copy-done.30, f32[416,768]{1,0:T(8,128)S(1)} %copy-done.22, ...), custom_call_target="tpu_custom_call" | custom-call | flops 4000000000 | bytes 12000000 | tf_op jit(solution)/shard_map/middle/pallas_call | solution.py:406
  180.2 4.4 collective-permute-done.12.skip_other_ref.refs_10_
  184.7 9.3 %leave.1 = (f32[416,256]{1,0:T(8,128)S(1)}, bf16[416,256]{1,0:T(8,128)(2,1)S(1)}, bf16[416,2560]{1,0:T(8,128)(2,1)S(1)}, bf16[416,512]{1,0:T(8,128)(2,1)S(1)}, b...) custom-call(s32[1]{0:T(128)} %bitcast.core_ref.refs_0_, ...), custom_call_target="tpu_custom_call" | custom-call | flops 24000000000 | bytes 72000000 | tf_op jit(solution)/shard_map/leave/pallas_call | solution.py:511
  216.2 3.7 collective-permute-start.18
  221.4 3.8 collective-permute-done.19
  231.9 5.4 %leave_back.1 = (bf16[416,2304]{1,0:T(8,128)(2,1)S(1)}, bf16[416,2560]{1,0:T(8,128)(2,1)S(1)}) custom-call(f32[2,19]{1,0:T(2,128)S(1)} %pad_maximum_fusion.5.coef_ref, f32[416,2304]{1,0:T(8,128)S(1)} %copy-done.86, s32[416,256]{1,0:T(8,128)S(1)} %bitcast.232, bf16[416,2560]{1,0:T(8,128)(2,1)S(1)} %copy-done.90, bf16[512,1152]{1,0:T(8,128)(2,1)S(1)} %bitcast.187, ...), custom_call_target="tpu_custom_call" | custom-call | flops 12000000000 | bytes 36000000 | tf_op jit(solution)/shard_map/leave_back/pallas_call | solution.py:584
  238.6 3.5 skip_grad.1
  243.9 3.2 collective-permute-done.20
  253.1 11.0 %middle_back.1 = (bf16[4,416,768]{2,1,0:T(8,128)(2,1)S(1)}, f32[416,768]{1,0:T(8,128)S(1)}, bf16[416,768]{1,0:T(8,128)(2,1)S(1)}, bf16[4,416,192]{2,1,0:T(8,128)(2,1)S(1)}, f32[16,768]{1,0:T(8,128)S(1)}) custom-call(bf16[416,768]{1,0:T(8,128)(2,1)S(1)} %get-tuple-element.128.refs_1_.refs_0_, bf16[4,768,1536]{2,1,0:T(8,128)(2,1)} %bitcast.170, ...), custom_call_target="tpu_custom_call" | custom-call | flops 22000001024 | bytes 66000000 | tf_op jit(solution)/shard_map/middle_back/pallas_call | solution.py:927
  269.7 13.5 %attn_back.1.refs_3_.refs_1_ = bf16[4,416,576]{2,1,0:T(8,128)(2,1)S(1)} custom-call(bf16[4,416,576]{2,1,0:T(8,128)(2,1)S(1)} %copy-done.100, bf16[4,416,192]{2,1,0:T(8,128)(2,1)S(1)} %get-tuple-element.143.refs_1_, bf16[768,1536]{1,0:T(8,128)(2,1)S(1)} %get-tuple-element.145.refs_2_), custom_call_target="tpu_custom_call" | custom-call | flops 27000000512 | bytes 81000000 | tf_op jit(solution)/shard_map/attn_back/pallas_call | solution.py:995
  286.6 4.9 %attn_grad.1 = (bf16[768,1536]{1,0:T(8,128)(2,1)}, bf16[768,1536]{1,0:T(8,128)(2,1)S(1)}) custom-call(bf16[416,768]{1,0:T(8,128)(2,1)S(1)} %copy-done.96, bf16[4,416,576]{2,1,0:T(8,128)(2,1)S(1)} %attn_back.1.refs_3_.refs_1_, bf16[416,768]{1,0:T(8,128)(2,1)S(1)} %get-tuple-element.146.refs_2_, bf16[4,416,192]{2,1,0:T(8,128)(2,1)S(1)} %copy-done.31, ...), custom_call_target="tpu_custom_call" | custom-call | flops 7200000000 | bytes 21600000 | tf_op jit(solution)/shard_map/attn_grad/pallas_call | solution.py:1025
  291.8 3.0 decoder_grad.1.refs_12_.refs_9_
  298.2 8.8 %enter_back.1 = (bf16[416,768]{1,0:T(8,128)(2,1)S(1)}, bf16[416,1024]{1,0:T(8,128)(2,1)S(1)}, f32[208,768]{1,0:T(8,128)S(1)}, f32[16,768]{1,0:T(8,128)S(1)}) custom-call(s32[1]{0:T(128)} %bitcast.core_ref.refs_0_, bf16[4,416,576]{2,1,0:T(8,128)(2,1)S(1)} %attn_back.1.refs_3_.refs_1_, bf16[768,1536]{1,0:T(8,128)(2,1)} %gather_step.18.own_ref.refs_6_.refs_2_, ...), custom_call_target="tpu_custom_call" | custom-call | flops 20800000000 | bytes 62400000 | tf_op jit(solution)/shard_map/enter_back/pallas_call | solution.py:1070
  309.1 3.2 collective-permute-done.27
  321.3 17.5 %collective-permute-done.26 = bf16[192,1536]{1,0:T(8,128)(2,1)S(1)} collective-permute-done((bf16[192,1536]{1,0:T(8,128)(2,1)S(1)}, bf16[192,1536]{1,0:T(8,128)(2,1)S(1)}, u32[]{:S(2)}, u32[]{:S(2)}) %collective-permute-start.26) | collective-permute-done | bytes 589856 | tf_op jit(solution)/shard_map/ppermute | solution.py:87
  346.1 8.4 %collective-permute-done.32 = bf16[192,768]{1,0:T(8,128)(2,1)S(1)} collective-permute-done((bf16[192,768]{1,0:T(8,128)(2,1)S(1)}, bf16[192,768]{1,0:T(8,128)(2,1)S(1)}, u32[]{:S(2)}, u32[]{:S(2)}) %collective-permute-start.32) | collective-permute-done | bytes 294944 | tf_op jit(solution)/shard_map/ppermute | solution.py:87
  369.9 3.7 collective-permute-done.39
  377.0 6.1 %collective-permute-done.43 = bf16[800,128]{1,0:T(8,128)(2,1)S(1)} collective-permute-done((bf16[800,128]{1,0:T(8,128)(2,1)S(1)}, bf16[800,128]{1,0:T(8,128)(2,1)S(1)}, u32[]{:S(2)}, u32[]{:S(2)}) %collective-permute-start.43) | collective-permute-done | bytes 204832 | tf_op jit(solution)/shard_map/ppermute | solution.py:87
  393.5 4.7 %collective-permute-done.40 = bf16[96,768]{1,0:T(8,128)(2,1)S(1)} collective-permute-done((bf16[96,768]{1,0:T(8,128)(2,1)S(1)}, bf16[96,768]{1,0:T(8,128)(2,1)S(1)}, u32[]{:S(2)}, u32[]{:S(2)}) %collective-permute-start.40) | collective-permute-done | bytes 147488 | tf_op jit(solution)/shard_map/ppermute | solution.py:87
  (537 shorter events, 202.9 us)
Async XLA Ops:
  7.3 147.5 %all-gather.2.cloned.1.call-start = ((), (), s32[]{:S(2)}) async-start(), calls=%async_computation | async-start | bytes 9732096 | tf_op jit(solution)/shard_map/all_gather | solution.py:1221
  10.4 19.8 %collective-permute-start = (bf16[800,128]{1,0:T(8,128)(2,1)S(1)}, bf16[800,128]{1,0:T(8,128)(2,1)S(1)}, u32[]{:S(2)}, u32[]{:S(2)}) collective-permute-start(bf16[800,128]{1,0:T(8,128)(2,1)S(1)} %pack.1), channel_id=1, source_target_pairs={{0,16},{4,20},{8,24},{12,28},{16,0},{20,4},{24,8},{28,12},{1,17},{... | collective-permute-start | bytes 614408 | tf_op jit(solution)/shard_map/ppermute | solution.py:87
  16.0 18.7 %collective-permute-start.2 = (bf16[96,768]{1,0:T(8,128)(2,1)}, bf16[96,768]{1,0:T(8,128)(2,1)S(1)}, u32[]{:S(2)}, u32[]{:S(2)}) collective-permute-start(bf16[96,768]{1,0:T(8,128)(2,1)} %pad_maximum_fusion.3), channel_id=1, source_target_pairs={{0,16},{4,20},{8,24},{12,28},{16,0},{20,4},{24,8},{28,12},{1,17},{... | collective-permute-start | bytes 442376 | tf_op jit(solution)/shard_map/ppermute | solution.py:87
  34.7 10.8 %collective-permute-start.4 = (bf16[192,768]{1,0:T(8,128)(2,1)S(1)}, bf16[192,768]{1,0:T(8,128)(2,1)}, u32[]{:S(2)}, u32[]{:S(2)}) collective-permute-start(bf16[192,768]{1,0:T(8,128)(2,1)S(1)} %bitcast.188), channel_id=1, source_target_pairs={{0,8},{4,12},{8,0},{12,4},{16,24},{20,28},{24,16},{28,20},{1,9},{5... | collective-permute-start | bytes 884744 | tf_op jit(solution)/shard_map/ppermute | solution.py:87
  38.4 50.2 %collective-permute-start.3 = (bf16[3200,128]{1,0:T(8,128)(2,1)S(1)}, bf16[3200,128]{1,0:T(8,128)(2,1)}, u32[]{:S(2)}, u32[]{:S(2)}) collective-permute-start(bf16[3200,128]{1,0:T(8,128)(2,1)S(1)} %bitcast.176), channel_id=1, source_target_pairs={{0,8},{4,12},{8,0},{12,4},{16,24},{20,28},{24,16},{28,20},{1,9},{5... | collective-permute-start | bytes 2457608 | tf_op jit(solution)/shard_map/ppermute | solution.py:87
  46.5 39.6 %collective-permute-start.5 = (bf16[384,768]{1,0:T(8,128)(2,1)S(1)}, bf16[384,768]{1,0:T(8,128)(2,1)}, u32[]{:S(2)}, u32[]{:S(2)}) collective-permute-start(bf16[384,768]{1,0:T(8,128)(2,1)S(1)} %bitcast.182), channel_id=1, source_target_pairs={{0,4},{4,0},{8,12},{12,8},{16,20},{20,16},{24,28},{28,24},{1,5},{5... | collective-permute-start | bytes 1769480 | tf_op jit(solution)/shard_map/ppermute | solution.py:87
  50.4 34.7 %collective-permute-start.6 = (bf16[128,1280]{1,0:T(8,128)(2,1)}, bf16[128,1280]{1,0:T(8,128)(2,1)S(1)}, u32[]{:S(2)}, u32[]{:S(2)}) collective-permute-start(bf16[128,1280]{1,0:T(8,128)(2,1)} %gate.2), channel_id=1, source_target_pairs={{0,16},{4,20},{8,24},{12,28},{16,0},{20,4},{24,8},{28,12},{1,17},{... | collective-permute-start | bytes 983048 | tf_op jit(solution)/shard_map/ppermute | solution.py:87
  89.9 31.9 %collective-permute-start.9 = (bf16[256,1280]{1,0:T(8,128)(2,1)}, bf16[256,1280]{1,0:T(8,128)(2,1)}, u32[]{:S(2)}, u32[]{:S(2)}) collective-permute-start(bf16[256,1280]{1,0:T(8,128)(2,1)} %bitcast.180), channel_id=1, source_target_pairs={{0,8},{4,12},{8,0},{12,4},{16,24},{20,28},{24,16},{28,20},{1,9},{5... | collective-permute-start | bytes 1966088 | tf_op jit(solution)/shard_map/ppermute | solution.py:87
  93.0 31.4 %collective-permute-start.8 = (bf16[768,768]{1,0:T(8,128)(2,1)}, bf16[768,768]{1,0:T(8,128)(2,1)}, u32[]{:S(2)}, u32[]{:S(2)}) collective-permute-start(bf16[768,768]{1,0:T(8,128)(2,1)} %bitcast.28.refs_3_.refs_1_), channel_id=1, source_target_pairs={{0,2},{1,3},{2,0},{3,1},{4,6},{5,7},{6,4},{7,5},{8,10},{9,11},{10,... | collective-permute-start | bytes 3538952 | tf_op jit(solution)/shard_map/ppermute | solution.py:87
  129.2 47.8 %collective-permute-start.11 = (bf16[512,1280]{1,0:T(8,128)(2,1)S(1)}, bf16[512,1280]{1,0:T(8,128)(2,1)}, u32[]{:S(2)}, u32[]{:S(2)}) collective-permute-start(bf16[512,1280]{1,0:T(8,128)(2,1)S(1)} %bitcast.168), channel_id=1, source_target_pairs={{0,4},{4,0},{8,12},{12,8},{16,20},{20,16},{24,28},{28,24},{1,5},{5... | collective-permute-start | bytes 3932168 | tf_op jit(solution)/shard_map/ppermute | solution.py:87
  251.9 12.2 %collective-permute-start.21 = (bf16[768,1536]{1,0:T(8,128)(2,1)S(1)}, bf16[768,1536]{1,0:T(8,128)(2,1)S(1)}, u32[]{:S(2)}, u32[]{:S(2)}) collective-permute-start(bf16[768,1536]{1,0:T(8,128)(2,1)S(1)} %get-tuple-element.134.refs_8_), channel_id=1, source_target_pairs={{0,1},{1,0},{2,3},{3,2},{4,5},{5,4},{6,7},{7,6},{8,9},{9,8},{10,11... | collective-permute-start | bytes 7077896 | tf_op jit(solution)/shard_map/ppermute | solution.py:87
  252.1 32.8 %collective-permute-start.23 = (bf16[512,1280]{1,0:T(8,128)(2,1)}, bf16[512,1280]{1,0:T(8,128)(2,1)S(1)}, u32[]{:S(2)}, u32[]{:S(2)}) collective-permute-start(bf16[512,1280]{1,0:T(8,128)(2,1)} %bitcast.54.refs_3_), channel_id=1, source_target_pairs={{0,4},{4,0},{8,12},{12,8},{16,20},{20,16},{24,28},{28,24},{1,5},{5... | collective-permute-start | bytes 3932168 | tf_op jit(solution)/shard_map/ppermute | solution.py:87
  265.9 42.8 %collective-permute-start.22 = (bf16[384,1536]{1,0:T(8,128)(2,1)}, bf16[384,1536]{1,0:T(8,128)(2,1)S(1)}, u32[]{:S(2)}, u32[]{:S(2)}) collective-permute-start(bf16[384,1536]{1,0:T(8,128)(2,1)} %bitcast.58.refs_3_), channel_id=1, source_target_pairs={{0,4},{4,0},{8,12},{12,8},{16,20},{20,16},{24,28},{28,24},{1,5},{5... | collective-permute-start | bytes 3538952 | tf_op jit(solution)/shard_map/ppermute | solution.py:87
  269.6 13.6 %collective-permute-start.24 = (bf16[768,1536]{1,0:T(8,128)(2,1)S(1)}, bf16[768,1536]{1,0:T(8,128)(2,1)S(1)}, u32[]{:S(2)}, u32[]{:S(2)}) collective-permute-start(bf16[768,1536]{1,0:T(8,128)(2,1)S(1)} %get-tuple-element.145.refs_2_), channel_id=1, source_target_pairs={{0,1},{1,0},{2,3},{3,2},{4,5},{5,4},{6,7},{7,6},{8,9},{9,8},{10,11... | collective-permute-start | bytes 7077896 | tf_op jit(solution)/shard_map/ppermute | solution.py:87
  283.9 28.4 %collective-permute-start.27 = (bf16[768,768]{1,0:T(8,128)(2,1)S(1)}, bf16[768,768]{1,0:T(8,128)(2,1)S(1)}, u32[]{:S(2)}, u32[]{:S(2)}) collective-permute-start(bf16[768,768]{1,0:T(8,128)(2,1)S(1)} %get-tuple-element.149.refs_3_), channel_id=1, source_target_pairs={{0,2},{1,3},{2,0},{3,1},{4,6},{5,7},{6,4},{7,5},{8,10},{9,11},{10,... | collective-permute-start | bytes 3538952 | tf_op jit(solution)/shard_map/ppermute | solution.py:87
  286.1 22.8 %collective-permute-start.28 = (bf16[256,1280]{1,0:T(8,128)(2,1)}, bf16[256,1280]{1,0:T(8,128)(2,1)S(1)}, u32[]{:S(2)}, u32[]{:S(2)}) collective-permute-start(bf16[256,1280]{1,0:T(8,128)(2,1)} %bitcast.62.refs_4_), channel_id=1, source_target_pairs={{0,8},{4,12},{8,0},{12,4},{16,24},{20,28},{24,16},{28,20},{1,9},{5... | collective-permute-start | bytes 1966088 | tf_op jit(solution)/shard_map/ppermute | solution.py:87
  291.5 15.5 %collective-permute-start.25 = (bf16[768,1536]{1,0:T(8,128)(2,1)}, bf16[768,1536]{1,0:T(8,128)(2,1)S(1)}, u32[]{:S(2)}, u32[]{:S(2)}) collective-permute-start(bf16[768,1536]{1,0:T(8,128)(2,1)} %get-tuple-element.152.refs_8_), channel_id=1, source_target_pairs={{0,1},{1,0},{2,3},{3,2},{4,5},{5,4},{6,7},{7,6},{8,9},{9,8},{10,11... | collective-permute-start | bytes 7077896 | tf_op jit(solution)/shard_map/ppermute | solution.py:87
  315.3 28.4 %collective-permute-start.33 = (bf16[768,768]{1,0:T(8,128)(2,1)S(1)}, bf16[768,768]{1,0:T(8,128)(2,1)S(1)}, u32[]{:S(2)}, u32[]{:S(2)}) collective-permute-start(bf16[768,768]{1,0:T(8,128)(2,1)S(1)} %get-tuple-element.161.refs_3_), channel_id=1, source_target_pairs={{0,2},{1,3},{2,0},{3,1},{4,6},{5,7},{6,4},{7,5},{8,10},{9,11},{10,... | collective-permute-start | bytes 3538952 | tf_op jit(solution)/shard_map/ppermute | solution.py:87
  316.4 22.4 %collective-permute-start.26 = (bf16[192,1536]{1,0:T(8,128)(2,1)S(1)}, bf16[192,1536]{1,0:T(8,128)(2,1)S(1)}, u32[]{:S(2)}, u32[]{:S(2)}) collective-permute-start(bf16[192,1536]{1,0:T(8,128)(2,1)S(1)} %bitcast.229), channel_id=1, source_target_pairs={{0,8},{4,12},{8,0},{12,4},{16,24},{20,28},{24,16},{28,20},{1,9},{5... | collective-permute-start | bytes 1769480 | tf_op jit(solution)/shard_map/ppermute | solution.py:87
  316.4 23.2 %collective-permute-start.31 = (bf16[384,768]{1,0:T(8,128)(2,1)S(1)}, bf16[384,768]{1,0:T(8,128)(2,1)S(1)}, u32[]{:S(2)}, u32[]{:S(2)}) collective-permute-start(bf16[384,768]{1,0:T(8,128)(2,1)S(1)} %bitcast.248), channel_id=1, source_target_pairs={{0,4},{4,0},{8,12},{12,8},{16,20},{20,16},{24,28},{28,24},{1,5},{5... | collective-permute-start | bytes 1769480 | tf_op jit(solution)/shard_map/ppermute | solution.py:87
  316.6 23.8 %collective-permute-start.41 = (bf16[128,1280]{1,0:T(8,128)(2,1)S(1)}, bf16[128,1280]{1,0:T(8,128)(2,1)S(1)}, u32[]{:S(2)}, u32[]{:S(2)}) collective-permute-start(bf16[128,1280]{1,0:T(8,128)(2,1)S(1)} %bitcast.236), channel_id=1, source_target_pairs={{0,16},{4,20},{8,24},{12,28},{16,0},{20,4},{24,8},{28,12},{1,17},{... | collective-permute-start | bytes 983048 | tf_op jit(solution)/shard_map/ppermute | solution.py:87
  320.3 37.7 %collective-permute-start.37 = (bf16[3200,128]{1,0:T(8,128)(2,1)}, bf16[3200,128]{1,0:T(8,128)(2,1)}, u32[]{:S(2)}, u32[]{:S(2)}) collective-permute-start(bf16[3200,128]{1,0:T(8,128)(2,1)} %bitcast.75.refs_3_), channel_id=1, source_target_pairs={{0,4},{4,0},{8,12},{12,8},{16,20},{20,16},{24,28},{28,24},{1,5},{5... | collective-permute-start | bytes 2457608 | tf_op jit(solution)/shard_map/ppermute | solution.py:87
  339.6 16.7 %collective-permute-start.30 = (bf16[96,1536]{1,0:T(8,128)(2,1)}, bf16[96,1536]{1,0:T(8,128)(2,1)}, u32[]{:S(2)}, u32[]{:S(2)}) collective-permute-start(bf16[96,1536]{1,0:T(8,128)(2,1)} %bitcast.77.refs_3_), channel_id=1, source_target_pairs={{0,16},{4,20},{8,24},{12,28},{16,0},{20,4},{24,8},{28,12},{1,17},{... | collective-permute-start | bytes 884744 | tf_op jit(solution)/shard_map/ppermute | solution.py:87
  339.8 14.7 %collective-permute-start.32 = (bf16[192,768]{1,0:T(8,128)(2,1)S(1)}, bf16[192,768]{1,0:T(8,128)(2,1)S(1)}, u32[]{:S(2)}, u32[]{:S(2)}) collective-permute-start(bf16[192,768]{1,0:T(8,128)(2,1)S(1)} %bitcast.219), channel_id=1, source_target_pairs={{0,8},{4,12},{8,0},{12,4},{16,24},{20,28},{24,16},{28,20},{1,9},{5... | collective-permute-start | bytes 884744 | tf_op jit(solution)/shard_map/ppermute | solution.py:87
  345.1 23.0 %collective-permute-start.36 = (bf16[384,768]{1,0:T(8,128)(2,1)}, bf16[384,768]{1,0:T(8,128)(2,1)}, u32[]{:S(2)}, u32[]{:S(2)}) collective-permute-start(bf16[384,768]{1,0:T(8,128)(2,1)} %bitcast.85.refs_3_), channel_id=1, source_target_pairs={{0,4},{4,0},{8,12},{12,8},{16,20},{20,16},{24,28},{28,24},{1,5},{5... | collective-permute-start | bytes 1769480 | tf_op jit(solution)/shard_map/ppermute | solution.py:87
  360.9 12.8 %collective-permute-start.39 = (bf16[1600,128]{1,0:T(8,128)(2,1)}, bf16[1600,128]{1,0:T(8,128)(2,1)}, u32[]{:S(2)}, u32[]{:S(2)}) collective-permute-start(bf16[1600,128]{1,0:T(8,128)(2,1)} %bitcast.92.refs_3_), channel_id=1, source_target_pairs={{0,8},{4,12},{8,0},{12,4},{16,24},{20,28},{24,16},{28,20},{1,9},{5... | collective-permute-start | bytes 1228808 | tf_op jit(solution)/shard_map/ppermute | solution.py:87
  361.9 12.9 %collective-permute-start.42 = (bf16[128,1280]{1,0:T(8,128)(2,1)}, bf16[128,1280]{1,0:T(8,128)(2,1)}, u32[]{:S(2)}, u32[]{:S(2)}) collective-permute-start(bf16[128,1280]{1,0:T(8,128)(2,1)} %reduce-precision_convert_fusion), channel_id=1, source_target_pairs={{0,2},{1,3},{2,0},{3,1},{4,6},{5,7},{6,4},{7,5},{8,10},{9,11},{10,... | collective-permute-start | bytes 983048 | tf_op jit(solution)/shard_map/ppermute | solution.py:87
  365.7 18.5 %collective-permute-start.35 = (bf16[96,768]{1,0:T(8,128)(2,1)}, bf16[96,768]{1,0:T(8,128)(2,1)S(1)}, u32[]{:S(2)}, u32[]{:S(2)}) collective-permute-start(bf16[96,768]{1,0:T(8,128)(2,1)} %bitcast.86.refs_3_), channel_id=1, source_target_pairs={{0,16},{4,20},{8,24},{12,28},{16,0},{20,4},{24,8},{28,12},{1,17},{... | collective-permute-start | bytes 442376 | tf_op jit(solution)/shard_map/ppermute | solution.py:87
  367.2 18.4 %collective-permute-start.34 = (bf16[96,768]{1,0:T(8,128)(2,1)}, bf16[96,768]{1,0:T(8,128)(2,1)S(1)}, u32[]{:S(2)}, u32[]{:S(2)}) collective-permute-start(bf16[96,768]{1,0:T(8,128)(2,1)} %copy-done.52), channel_id=1, source_target_pairs={{0,2},{1,3},{2,0},{3,1},{4,6},{5,7},{6,4},{7,5},{8,10},{9,11},{10,... | collective-permute-start | bytes 442376 | tf_op jit(solution)/shard_map/ppermute | solution.py:87
  376.7 14.0 %collective-permute-start.53 = (f32[128,1280]{1,0:T(8,128)}, f32[128,1280]{1,0:T(8,128)}, u32[]{:S(2)}, u32[]{:S(2)}) collective-permute-start(f32[128,1280]{1,0:T(8,128)} %convert_add_fusion), channel_id=1, source_target_pairs={{0,1},{1,0},{2,3},{3,2},{4,5},{5,4},{6,7},{7,6},{8,9},{9,8},{10,11... | collective-permute-start | bytes 1966088 | tf_op jit(solution)/shard_map/ppermute | solution.py:87
  376.8 11.8 %collective-permute-start.38 = (bf16[192,768]{1,0:T(8,128)(2,1)}, bf16[192,768]{1,0:T(8,128)(2,1)S(1)}, u32[]{:S(2)}, u32[]{:S(2)}) collective-permute-start(bf16[192,768]{1,0:T(8,128)(2,1)} %bitcast.94.refs_3_), channel_id=1, source_target_pairs={{0,8},{4,12},{8,0},{12,4},{16,24},{20,28},{24,16},{28,20},{1,9},{5... | collective-permute-start | bytes 884744 | tf_op jit(solution)/shard_map/ppermute | solution.py:87
  388.6 9.6 %collective-permute-start.40 = (bf16[96,768]{1,0:T(8,128)(2,1)S(1)}, bf16[96,768]{1,0:T(8,128)(2,1)S(1)}, u32[]{:S(2)}, u32[]{:S(2)}) collective-permute-start(bf16[96,768]{1,0:T(8,128)(2,1)S(1)} %bitcast.249), channel_id=1, source_target_pairs={{0,16},{4,20},{8,24},{12,28},{16,0},{20,4},{24,8},{28,12},{1,17},{... | collective-permute-start | bytes 442376 | tf_op jit(solution)/shard_map/ppermute | solution.py:87
  (174 other events, 1079.9 us)
Sparse Core Ops, SparseCore 0:
  11.6 107.3 all-gather.1

commit v6 on v5

--- a/solution.py
+++ b/solution.py
@@ -1313,7 +1313,7 @@
     packed = jnp.concatenate(
         [pat_sums.reshape(-1), cross_sum[None], jnp.sum(keep)[None]]
     )
-    packed = pad_to(packed, 0, 4 * LANES).reshape(4, LANES)
+    packed = pad_to(packed, 0, 8 * LANES).reshape(8, LANES)
     packed = butterfly(packed).reshape(-1)
     pat_all = packed[: PATIENTS * 3 * CLASSES].reshape(PATIENTS, CLASSES, 3)
     ce_total = packed[PATIENTS * 3 * CLASSES]

time: 459 us -> 460 us (level)
  transfers between devices with their start and end apart: 55 -> 55, of which waited for: 28 -> 28; matrix products, arithmetic and copies ran while one was open for 10% -> 10% of each run, Pallas kernels for 22% -> 21%
where the time goes in v6:
time: 460 us; the launch traced here: 452 us
  waiting for transfers between devices  124 us (27%)
  Pallas kernels  124 us (27%)
  local copies, waits for them, and re-layouts  76.1 us (17%)
  starting transfers between devices  59.8 us (13%)
  other arithmetic  41.3 us (9%)
  between operations  25.6 us (6%)
    ppermute x40, waiting for transfers between devices, swap(): return lax.ppermute(value, axis, [(i, i ^ 1 << bit) for i in range(size)])  110 us
    unnamed x321, local copies, waits for them, and re-layouts  52 us
    ppermute x40, starting transfers between devices, swap(): return lax.ppermute(value, axis, [(i, i ^ 1 << bit) for i in range(size)])  43.3 us
    pallas_call x18, Pallas kernels, step(): pl.pallas_call(kernel, grid=(steps,), in_specs=[SCALAR] + [block(shape)]...  17.5 us
    ppermute x14, starting transfers between devices, hop(): lax.ppermute(value, ('dp', 'mp'), [(i, i ^ move) for i in range(size)])  16.5 us
    ppermute x14, waiting for transfers between devices, hop(): lax.ppermute(value, ('dp', 'mp'), [(i, i ^ move) for i in range(size)])  14.7 us
    pallas_call x1, Pallas kernels, attn_back(): pl.pallas_call(kernel, grid=(parts,), in_specs=[whole(width), whole(width...  13.5 us
    sub x9, other arithmetic, adamw(): weight - rate * (first_hat / (jnp.sqrt(second_hat) + adam_eps) + decay_ra...  12.9 us
  transfers between devices with their start and end apart: 55, of which 28 were waited for; matrix products, arithmetic and copies ran while one was open for 10% of the time, Pallas kernels for 21%

profile of v6, /device:TPU:0, one launch (start us, length us, event | category | flops | bytes accessed | tf_op | source)
XLA Modules:
  0.0 451.6 jit_solution(11869219348711669001)
XLA Ops:
  10.4 4.1 collective-permute-start
  16.7 13.4 %collective-permute-done = bf16[800,128]{1,0:T(8,128)(2,1)S(1)} collective-permute-done((bf16[800,128]{1,0:T(8,128)(2,1)S(1)}, bf16[800,128]{1,0:T(8,128)(2,1)S(1)}, u32[]{:S(2)}, u32[]{:S(2)}) %collective-permute-start) | collective-permute-done | bytes 204832 | tf_op jit(solution)/shard_map/ppermute | solution.py:87
  38.4 3.5 collective-permute-start.3
  41.9 3.6 collective-permute-done.4
  50.4 6.1 %collective-permute-start.6 = (bf16[128,1280]{1,0:T(8,128)(2,1)}, bf16[128,1280]{1,0:T(8,128)(2,1)S(1)}, u32[]{:S(2)}, u32[]{:S(2)}) collective-permute-start(bf16[128,1280]{1,0:T(8,128)(2,1)} %gate.2), channel_id=1, source_target_pairs={{0,16},{4,20},{8,24},{12,28},{16,0},{20,4},{24,8},{28,12},{1,17},{... | collective-permute-start | bytes 983048 | tf_op jit(solution)/shard_map/ppermute | solution.py:87
  56.4 28.6 %collective-permute-done.6 = bf16[128,1280]{1,0:T(8,128)(2,1)S(1)} collective-permute-done((bf16[128,1280]{1,0:T(8,128)(2,1)}, bf16[128,1280]{1,0:T(8,128)(2,1)S(1)}, u32[]{:S(2)}, u32[]{:S(2)}) %collective-permute-start.6) | collective-permute-done | bytes 327712 | tf_op jit(solution)/shard_map/ppermute | solution.py:87
  89.9 3.1 collective-permute-start.9
  97.7 2.9 reshape.453
  100.6 3.8 slice.144
  118.9 2.9 collective-permute-done.9
  124.5 3.2 gather_step.18.own_ref.refs_6_.refs_2_
  136.1 12.6 %enter.1 = (bf16[416,1024]{1,0:T(8,128)(2,1)S(1)}, bf16[416,1024]{1,0:T(8,128)(2,1)S(1)}, f32[416,768]{1,0:T(8,128)S(1)}, bf16[416,768]{1,0:T(8,128)(2,1)S(1)}, ...) custom-call(bf16[416,256]{1,0:T(8,128)(2,1)S(1)} %bitcast.240, bf16[256,1024]{1,0:T(8,128)(2,1)S(1)} %copy-done.94, ...), custom_call_target="tpu_custom_call" | custom-call | flops 25999998976 | bytes 78000000 | tf_op jit(solution)/shard_map/enter/pallas_call | solution.py:331
  154.7 3.7 copy-done.2
  162.0 12.0 %middle.1 = (f32[416,768]{1,0:T(8,128)S(1)}, bf16[416,768]{1,0:T(8,128)(2,1)S(1)}, bf16[4,416,768]{2,1,0:T(8,128)(2,1)S(1)}, bf16[4,416,768]{2,1,0:T(8,128)(2,1)...) custom-call(bf16[4,416,192]{2,1,0:T(8,128)(2,1)S(1)} %copy-done.30, f32[416,768]{1,0:T(8,128)S(1)} %copy-done.22, ...), custom_call_target="tpu_custom_call" | custom-call | flops 4000000000 | bytes 12000000 | tf_op jit(solution)/shard_map/middle/pallas_call | solution.py:406
  180.2 4.4 collective-permute-done.12.skip_other_ref.refs_10_
  184.7 9.3 %leave.1 = (f32[416,256]{1,0:T(8,128)S(1)}, bf16[416,256]{1,0:T(8,128)(2,1)S(1)}, bf16[416,2560]{1,0:T(8,128)(2,1)S(1)}, bf16[416,512]{1,0:T(8,128)(2,1)S(1)}, b...) custom-call(s32[1]{0:T(128)} %bitcast.core_ref.refs_0_, ...), custom_call_target="tpu_custom_call" | custom-call | flops 24000000000 | bytes 72000000 | tf_op jit(solution)/shard_map/leave/pallas_call | solution.py:511
  217.6 3.7 collective-permute-start.18
  222.8 3.8 collective-permute-done.19
  233.3 5.4 %leave_back.1 = (bf16[416,2304]{1,0:T(8,128)(2,1)S(1)}, bf16[416,2560]{1,0:T(8,128)(2,1)S(1)}) custom-call(f32[2,19]{1,0:T(2,128)S(1)} %pad_maximum_fusion.5.coef_ref, f32[416,2304]{1,0:T(8,128)S(1)} %copy-done.86, s32[416,256]{1,0:T(8,128)S(1)} %bitcast.233, bf16[416,2560]{1,0:T(8,128)(2,1)S(1)} %copy-done.90, bf16[512,1152]{1,0:T(8,128)(2,1)S(1)} %bitcast.188, ...), custom_call_target="tpu_custom_call" | custom-call | flops 12000000000 | bytes 36000000 | tf_op jit(solution)/shard_map/leave_back/pallas_call | solution.py:584
  240.0 3.5 skip_grad.1
  245.3 3.2 collective-permute-done.20
  254.6 11.0 %middle_back.1 = (bf16[4,416,768]{2,1,0:T(8,128)(2,1)S(1)}, f32[416,768]{1,0:T(8,128)S(1)}, bf16[416,768]{1,0:T(8,128)(2,1)S(1)}, bf16[4,416,192]{2,1,0:T(8,128)(2,1)S(1)}, f32[16,768]{1,0:T(8,128)S(1)}) custom-call(bf16[416,768]{1,0:T(8,128)(2,1)S(1)} %get-tuple-element.128.refs_1_.refs_0_, bf16[4,768,1536]{2,1,0:T(8,128)(2,1)} %bitcast.171, ...), custom_call_target="tpu_custom_call" | custom-call | flops 22000001024 | bytes 66000000 | tf_op jit(solution)/shard_map/middle_back/pallas_call | solution.py:927
  271.1 13.5 %attn_back.1.refs_3_.refs_1_ = bf16[4,416,576]{2,1,0:T(8,128)(2,1)S(1)} custom-call(bf16[4,416,576]{2,1,0:T(8,128)(2,1)S(1)} %copy-done.100, bf16[4,416,192]{2,1,0:T(8,128)(2,1)S(1)} %get-tuple-element.143.refs_1_, bf16[768,1536]{1,0:T(8,128)(2,1)S(1)} %get-tuple-element.145.refs_2_), custom_call_target="tpu_custom_call" | custom-call | flops 27000000512 | bytes 81000000 | tf_op jit(solution)/shard_map/attn_back/pallas_call | solution.py:995
  288.0 4.9 %attn_grad.1 = (bf16[768,1536]{1,0:T(8,128)(2,1)}, bf16[768,1536]{1,0:T(8,128)(2,1)S(1)}) custom-call(bf16[416,768]{1,0:T(8,128)(2,1)S(1)} %copy-done.96, bf16[4,416,576]{2,1,0:T(8,128)(2,1)S(1)} %attn_back.1.refs_3_.refs_1_, bf16[416,768]{1,0:T(8,128)(2,1)S(1)} %get-tuple-element.146.refs_2_, bf16[4,416,192]{2,1,0:T(8,128)(2,1)S(1)} %copy-done.31, ...), custom_call_target="tpu_custom_call" | custom-call | flops 7200000000 | bytes 21600000 | tf_op jit(solution)/shard_map/attn_grad/pallas_call | solution.py:1025
  293.2 3.0 decoder_grad.1.refs_12_.refs_9_
  299.7 8.8 %enter_back.1 = (bf16[416,768]{1,0:T(8,128)(2,1)S(1)}, bf16[416,1024]{1,0:T(8,128)(2,1)S(1)}, f32[208,768]{1,0:T(8,128)S(1)}, f32[16,768]{1,0:T(8,128)S(1)}) custom-call(s32[1]{0:T(128)} %bitcast.core_ref.refs_0_, bf16[4,416,576]{2,1,0:T(8,128)(2,1)S(1)} %attn_back.1.refs_3_.refs_1_, bf16[768,1536]{1,0:T(8,128)(2,1)} %gather_step.18.own_ref.refs_6_.refs_2_, ...), custom_call_target="tpu_custom_call" | custom-call | flops 20800000000 | bytes 62400000 | tf_op jit(solution)/shard_map/enter_back/pallas_call | solution.py:1070
  310.5 3.2 collective-permute-done.27
  322.7 17.5 %collective-permute-done.26 = bf16[192,1536]{1,0:T(8,128)(2,1)S(1)} collective-permute-done((bf16[192,1536]{1,0:T(8,128)(2,1)S(1)}, bf16[192,1536]{1,0:T(8,128)(2,1)S(1)}, u32[]{:S(2)}, u32[]{:S(2)}) %collective-permute-start.26) | collective-permute-done | bytes 589856 | tf_op jit(solution)/shard_map/ppermute | solution.py:87
  347.6 8.4 %collective-permute-done.32 = bf16[192,768]{1,0:T(8,128)(2,1)S(1)} collective-permute-done((bf16[192,768]{1,0:T(8,128)(2,1)S(1)}, bf16[192,768]{1,0:T(8,128)(2,1)S(1)}, u32[]{:S(2)}, u32[]{:S(2)}) %collective-permute-start.32) | collective-permute-done | bytes 294944 | tf_op jit(solution)/shard_map/ppermute | solution.py:87
  371.4 3.7 collective-permute-done.39
  378.4 6.1 %collective-permute-done.43 = bf16[800,128]{1,0:T(8,128)(2,1)S(1)} collective-permute-done((bf16[800,128]{1,0:T(8,128)(2,1)S(1)}, bf16[800,128]{1,0:T(8,128)(2,1)S(1)}, u32[]{:S(2)}, u32[]{:S(2)}) %collective-permute-start.43) | collective-permute-done | bytes 204832 | tf_op jit(solution)/shard_map/ppermute | solution.py:87
  394.9 4.7 %collective-permute-done.40 = bf16[96,768]{1,0:T(8,128)(2,1)S(1)} collective-permute-done((bf16[96,768]{1,0:T(8,128)(2,1)S(1)}, bf16[96,768]{1,0:T(8,128)(2,1)S(1)}, u32[]{:S(2)}, u32[]{:S(2)}) %collective-permute-start.40) | collective-permute-done | bytes 147488 | tf_op jit(solution)/shard_map/ppermute | solution.py:87
  (538 shorter events, 204.4 us)
Async XLA Ops:
  7.3 147.5 %all-gather.2.cloned.1.call-start = ((), (), s32[]{:S(2)}) async-start(), calls=%async_computation | async-start | bytes 9732096 | tf_op jit(solution)/shard_map/all_gather | solution.py:1221
  10.4 19.8 %collective-permute-start = (bf16[800,128]{1,0:T(8,128)(2,1)S(1)}, bf16[800,128]{1,0:T(8,128)(2,1)S(1)}, u32[]{:S(2)}, u32[]{:S(2)}) collective-permute-start(bf16[800,128]{1,0:T(8,128)(2,1)S(1)} %pack.1), channel_id=1, source_target_pairs={{0,16},{4,20},{8,24},{12,28},{16,0},{20,4},{24,8},{28,12},{1,17},{... | collective-permute-start | bytes 614408 | tf_op jit(solution)/shard_map/ppermute | solution.py:87
  16.0 18.7 %collective-permute-start.2 = (bf16[96,768]{1,0:T(8,128)(2,1)}, bf16[96,768]{1,0:T(8,128)(2,1)S(1)}, u32[]{:S(2)}, u32[]{:S(2)}) collective-permute-start(bf16[96,768]{1,0:T(8,128)(2,1)} %pad_maximum_fusion.3), channel_id=1, source_target_pairs={{0,16},{4,20},{8,24},{12,28},{16,0},{20,4},{24,8},{28,12},{1,17},{... | collective-permute-start | bytes 442376 | tf_op jit(solution)/shard_map/ppermute | solution.py:87
  34.7 10.8 %collective-permute-start.4 = (bf16[192,768]{1,0:T(8,128)(2,1)S(1)}, bf16[192,768]{1,0:T(8,128)(2,1)}, u32[]{:S(2)}, u32[]{:S(2)}) collective-permute-start(bf16[192,768]{1,0:T(8,128)(2,1)S(1)} %bitcast.189), channel_id=1, source_target_pairs={{0,8},{4,12},{8,0},{12,4},{16,24},{20,28},{24,16},{28,20},{1,9},{5... | collective-permute-start | bytes 884744 | tf_op jit(solution)/shard_map/ppermute | solution.py:87
  38.4 50.2 %collective-permute-start.3 = (bf16[3200,128]{1,0:T(8,128)(2,1)S(1)}, bf16[3200,128]{1,0:T(8,128)(2,1)}, u32[]{:S(2)}, u32[]{:S(2)}) collective-permute-start(bf16[3200,128]{1,0:T(8,128)(2,1)S(1)} %bitcast.177), channel_id=1, source_target_pairs={{0,8},{4,12},{8,0},{12,4},{16,24},{20,28},{24,16},{28,20},{1,9},{5... | collective-permute-start | bytes 2457608 | tf_op jit(solution)/shard_map/ppermute | solution.py:87
  46.5 39.6 %collective-permute-start.5 = (bf16[384,768]{1,0:T(8,128)(2,1)S(1)}, bf16[384,768]{1,0:T(8,128)(2,1)}, u32[]{:S(2)}, u32[]{:S(2)}) collective-permute-start(bf16[384,768]{1,0:T(8,128)(2,1)S(1)} %bitcast.183), channel_id=1, source_target_pairs={{0,4},{4,0},{8,12},{12,8},{16,20},{20,16},{24,28},{28,24},{1,5},{5... | collective-permute-start | bytes 1769480 | tf_op jit(solution)/shard_map/ppermute | solution.py:87
  50.4 34.7 %collective-permute-start.6 = (bf16[128,1280]{1,0:T(8,128)(2,1)}, bf16[128,1280]{1,0:T(8,128)(2,1)S(1)}, u32[]{:S(2)}, u32[]{:S(2)}) collective-permute-start(bf16[128,1280]{1,0:T(8,128)(2,1)} %gate.2), channel_id=1, source_target_pairs={{0,16},{4,20},{8,24},{12,28},{16,0},{20,4},{24,8},{28,12},{1,17},{... | collective-permute-start | bytes 983048 | tf_op jit(solution)/shard_map/ppermute | solution.py:87
  89.9 31.9 %collective-permute-start.9 = (bf16[256,1280]{1,0:T(8,128)(2,1)}, bf16[256,1280]{1,0:T(8,128)(2,1)}, u32[]{:S(2)}, u32[]{:S(2)}) collective-permute-start(bf16[256,1280]{1,0:T(8,128)(2,1)} %bitcast.181), channel_id=1, source_target_pairs={{0,8},{4,12},{8,0},{12,4},{16,24},{20,28},{24,16},{28,20},{1,9},{5... | collective-permute-start | bytes 1966088 | tf_op jit(solution)/shard_map/ppermute | solution.py:87
  93.0 31.4 %collective-permute-start.8 = (bf16[768,768]{1,0:T(8,128)(2,1)}, bf16[768,768]{1,0:T(8,128)(2,1)}, u32[]{:S(2)}, u32[]{:S(2)}) collective-permute-start(bf16[768,768]{1,0:T(8,128)(2,1)} %bitcast.28.refs_3_.refs_1_), channel_id=1, source_target_pairs={{0,2},{1,3},{2,0},{3,1},{4,6},{5,7},{6,4},{7,5},{8,10},{9,11},{10,... | collective-permute-start | bytes 3538952 | tf_op jit(solution)/shard_map/ppermute | solution.py:87
  129.2 47.8 %collective-permute-start.11 = (bf16[512,1280]{1,0:T(8,128)(2,1)S(1)}, bf16[512,1280]{1,0:T(8,128)(2,1)}, u32[]{:S(2)}, u32[]{:S(2)}) collective-permute-start(bf16[512,1280]{1,0:T(8,128)(2,1)S(1)} %bitcast.169), channel_id=1, source_target_pairs={{0,4},{4,0},{8,12},{12,8},{16,20},{20,16},{24,28},{28,24},{1,5},{5... | collective-permute-start | bytes 3932168 | tf_op jit(solution)/shard_map/ppermute | solution.py:87
  253.4 12.2 %collective-permute-start.21 = (bf16[768,1536]{1,0:T(8,128)(2,1)S(1)}, bf16[768,1536]{1,0:T(8,128)(2,1)S(1)}, u32[]{:S(2)}, u32[]{:S(2)}) collective-permute-start(bf16[768,1536]{1,0:T(8,128)(2,1)S(1)} %get-tuple-element.134.refs_8_), channel_id=1, source_target_pairs={{0,1},{1,0},{2,3},{3,2},{4,5},{5,4},{6,7},{7,6},{8,9},{9,8},{10,11... | collective-permute-start | bytes 7077896 | tf_op jit(solution)/shard_map/ppermute | solution.py:87
  253.6 32.8 %collective-permute-start.23 = (bf16[512,1280]{1,0:T(8,128)(2,1)}, bf16[512,1280]{1,0:T(8,128)(2,1)S(1)}, u32[]{:S(2)}, u32[]{:S(2)}) collective-permute-start(bf16[512,1280]{1,0:T(8,128)(2,1)} %bitcast.54.refs_3_), channel_id=1, source_target_pairs={{0,4},{4,0},{8,12},{12,8},{16,20},{20,16},{24,28},{28,24},{1,5},{5... | collective-permute-start | bytes 3932168 | tf_op jit(solution)/shard_map/ppermute | solution.py:87
  267.3 42.8 %collective-permute-start.22 = (bf16[384,1536]{1,0:T(8,128)(2,1)}, bf16[384,1536]{1,0:T(8,128)(2,1)S(1)}, u32[]{:S(2)}, u32[]{:S(2)}) collective-permute-start(bf16[384,1536]{1,0:T(8,128)(2,1)} %bitcast.58.refs_3_), channel_id=1, source_target_pairs={{0,4},{4,0},{8,12},{12,8},{16,20},{20,16},{24,28},{28,24},{1,5},{5... | collective-permute-start | bytes 3538952 | tf_op jit(solution)/shard_map/ppermute | solution.py:87
  271.0 13.6 %collective-permute-start.24 = (bf16[768,1536]{1,0:T(8,128)(2,1)S(1)}, bf16[768,1536]{1,0:T(8,128)(2,1)S(1)}, u32[]{:S(2)}, u32[]{:S(2)}) collective-permute-start(bf16[768,1536]{1,0:T(8,128)(2,1)S(1)} %get-tuple-element.145.refs_2_), channel_id=1, source_target_pairs={{0,1},{1,0},{2,3},{3,2},{4,5},{5,4},{6,7},{7,6},{8,9},{9,8},{10,11... | collective-permute-start | bytes 7077896 | tf_op jit(solution)/shard_map/ppermute | solution.py:87
  285.3 28.4 %collective-permute-start.27 = (bf16[768,768]{1,0:T(8,128)(2,1)S(1)}, bf16[768,768]{1,0:T(8,128)(2,1)S(1)}, u32[]{:S(2)}, u32[]{:S(2)}) collective-permute-start(bf16[768,768]{1,0:T(8,128)(2,1)S(1)} %get-tuple-element.149.refs_3_), channel_id=1, source_target_pairs={{0,2},{1,3},{2,0},{3,1},{4,6},{5,7},{6,4},{7,5},{8,10},{9,11},{10,... | collective-permute-start | bytes 3538952 | tf_op jit(solution)/shard_map/ppermute | solution.py:87
  287.6 22.8 %collective-permute-start.28 = (bf16[256,1280]{1,0:T(8,128)(2,1)}, bf16[256,1280]{1,0:T(8,128)(2,1)S(1)}, u32[]{:S(2)}, u32[]{:S(2)}) collective-permute-start(bf16[256,1280]{1,0:T(8,128)(2,1)} %bitcast.62.refs_4_), channel_id=1, source_target_pairs={{0,8},{4,12},{8,0},{12,4},{16,24},{20,28},{24,16},{28,20},{1,9},{5... | collective-permute-start | bytes 1966088 | tf_op jit(solution)/shard_map/ppermute | solution.py:87
  292.9 15.5 %collective-permute-start.25 = (bf16[768,1536]{1,0:T(8,128)(2,1)}, bf16[768,1536]{1,0:T(8,128)(2,1)S(1)}, u32[]{:S(2)}, u32[]{:S(2)}) collective-permute-start(bf16[768,1536]{1,0:T(8,128)(2,1)} %get-tuple-element.152.refs_8_), channel_id=1, source_target_pairs={{0,1},{1,0},{2,3},{3,2},{4,5},{5,4},{6,7},{7,6},{8,9},{9,8},{10,11... | collective-permute-start | bytes 7077896 | tf_op jit(solution)/shard_map/ppermute | solution.py:87
  316.7 28.4 %collective-permute-start.33 = (bf16[768,768]{1,0:T(8,128)(2,1)S(1)}, bf16[768,768]{1,0:T(8,128)(2,1)S(1)}, u32[]{:S(2)}, u32[]{:S(2)}) collective-permute-start(bf16[768,768]{1,0:T(8,128)(2,1)S(1)} %get-tuple-element.161.refs_3_), channel_id=1, source_target_pairs={{0,2},{1,3},{2,0},{3,1},{4,6},{5,7},{6,4},{7,5},{8,10},{9,11},{10,... | collective-permute-start | bytes 3538952 | tf_op jit(solution)/shard_map/ppermute | solution.py:87
  317.8 22.4 %collective-permute-start.26 = (bf16[192,1536]{1,0:T(8,128)(2,1)S(1)}, bf16[192,1536]{1,0:T(8,128)(2,1)S(1)}, u32[]{:S(2)}, u32[]{:S(2)}) collective-permute-start(bf16[192,1536]{1,0:T(8,128)(2,1)S(1)} %bitcast.230), channel_id=1, source_target_pairs={{0,8},{4,12},{8,0},{12,4},{16,24},{20,28},{24,16},{28,20},{1,9},{5... | collective-permute-start | bytes 1769480 | tf_op jit(solution)/shard_map/ppermute | solution.py:87
  317.8 23.2 %collective-permute-start.31 = (bf16[384,768]{1,0:T(8,128)(2,1)S(1)}, bf16[384,768]{1,0:T(8,128)(2,1)S(1)}, u32[]{:S(2)}, u32[]{:S(2)}) collective-permute-start(bf16[384,768]{1,0:T(8,128)(2,1)S(1)} %bitcast.249), channel_id=1, source_target_pairs={{0,4},{4,0},{8,12},{12,8},{16,20},{20,16},{24,28},{28,24},{1,5},{5... | collective-permute-start | bytes 1769480 | tf_op jit(solution)/shard_map/ppermute | solution.py:87
  318.0 23.8 %collective-permute-start.41 = (bf16[128,1280]{1,0:T(8,128)(2,1)S(1)}, bf16[128,1280]{1,0:T(8,128)(2,1)S(1)}, u32[]{:S(2)}, u32[]{:S(2)}) collective-permute-start(bf16[128,1280]{1,0:T(8,128)(2,1)S(1)} %bitcast.237), channel_id=1, source_target_pairs={{0,16},{4,20},{8,24},{12,28},{16,0},{20,4},{24,8},{28,12},{1,17},{... | collective-permute-start | bytes 983048 | tf_op jit(solution)/shard_map/ppermute | solution.py:87
  321.8 37.7 %collective-permute-start.37 = (bf16[3200,128]{1,0:T(8,128)(2,1)}, bf16[3200,128]{1,0:T(8,128)(2,1)}, u32[]{:S(2)}, u32[]{:S(2)}) collective-permute-start(bf16[3200,128]{1,0:T(8,128)(2,1)} %bitcast.75.refs_3_), channel_id=1, source_target_pairs={{0,4},{4,0},{8,12},{12,8},{16,20},{20,16},{24,28},{28,24},{1,5},{5... | collective-permute-start | bytes 2457608 | tf_op jit(solution)/shard_map/ppermute | solution.py:87
  341.0 16.7 %collective-permute-start.30 = (bf16[96,1536]{1,0:T(8,128)(2,1)}, bf16[96,1536]{1,0:T(8,128)(2,1)}, u32[]{:S(2)}, u32[]{:S(2)}) collective-permute-start(bf16[96,1536]{1,0:T(8,128)(2,1)} %bitcast.77.refs_3_), channel_id=1, source_target_pairs={{0,16},{4,20},{8,24},{12,28},{16,0},{20,4},{24,8},{28,12},{1,17},{... | collective-permute-start | bytes 884744 | tf_op jit(solution)/shard_map/ppermute | solution.py:87
  341.2 14.7 %collective-permute-start.32 = (bf16[192,768]{1,0:T(8,128)(2,1)S(1)}, bf16[192,768]{1,0:T(8,128)(2,1)S(1)}, u32[]{:S(2)}, u32[]{:S(2)}) collective-permute-start(bf16[192,768]{1,0:T(8,128)(2,1)S(1)} %bitcast.220), channel_id=1, source_target_pairs={{0,8},{4,12},{8,0},{12,4},{16,24},{20,28},{24,16},{28,20},{1,9},{5... | collective-permute-start | bytes 884744 | tf_op jit(solution)/shard_map/ppermute | solution.py:87
  346.6 23.1 %collective-permute-start.36 = (bf16[384,768]{1,0:T(8,128)(2,1)}, bf16[384,768]{1,0:T(8,128)(2,1)}, u32[]{:S(2)}, u32[]{:S(2)}) collective-permute-start(bf16[384,768]{1,0:T(8,128)(2,1)} %bitcast.85.refs_3_), channel_id=1, source_target_pairs={{0,4},{4,0},{8,12},{12,8},{16,20},{20,16},{24,28},{28,24},{1,5},{5... | collective-permute-start | bytes 1769480 | tf_op jit(solution)/shard_map/ppermute | solution.py:87
  362.3 12.8 %collective-permute-start.39 = (bf16[1600,128]{1,0:T(8,128)(2,1)}, bf16[1600,128]{1,0:T(8,128)(2,1)}, u32[]{:S(2)}, u32[]{:S(2)}) collective-permute-start(bf16[1600,128]{1,0:T(8,128)(2,1)} %bitcast.92.refs_3_), channel_id=1, source_target_pairs={{0,8},{4,12},{8,0},{12,4},{16,24},{20,28},{24,16},{28,20},{1,9},{5... | collective-permute-start | bytes 1228808 | tf_op jit(solution)/shard_map/ppermute | solution.py:87
  363.4 12.9 %collective-permute-start.42 = (bf16[128,1280]{1,0:T(8,128)(2,1)}, bf16[128,1280]{1,0:T(8,128)(2,1)}, u32[]{:S(2)}, u32[]{:S(2)}) collective-permute-start(bf16[128,1280]{1,0:T(8,128)(2,1)} %reduce-precision_convert_fusion), channel_id=1, source_target_pairs={{0,2},{1,3},{2,0},{3,1},{4,6},{5,7},{6,4},{7,5},{8,10},{9,11},{10,... | collective-permute-start | bytes 983048 | tf_op jit(solution)/shard_map/ppermute | solution.py:87
  367.2 18.5 %collective-permute-start.35 = (bf16[96,768]{1,0:T(8,128)(2,1)}, bf16[96,768]{1,0:T(8,128)(2,1)S(1)}, u32[]{:S(2)}, u32[]{:S(2)}) collective-permute-start(bf16[96,768]{1,0:T(8,128)(2,1)} %bitcast.86.refs_3_), channel_id=1, source_target_pairs={{0,16},{4,20},{8,24},{12,28},{16,0},{20,4},{24,8},{28,12},{1,17},{... | collective-permute-start | bytes 442376 | tf_op jit(solution)/shard_map/ppermute | solution.py:87
  368.6 18.4 %collective-permute-start.34 = (bf16[96,768]{1,0:T(8,128)(2,1)}, bf16[96,768]{1,0:T(8,128)(2,1)S(1)}, u32[]{:S(2)}, u32[]{:S(2)}) collective-permute-start(bf16[96,768]{1,0:T(8,128)(2,1)} %copy-done.52), channel_id=1, source_target_pairs={{0,2},{1,3},{2,0},{3,1},{4,6},{5,7},{6,4},{7,5},{8,10},{9,11},{10,... | collective-permute-start | bytes 442376 | tf_op jit(solution)/shard_map/ppermute | solution.py:87
  378.2 14.0 %collective-permute-start.53 = (f32[128,1280]{1,0:T(8,128)}, f32[128,1280]{1,0:T(8,128)}, u32[]{:S(2)}, u32[]{:S(2)}) collective-permute-start(f32[128,1280]{1,0:T(8,128)} %convert_add_fusion), channel_id=1, source_target_pairs={{0,1},{1,0},{2,3},{3,2},{4,5},{5,4},{6,7},{7,6},{8,9},{9,8},{10,11... | collective-permute-start | bytes 1966088 | tf_op jit(solution)/shard_map/ppermute | solution.py:87
  378.2 11.8 %collective-permute-start.38 = (bf16[192,768]{1,0:T(8,128)(2,1)}, bf16[192,768]{1,0:T(8,128)(2,1)S(1)}, u32[]{:S(2)}, u32[]{:S(2)}) collective-permute-start(bf16[192,768]{1,0:T(8,128)(2,1)} %bitcast.94.refs_3_), channel_id=1, source_target_pairs={{0,8},{4,12},{8,0},{12,4},{16,24},{20,28},{24,16},{28,20},{1,9},{5... | collective-permute-start | bytes 884744 | tf_op jit(solution)/shard_map/ppermute | solution.py:87
  390.1 9.6 %collective-permute-start.40 = (bf16[96,768]{1,0:T(8,128)(2,1)S(1)}, bf16[96,768]{1,0:T(8,128)(2,1)S(1)}, u32[]{:S(2)}, u32[]{:S(2)}) collective-permute-start(bf16[96,768]{1,0:T(8,128)(2,1)S(1)} %bitcast.250), channel_id=1, source_target_pairs={{0,16},{4,20},{8,24},{12,28},{16,0},{20,4},{24,8},{28,12},{1,17},{... | collective-permute-start | bytes 442376 | tf_op jit(solution)/shard_map/ppermute | solution.py:87
  (174 other events, 1083.0 us)
Sparse Core Ops, SparseCore 0:
  11.6 107.3 all-gather.1
